TPU v7x, 32 devices: a whole 2x2x4 slice. The times are simulated.
32 devices in a mesh: seq: 8 (over z, y), batch: 4 (over x, core).
Axes of the slice: x: 2, y: 2, z: 4, core: 2. Of those that a mesh axis runs over, the one named last changes fastest.
Arguments:
- tokens: bfloat16 [28, 1152, 768], P('batch', 'seq'), may hold values from -6 to 6
- cotangent: bfloat16 [28, 1152, 768], P('batch', 'seq'), may hold values from -6 to 6
- gain_in: float32 [768], replicated, may hold values from 0.5 to 1.5
- w_mix: bfloat16 [768, 1920], replicated, may hold values from -0.21875 to 0.21875
- lower: float32 [384], replicated, may hold values from 0.5 to 0.96
- fbias: float32 [384], replicated, may hold values from -1 to 11
- phase: float32 [384], replicated, may hold values from -0.5 to 0.5
- gain_out: float32 [768], replicated, may hold values from 0.5 to 1.5
- w_out: bfloat16 [768, 768], replicated, may hold values from -0.4375 to 0.4375
- gain_ffn: float32 [768], replicated, may hold values from 0.5 to 1.5
- w_gu: bfloat16 [768, 3072], replicated, may hold values from -0.21875 to 0.21875
- w_down: bfloat16 [1536, 768], replicated, may hold values from -0.3125 to 0.3125
Outputs:
- output: bfloat16 [28, 1152, 768], P('batch', 'seq')
- grad_tokens: float32 [28, 1152, 768], P('batch', 'seq')
- grad_w_mix: float32 [768, 1920], P('seq')
- grad_w_out: float32 [768, 768], P('seq')
- grad_w_gu: float32 [768, 3072], P('seq')
- grad_w_down: float32 [1536, 768], P('seq')
- grad_gain_in: float32 [768], replicated
- grad_gain_out: float32 [768], replicated
- grad_gain_ffn: float32 [768], replicated
- grad_lower: float32 [384], replicated
- grad_fbias: float32 [384], replicated
- grad_phase: float32 [384], replicated
All inputs are finite; a program needn't handle non-finite values.
Results may differ from a plain program's by a relative error of at most 0.0099.
Values sent between devices are 32-bit elements; how exact they have to be, the bound alone decides.
No kernel may reach another device: no remote copies, remote signals or barrier semaphores. Data moves between devices by JAX's collectives and lax.ppermute only.
A program may use at most 192 MiB of HBM per device.

v0:
```python
import jax
import jax.numpy as jnp
from jax import lax
from jax.sharding import PartitionSpec as P

epsilon = 1e-06


def prefix(value, axis, join, neutral, backward):
    count, mine = (lax.axis_size(axis), lax.axis_index(axis))
    pieces = jax.tree.map(lambda part: lax.all_gather(part, axis), value)
    if backward:
        pieces = jax.tree.map(lambda part: part[::-1], pieces)
        mine = count - 1 - mine
    subtotal = jax.tree.map(
        lambda part, zero: jnp.full_like(part, 0) + jnp.asarray(zero, part.dtype), value, neutral
    )

    def step(position, subtotal):
        longer = join(subtotal, jax.tree.map(lambda part: part[position], pieces))
        return jax.tree.map(lambda new, old: jnp.where(position < mine, new, old), longer, subtotal)

    return lax.fori_loop(0, count - 1, step, subtotal)


def combine(earlier, later_part):
    mul_r, mul_i, add_r, add_i = earlier
    new_r, new_i, plus_r, plus_i = later_part
    out_mr = mul_r * new_r - mul_i * new_i
    out_mi = mul_r * new_i + mul_i * new_r
    out_ar = new_r * add_r - new_i * add_i + plus_r
    out_ai = new_r * add_i + new_i * add_r + plus_i
    return (out_mr, out_mi, out_ar, out_ai)


def inverse_rms(values):
    return lax.rsqrt(jnp.mean(values * values, axis=-1, keepdims=True) + epsilon)


def norm_back(upstream, normed, scale):
    return scale * (upstream - normed * jnp.mean(upstream * normed, axis=-1, keepdims=True))


def silu_slope(values):
    sigma = jax.nn.sigmoid(values)
    return sigma * (1.0 + values * (1.0 - sigma))


def outer_sum(left, right):
    return lax.dot_general(
        left, right, (((0,), (0,)), ((), ())), preferred_element_type=jnp.float32
    )


def back_product(grad, weight):
    return lax.dot_general(
        grad, weight, (((1,), (1,)), ((), ())), preferred_element_type=jnp.float32
    )


def per_device(
    tokens, cotangent, gain_in, w_mix, lower, fbias, phase, gain_out, w_out, gain_ffn, w_gu, w_down
):
    seqs, positions, width = tokens.shape
    chans = lower.shape[0]
    units = w_down.shape[0]
    total_rows = seqs * positions
    lanes = seqs * chans
    inputs = jnp.transpose(tokens, (1, 0, 2)).astype(jnp.float32).reshape(total_rows, width)
    scale_in = inverse_rms(inputs)
    normed_in = inputs * scale_in
    low_in = (normed_in * gain_in).astype(jnp.bfloat16)
    projected = jnp.dot(low_in, w_mix, preferred_element_type=jnp.float32)
    in_r = projected[:, :chans]
    in_i = projected[:, chans : 2 * chans]
    forget = projected[:, 2 * chans : 3 * chans] + fbias
    gate_pre = projected[:, 3 * chans :]
    act_r = jax.nn.silu(in_r)
    act_i = jax.nn.silu(in_i)
    sig_forget = jax.nn.sigmoid(forget)
    retain = lower + (1.0 - lower) * sig_forget
    intake = 1.0 - retain
    cosine = jnp.cos(phase)
    sine_part = jnp.sin(phase)
    shaped = (positions, lanes)
    pairs = (seqs, chans)
    mult_r = (retain * cosine).reshape(shaped)
    mult_i = (retain * sine_part).reshape(shaped)
    feed_r = (intake * act_r).reshape(shaped)
    feed_i = (intake * act_i).reshape(shaped)
    cum_r, cum_i, local_r, local_i = lax.associative_scan(
        combine, (mult_r, mult_i, feed_r, feed_i), axis=0
    )
    block_ends = (
        cum_r[-1].reshape(pairs),
        cum_i[-1].reshape(pairs),
        local_r[-1].reshape(pairs),
        local_i[-1].reshape(pairs),
    )
    unit_ones = jnp.ones(pairs, jnp.float32)
    nothing = jnp.zeros(pairs, jnp.float32)
    carried = prefix(block_ends, "seq", combine, (unit_ones, nothing, nothing, nothing), False)
    start_r = carried[2].reshape(1, lanes)
    start_i = carried[3].reshape(1, lanes)
    state_r = local_r + cum_r * start_r - cum_i * start_i
    state_i = local_i + cum_r * start_i + cum_i * start_r
    flat = (total_rows, chans)
    states = jnp.concatenate([state_r.reshape(flat), state_i.reshape(flat)], axis=-1)
    scale_out = inverse_rms(states)
    normed_out = states * scale_out
    gate_act = jax.nn.silu(gate_pre)
    mixed_low = (normed_out * gain_out * gate_act).astype(jnp.bfloat16)
    after_mix = inputs + jnp.dot(mixed_low, w_out, preferred_element_type=jnp.float32)
    scale_ffn = inverse_rms(after_mix)
    normed_ffn = after_mix * scale_ffn
    ffn_low = (normed_ffn * gain_ffn).astype(jnp.bfloat16)
    gate_up = jnp.dot(ffn_low, w_gu, preferred_element_type=jnp.float32)
    gate_part = gate_up[:, :units]
    up_part = gate_up[:, units:]
    hidden_low = (jax.nn.silu(gate_part) * up_part).astype(jnp.bfloat16)
    result = after_mix + jnp.dot(hidden_low, w_down, preferred_element_type=jnp.float32)
    output = jnp.transpose(result.astype(jnp.bfloat16).reshape(positions, seqs, width), (1, 0, 2))
    upstream = jnp.transpose(cotangent, (1, 0, 2)).astype(jnp.float32).reshape(total_rows, width)
    upstream_low = upstream.astype(jnp.bfloat16)
    grad_down = outer_sum(hidden_low, upstream_low)
    grad_hidden = back_product(upstream_low, w_down)
    grad_up = grad_hidden * jax.nn.silu(gate_part)
    grad_gate_part = grad_hidden * up_part * silu_slope(gate_part)
    grad_gu_low = jnp.concatenate([grad_gate_part, grad_up], axis=-1).astype(jnp.bfloat16)
    grad_gu = outer_sum(ffn_low, grad_gu_low)
    grad_ffn_in = back_product(grad_gu_low, w_gu)
    sum_gain_ffn = jnp.sum(grad_ffn_in * normed_ffn, axis=0)
    grad_mid = upstream + norm_back(grad_ffn_in * gain_ffn, normed_ffn, scale_ffn)
    grad_mid_low = grad_mid.astype(jnp.bfloat16)
    grad_out = outer_sum(mixed_low, grad_mid_low)
    grad_mixed = back_product(grad_mid_low, w_out)
    grad_gate = grad_mixed * normed_out * gain_out * silu_slope(gate_pre)
    grad_normed = grad_mixed * gate_act
    sum_gain_out = jnp.sum(grad_normed * normed_out, axis=0)
    grad_states = norm_back(grad_normed * gain_out, normed_out, scale_out)
    seed_r = grad_states[:, :chans].reshape(shaped)
    seed_i = grad_states[:, chans:].reshape(shaped)
    edge_one = jnp.ones((1, lanes), jnp.float32)
    edge_zero = jnp.zeros((1, lanes), jnp.float32)
    next_r = jnp.concatenate([mult_r[1:], edge_one], axis=0)
    next_i = jnp.concatenate([-mult_i[1:], edge_zero], axis=0)
    back_r, back_i, qloc_r, qloc_i = lax.associative_scan(
        combine, (next_r, next_i, seed_r, seed_i), reverse=True, axis=0
    )
    first_r = mult_r[0]
    first_i = -mult_i[0]
    block_starts = (
        (first_r * back_r[0] - first_i * back_i[0]).reshape(pairs),
        (first_r * back_i[0] + first_i * back_r[0]).reshape(pairs),
        (first_r * qloc_r[0] - first_i * qloc_i[0]).reshape(pairs),
        (first_r * qloc_i[0] + first_i * qloc_r[0]).reshape(pairs),
    )
    incoming = prefix(block_starts, "seq", combine, (unit_ones, nothing, nothing, nothing), True)
    enter_r = incoming[2].reshape(1, lanes)
    enter_i = incoming[3].reshape(1, lanes)
    adj_r = qloc_r + back_r * enter_r - back_i * enter_i
    adj_i = qloc_i + back_r * enter_i + back_i * enter_r
    before_r = jnp.concatenate([start_r, state_r[:-1]], axis=0)
    before_i = jnp.concatenate([start_i, state_i[:-1]], axis=0)
    grad_mr = (adj_r * before_r + adj_i * before_i).reshape(flat)
    grad_mi = (adj_i * before_r - adj_r * before_i).reshape(flat)
    adj_r = adj_r.reshape(flat)
    adj_i = adj_i.reshape(flat)
    grad_retain = grad_mr * cosine + grad_mi * sine_part - (adj_r * act_r + adj_i * act_i)
    sum_phase = jnp.sum(retain * (grad_mi * cosine - grad_mr * sine_part), axis=0)
    sum_lower = jnp.sum(grad_retain * (1.0 - sig_forget), axis=0)
    grad_forget = grad_retain * (1.0 - lower) * sig_forget * (1.0 - sig_forget)
    sum_fbias = jnp.sum(grad_forget, axis=0)
    grad_pre_low = jnp.concatenate(
        [
            adj_r * intake * silu_slope(in_r),
            adj_i * intake * silu_slope(in_i),
            grad_forget,
            grad_gate,
        ],
        axis=-1,
    ).astype(jnp.bfloat16)
    grad_mix = outer_sum(low_in, grad_pre_low)
    grad_in = back_product(grad_pre_low, w_mix)
    sum_gain_in = jnp.sum(grad_in * normed_in, axis=0)
    grad_inputs = grad_mid + norm_back(grad_in * gain_in, normed_in, scale_in)
    grad_tokens = jnp.transpose(grad_inputs.reshape(positions, seqs, width), (1, 0, 2))
    vectors = lax.psum(
        (sum_gain_in, sum_gain_out, sum_gain_ffn, sum_lower, sum_fbias, sum_phase), ("seq", "batch")
    )
    parted = (
        lax.psum_scatter(grad_mix, "seq", scatter_dimension=0, tiled=True),
        lax.psum_scatter(grad_out, "seq", scatter_dimension=0, tiled=True),
        lax.psum_scatter(grad_gu, "seq", scatter_dimension=0, tiled=True),
        lax.psum_scatter(grad_down, "seq", scatter_dimension=0, tiled=True),
    )
    summed = lax.psum((parted[0], parted[1], parted[2], parted[3]), "batch")
    return (
        output,
        grad_tokens,
        summed[0],
        summed[1],
        summed[2],
        summed[3],
        vectors[0],
        vectors[1],
        vectors[2],
        vectors[3],
        vectors[4],
        vectors[5],
    )


def solution(mesh):
    in_specs = (
        P("batch", "seq", None),
        P("batch", "seq", None),
        P(),
        P(),
        P(),
        P(),
        P(),
        P(),
        P(),
        P(),
        P(),
        P(),
    )
    out_specs = (
        P("batch", "seq", None),
        P("batch", "seq", None),
        P("seq", None),
        P("seq", None),
        P("seq", None),
        P("seq", None),
        P(),
        P(),
        P(),
        P(),
        P(),
        P(),
    )
    return jax.shard_map(
        per_device, mesh=mesh, in_specs=in_specs, out_specs=out_specs, check_vma=False
    )
```

profile of v0, /device:TPU:0, one launch (start us, length us, event | category | flops | bytes accessed | tf_op | source)
XLA Modules:
  0.0 1696.2 jit_solution(1956065844702931970)
XLA Ops:
  11.6 5.5 copy.32
  21.9 5.3 fusion.39
  353.2 5.2 pad.398
  360.5 5.2 pad.400
  371.7 32.3 %all_gather.24 = f32[8,7,384]{2,1,0:T(8,128)S(1)} all-gather(f32[1,7,384]{2,1,0:T(8,128)S(1)} %all_gather_reshape_squeeze.12), channel_id=1, replica_groups=mesh['seq'=8,'batch'=4] {'seq'}, dimensions={0}, use_global_device_ids=true | all-gather | bytes 96768 | tf_op jit(solution)/shard_map/all_gather | solution.py:11
  410.2 30.5 %all_gather.25 = f32[8,7,384]{2,1,0:T(8,128)S(1)} all-gather(f32[1,7,384]{2,1,0:T(8,128)S(1)} %all_gather_reshape_squeeze.13), channel_id=1, replica_groups=mesh['seq'=8,'batch'=4] {'seq'}, dimensions={0}, use_global_device_ids=true | all-gather | bytes 96768 | tf_op jit(solution)/shard_map/all_gather | solution.py:11
  448.0 5.2 pad.373
  454.1 30.5 %all_gather.26 = f32[8,7,384]{2,1,0:T(8,128)S(1)} all-gather(f32[1,7,384]{2,1,0:T(8,128)S(1)} %all_gather_reshape_squeeze.14), channel_id=1, replica_groups=mesh['seq'=8,'batch'=4] {'seq'}, dimensions={0}, use_global_device_ids=true | all-gather | bytes 96768 | tf_op jit(solution)/shard_map/all_gather | solution.py:11
  484.7 5.2 pad.403
  490.9 30.5 %all_gather.27 = f32[8,7,384]{2,1,0:T(8,128)S(1)} all-gather(f32[1,7,384]{2,1,0:T(8,128)S(1)} %all_gather_reshape_squeeze.15), channel_id=1, replica_groups=mesh['seq'=8,'batch'=4] {'seq'}, dimensions={0}, use_global_device_ids=true | all-gather | bytes 96768 | tf_op jit(solution)/shard_map/all_gather | solution.py:11
  522.0 6.9 multiply_add_fusion.4
  542.3 8.1 fusion.40
  550.4 9.7 multiply_convert_fusion.1
  560.1 8.2 multiply_reduce_fusion
  573.8 7.2 fusion.43
  620.6 7.0 multiply_reduce_fusion.1
  662.9 10.6 slice.1065
  673.5 10.6 slice.1051
  684.1 10.6 slice.1057
  694.7 10.5 slice.1067
  705.2 10.6 slice.1054
  715.8 10.5 slice.1062
  726.3 10.5 slice.1060
  736.8 10.5 slice.1073
  878.6 10.6 slice.1049
  889.2 10.8 slice.1153
  980.1 10.6 slice.1158
  990.7 10.6 slice.1187
  1040.4 5.2 pad.454
  1053.9 20.4 %rev.29 = f32[144,2688]{1,0:T(8,128)} reverse(f32[144,2688]{1,0:T(8,128)} %add.1132), dimensions={0} | reverse | bytes 3096576 | tf_op jit(solution)/shard_map/rev | solution.py:147
  1075.3 5.2 pad.457
  1096.0 20.4 %rev.28 = f32[144,2688]{1,0:T(8,128)} reverse(f32[144,2688]{1,0:T(8,128)} %add.1113), dimensions={0} | reverse | bytes 3096576 | tf_op jit(solution)/shard_map/rev | solution.py:147
  1125.7 20.4 %rev.35 = f32[144,2688]{1,0:T(8,128)} reverse(f32[144,2688]{1,0:T(8,128)} %add.1139), dimensions={0} | reverse | bytes 3096576 | tf_op jit(solution)/shard_map/rev | solution.py:147
  1157.5 20.4 %rev.34 = f32[144,2688]{1,0:T(8,128)} reverse(f32[144,2688]{1,0:T(8,128)} %add.1134), dimensions={0} | reverse | bytes 3096576 | tf_op jit(solution)/shard_map/rev | solution.py:147
  1179.7 30.5 %all-gather.7 = f32[8,7,384]{2,1,0:T(8,128)S(1)} all-gather(f32[1,7,384]{2,1,0:T(8,128)S(1)} %get-tuple-element.466), channel_id=5, replica_groups=mesh['seq'=8,'batch'=4] {'seq'}, dimensions={0}, use_global_device_ids=true | all-gather | bytes 96768 | tf_op jit(solution)/shard_map/all_gather | solution.py:11
  1210.2 30.5 %all-gather.6 = f32[8,7,384]{2,1,0:T(8,128)S(1)} all-gather(f32[1,7,384]{2,1,0:T(8,128)S(1)} %get-tuple-element.467), channel_id=4, replica_groups=mesh['seq'=8,'batch'=4] {'seq'}, dimensions={0}, use_global_device_ids=true | all-gather | bytes 96768 | tf_op jit(solution)/shard_map/all_gather | solution.py:11
  1240.8 30.5 %all-gather.4 = f32[8,7,384]{2,1,0:T(8,128)S(1)} all-gather(f32[1,7,384]{2,1,0:T(8,128)S(1)} %get-tuple-element.470), channel_id=2, replica_groups=mesh['seq'=8,'batch'=4] {'seq'}, dimensions={0}, use_global_device_ids=true | all-gather | bytes 96768 | tf_op jit(solution)/shard_map/all_gather | solution.py:11
  1271.3 30.5 %all-gather.5 = f32[8,7,384]{2,1,0:T(8,128)S(1)} all-gather(f32[1,7,384]{2,1,0:T(8,128)S(1)} %get-tuple-element.471), channel_id=3, replica_groups=mesh['seq'=8,'batch'=4] {'seq'}, dimensions={0}, use_global_device_ids=true | all-gather | bytes 96768 | tf_op jit(solution)/shard_map/all_gather | solution.py:11
  1302.5 6.2 multiply_add_fusion.2
  1323.4 5.5 fusion.24
  1332.4 6.2 fusion.22
  1339.4 12.5 fusion.9
  1352.0 7.2 add_convert_fusion
  1365.8 85.7 %reduce-scatter.5.cloned.1.call-done = f32[96,1920]{1,0:T(8,128)} async-done(((f32[768,1920]{1,0:T(8,128)}), f32[96,1920]{1,0:T(8,128)}) %reduce-scatter.5.cloned.1.call-update) | async-done | bytes 737296 | tf_op jit(solution)/shard_map/reduce_scatter | solution.py:192
  1451.5 166.6 %reduce-scatter.9.cloned.1.call-done = f32[96,3072]{1,0:T(8,128)} async-done(((f32[768,3072]{1,0:T(8,128)}), f32[96,3072]{1,0:T(8,128)}) %reduce-scatter.9.cloned.1.call-update) | async-done | bytes 1179664 | tf_op jit(solution)/shard_map/reduce_scatter | solution.py:194
  1618.2 6.2 multiply_reduce_fusion.2
  1636.1 40.4 %all-reduce.116 = (f32[768]{0:T(1024)}, f32[768]{0:T(1024)}, f32[768]{0:T(1024)}, f32[384]{0:T(512)}, f32[384]{0:T(512)}, /*index=5*/f32[384]{0:T(512)}) all-reduce(f32[768]{0:T(1024)S(1)} %get-tuple-element.381, f32[768]{0:T(1024)S(1)} %copy-done.184, f32[768]{0:T(1024)S(1)} %copy-done.183, ...), channel_id=1, replica_groups=mesh['seq'=8,'batch'=4] {'seq','batch'}, use_global_device_ids=true, to_apply=%region_19.20 | all-reduce | flops 3456 | bytes 27648 | tf_op jit(solution)/shard_map/psum | solution.py:188
  1676.5 8.2 all-reduce.120.cloned.1.call-done
  (895 shorter events, 791.8 us)
Async XLA Ops:
  7.2 14.7 copy-start
  7.2 1358.6 %reduce-scatter.7.cloned.1.call-start = ((), (), s32[]{:S(2)}) async-start(), calls=%async_computation.5 | async-start | bytes 2654208 | tf_op jit(solution)/shard_map/reduce_scatter | solution.py:193
  11.2 16.0 copy-start.166
  11.3 16.0 copy-start.170
  11.3 16.0 copy-start.172
  11.6 10.3 copy-start.177
  183.6 36.8 %copy-start.114 = (f32[4,2688]{1,0:T(4,128)}, f32[4,2688]{1,0:T(4,128)S(1)}, u32[]{:S(2)}) copy-start(f32[4,2688]{1,0:T(4,128)S(1)} %slice.950) | copy-start | bytes 129028
  186.0 34.3 %copy-start.115 = (f32[4,2688]{1,0:T(4,128)}, f32[4,2688]{1,0:T(4,128)S(1)}, u32[]{:S(2)}) copy-start(f32[4,2688]{1,0:T(4,128)S(1)} %slice.980) | copy-start | bytes 129028
  207.1 6.7 copy-start.160
  207.1 6.7 copy-start.161
  241.2 6.5 copy-start.93
  241.2 6.5 copy-start.96
  247.7 9.2 copy-start.113
  248.4 9.9 copy-start.112
  248.4 11.4 copy-start.133
  259.7 11.4 copy-start.68
  259.7 11.4 copy-start.70
  284.6 8.3 copy-start.150
  285.3 11.8 copy-start.151
  306.0 8.6 copy-start.41
  319.5 6.5 copy-start.87
  320.3 7.7 copy-start.142
  370.7 70.0 %copy-start.162 = (f32[1,1,7,384]{3,1,2,0:T(1,128)S(1)}, f32[1,1,7,384]{3,1,2,0:T(1,128)}, u32[]{:S(2)}) copy-start(f32[1,1,7,384]{3,1,2,0:T(1,128)} %copy.40) | copy-start | bytes 32260
  453.1 68.3 %copy-start.118 = (f32[7,384]{1,0:T(8,128)S(1)}, f32[7,384]{1,0:T(8,128)}, u32[]{:S(2)}) copy-start(f32[7,384]{1,0:T(8,128)} %custom-call.1) | copy-start | bytes 32260
  453.1 68.3 %copy-start.120 = (f32[7,384]{1,0:T(8,128)S(1)}, f32[7,384]{1,0:T(8,128)}, u32[]{:S(2)}) copy-start(f32[7,384]{1,0:T(8,128)} %custom-call) | copy-start | bytes 32260
  521.9 7.0 copy-start.119
  522.0 6.9 copy-start.121
  542.2 26.1 %copy-start.57 = (f32[1008,768]{1,0:T(8,128)}, f32[1008,768]{1,0:T(8,128)S(1)}, u32[]{:S(2)}) copy-start(f32[1008,768]{1,0:T(8,128)S(1)} %get-tuple-element.605) | copy-start | bytes 9289732
  542.3 8.1 copy-start.31
  542.3 8.1 copy-start.186
  573.8 792.1 %reduce-scatter.11.cloned.1.call-start = ((), (), s32[]{:S(2)}) async-start(), calls=%async_computation.7 | async-start | bytes 5308416 | tf_op jit(solution)/shard_map/reduce_scatter | solution.py:195
  581.0 870.5 %reduce-scatter.5.cloned.1.call-start = ((), (), s32[]{:S(2)}) async-start(), calls=%async_computation.4 | async-start | bytes 6635520 | tf_op jit(solution)/shard_map/reduce_scatter | solution.py:192
  620.6 7.0 copy-start.2
  838.1 31.8 %copy-start.116 = (f32[4,2688]{1,0:T(4,128)}, f32[4,2688]{1,0:T(4,128)S(1)}, u32[]{:S(2)}) copy-start(f32[4,2688]{1,0:T(4,128)S(1)} %slice.1099) | copy-start | bytes 129028
  838.7 31.2 %copy-start.117 = (f32[4,2688]{1,0:T(4,128)}, f32[4,2688]{1,0:T(4,128)S(1)}, u32[]{:S(2)}) copy-start(f32[4,2688]{1,0:T(4,128)S(1)} %slice.1129) | copy-start | bytes 129028
  855.4 12.9 copy-start.135
  921.9 16.0 copy-start.132
  952.5 8.4 copy-start.153
  954.8 10.3 copy-start.154
  990.7 13.5 copy-start.86
  1006.1 8.8 copy-start.85
  1157.5 144.4 %copy-start.125 = (f32[7,384]{1,0:T(8,128)S(1)}, f32[7,384]{1,0:T(8,128)}, u32[]{:S(2)}) copy-start(f32[7,384]{1,0:T(8,128)} %custom-call.3) | copy-start | bytes 32260
  1157.5 144.4 %copy-start.126 = (f32[7,384]{1,0:T(8,128)S(1)}, f32[7,384]{1,0:T(8,128)}, u32[]{:S(2)}) copy-start(f32[7,384]{1,0:T(8,128)} %custom-call.2) | copy-start | bytes 32260
  1177.9 124.6 %copy-start.136 = (f32[1,1,7,384]{3,1,2,0:T(1,128)S(1)}, f32[1,1,7,384]{3,1,2,0:T(1,128)}, u32[]{:S(2)}) copy-start(f32[1,1,7,384]{3,1,2,0:T(1,128)} %copy.43) | copy-start | bytes 32260
  1177.9 124.6 %copy-start.137 = (f32[1,1,7,384]{3,1,2,0:T(1,128)S(1)}, f32[1,1,7,384]{3,1,2,0:T(1,128)}, u32[]{:S(2)}) copy-start(f32[1,1,7,384]{3,1,2,0:T(1,128)} %copy.44) | copy-start | bytes 32260
  1323.4 9.0 copy-start.91
  1338.7 279.4 %reduce-scatter.9.cloned.1.call-start = ((), (), s32[]{:S(2)}) async-start(), calls=%async_computation.6 | async-start | bytes 10616832 | tf_op jit(solution)/shard_map/reduce_scatter | solution.py:194
  1351.9 332.8 %all-reduce.120.cloned.1.call-start = ((), (), s32[]{:S(2)}) async-start(), calls=%async_computation.8 | async-start | bytes 5603328 | tf_op jit(solution)/shard_map/psum | solution.py:197
  (147 other events, 440.2 us)
Sparse Core Ops, SparseCore 0:
  573.9 69.8 reduce-scatter.6
  647.4 94.3 reduce-scatter.10
  1338.8 112.6 reduce-scatter.4
  1455.0 163.1 reduce-scatter.8
  1620.6 64.0 all-reduce.119
where the time goes:
time: 1730 us; the launch traced here: 1700 us
  local copies, waits for them, and re-layouts  836 us (48%)
  blocking collectives  287 us (17%)
  waiting for transfers between devices  261 us (15%)
  other arithmetic  214 us (12%)
  matrix products  82.2 us (5%)
    slice x99, local copies, waits for them, and re-layouts, per_device(): lax.associative_scan(combine, (next_r, next_i, seed_r, seed_i), reverse=T...  269 us
    all_gather x8, blocking collectives, prefix(): pieces = jax.tree.map(lambda part: lax.all_gather(part, axis), value)  246 us
    reduce_scatter x1, waiting for transfers between devices, per_device(): lax.psum_scatter(grad_gu, 'seq', scatter_dimension=0, tiled=True)  167 us
    slice x87, local copies, waits for them, and re-layouts, per_device(): lax.associative_scan(combine, (mult_r, mult_i, feed_r, feed_i), axis=0)  141 us
    pad x48, local copies, waits for them, and re-layouts, per_device(): lax.associative_scan(combine, (next_r, next_i, seed_r, seed_i), reverse=T...  112 us
    pad x48, local copies, waits for them, and re-layouts, per_device(): lax.associative_scan(combine, (mult_r, mult_i, feed_r, feed_i), axis=0)  112 us
    reduce_scatter x1, waiting for transfers between devices, per_device(): lax.psum_scatter(grad_mix, 'seq', scatter_dimension=0, tiled=True)  85.7 us
    rev x4, local copies, waits for them, and re-layouts, per_device(): lax.associative_scan(combine, (next_r, next_i, seed_r, seed_i), reverse=T...  81.6 us
  transfers between devices with their start and end apart: 5, of which 3 were waited for; matrix products, arithmetic and copies ran while one was open for 40% of the time, Pallas kernels for 0%

commit v1 on v0

v1 whole, which is shorter than its diff:
```python
import functools

import jax
import jax.numpy as jnp
import numpy as np
from jax import lax
from jax.experimental import pallas as pl
from jax.experimental.pallas import tpu as pltpu
from jax.sharding import PartitionSpec as P

epsilon = 1e-06
LANES = 128
SUB = 8
F32 = jnp.float32
BF16 = jnp.bfloat16
MIB = 2**20
VM = 8


def sigmoid(values):
    return 0.5 * jnp.tanh(0.5 * values) + 0.5


def forget_gate(forget, lower):
    decay = jnp.exp(jnp.minimum(-forget, 80.0))
    total = 1.0 + decay
    guess = pl.reciprocal(total, approx=True)
    open_part = guess * (2.0 - total * guess)
    shut_part = decay * open_part
    intake = (1.0 - lower) * shut_part
    return open_part, shut_part, intake, 1.0 - intake


def dot(left, right, left_dim, right_dim):
    return lax.dot_general(
        left, right, (((left_dim,), (right_dim,)), ((), ())), preferred_element_type=F32
    )


def row_block(rows, most):
    best = 16
    for size in range(16, most + 1, 16):
        if rows % size == 0:
            best = size
    return best


def rows_at(step, size):
    return pl.ds(pl.multiple_of(step * size, 16), size)


def tile_of(ref, tile):
    return ref[:, tile * LANES : (tile + 1) * LANES]


def fold_rows(values):
    rows, lanes = values.shape
    return jnp.sum(values.reshape(rows // SUB, SUB, lanes), axis=0)


def loop(count, body):
    lax.fori_loop(0, count, lambda step, _: (body(step), 0)[1], 0)


def project_kernel(shape, tokens, gain, weight, lower, fbias, phase, low, pre, chunks, ends):
    seqs, positions, chans = shape
    tiles = chans // LANES
    steps = positions // SUB
    rows = seqs * positions
    size = row_block(rows, 336)

    def project(step):
        at = rows_at(step, size)
        inputs = tokens[at, :].astype(F32)
        scale = lax.rsqrt(jnp.mean(inputs * inputs, axis=-1, keepdims=True) + epsilon)
        block = (inputs * scale * gain[...]).astype(BF16)
        low[at, :] = block
        for part in range(3):
            made = dot(block, weight[:, part * chans : (part + 1) * chans], 1, 0)
            if part == 2:
                made = made + fbias[...]
            for tile in range(tiles):
                pre[part * tiles + tile, at, :] = made[:, tile * LANES : (tile + 1) * LANES]

    loop(rows // size, project)

    cosine, sine = jnp.cos(phase[...]), jnp.sin(phase[...])

    def scan(seq):
        for tile in range(tiles):
            lanes = slice(tile * LANES, (tile + 1) * LANES)
            low_bound, cos_t, sin_t = lower[:, lanes], cosine[:, lanes], sine[:, lanes]
            product = jnp.ones((SUB, LANES), F32)
            state_r = jnp.zeros((SUB, LANES), F32)
            state_i = jnp.zeros((SUB, LANES), F32)
            for step in range(steps):
                at = pl.ds(seq * positions + step, SUB, stride=steps)
                in_r, in_i = pre[tile, at, :], pre[tiles + tile, at, :]
                _, _, intake, retain = forget_gate(pre[2 * tiles + tile, at, :], low_bound)
                mul_r, mul_i = retain * cos_t, retain * sin_t
                add_r, add_i = intake * (in_r * sigmoid(in_r)), intake * (in_i * sigmoid(in_i))
                state_r, state_i = (
                    mul_r * state_r - mul_i * state_i + add_r,
                    mul_r * state_i + mul_i * state_r + add_i,
                )
                product = product * retain
            at = pl.ds(pl.multiple_of(seq * SUB, SUB), SUB)
            chunks[tile, at, :] = product
            chunks[tiles + tile, at, :] = state_r
            chunks[2 * tiles + tile, at, :] = state_i

    chunks[...] = jnp.zeros(chunks.shape, F32)
    loop(seqs, scan)

    span_c, span_s = jnp.cos(phase[...] * steps), jnp.sin(phase[...] * steps)
    pad = ends.shape[1]
    for tile in range(tiles):
        lanes = slice(tile * LANES, (tile + 1) * LANES)
        mul_r, mul_i = jnp.ones((pad, LANES), F32), jnp.zeros((pad, LANES), F32)
        add_r, add_i = jnp.zeros((pad, LANES), F32), jnp.zeros((pad, LANES), F32)
        for chunk in range(SUB):
            at = pl.ds(chunk, pad, stride=SUB)
            product = chunks[tile, at, :]
            new_r, new_i = product * span_c[:, lanes], product * span_s[:, lanes]
            plus_r, plus_i = chunks[tiles + tile, at, :], chunks[2 * tiles + tile, at, :]
            mul_r, mul_i = mul_r * new_r - mul_i * new_i, mul_r * new_i + mul_i * new_r
            add_r, add_i = (
                new_r * add_r - new_i * add_i + plus_r,
                new_r * add_i + new_i * add_r + plus_i,
            )
        ends[tile] = mul_r
        ends[tiles + tile] = mul_i
        ends[2 * tiles + tile] = add_r
        ends[3 * tiles + tile] = add_i


def gate_kernel(low, weight, gate):
    rows, width = gate.shape
    chans3 = weight.shape[1] - width
    size = row_block(rows, 336)

    def step_of(step):
        at = rows_at(step, size)
        gate[at, :] = dot(low[at, :], weight[:, chans3:], 1, 0)

    loop(rows // size, step_of)


def hidden_back_kernel(upstream, weight, made):
    rows, units = made.shape
    size = row_block(rows, 336)

    def step_of(step):
        at = rows_at(step, size)
        for part in range(units // 256):
            cols = slice(part * 256, (part + 1) * 256)
            made[at, cols] = dot(upstream[at, :], weight[cols, :], 1, 1).astype(BF16)

    loop(rows // size, step_of)


def mix_kernel(
    shape, pre, chunks, start, gate, tokens, phase, lower, gain_out, gain_ffn, w_out,
    states, entries, mixed, after, ffn_low,
):
    seqs, positions, chans = shape
    tiles = chans // LANES
    steps = positions // SUB
    rows = seqs * positions
    size = row_block(rows, 144)
    pad = start.shape[1]
    span_c, span_s = jnp.cos(phase[...] * steps), jnp.sin(phase[...] * steps)
    for tile in range(tiles):
        lanes = slice(tile * LANES, (tile + 1) * LANES)
        now_r, now_i = start[tile], start[tiles + tile]
        for chunk in range(SUB):
            at = pl.ds(chunk, pad, stride=SUB)
            entries[tile, at, :] = now_r
            entries[tiles + tile, at, :] = now_i
            product = chunks[tile, at, :]
            new_r, new_i = product * span_c[:, lanes], product * span_s[:, lanes]
            now_r, now_i = (
                new_r * now_r - new_i * now_i + chunks[tiles + tile, at, :],
                new_r * now_i + new_i * now_r + chunks[2 * tiles + tile, at, :],
            )
    cosine, sine = jnp.cos(phase[...]), jnp.sin(phase[...])

    def scan(seq):
        for tile in range(tiles):
            lanes = slice(tile * LANES, (tile + 1) * LANES)
            low_bound, cos_t, sin_t = lower[:, lanes], cosine[:, lanes], sine[:, lanes]
            at = pl.ds(pl.multiple_of(seq * SUB, SUB), SUB)
            state_r, state_i = entries[tile, at, :], entries[tiles + tile, at, :]
            for step in range(steps):
                at = pl.ds(seq * positions + step, SUB, stride=steps)
                in_r, in_i = pre[tile, at, :], pre[tiles + tile, at, :]
                _, _, intake, retain = forget_gate(pre[2 * tiles + tile, at, :], low_bound)
                mul_r, mul_i = retain * cos_t, retain * sin_t
                add_r, add_i = intake * (in_r * sigmoid(in_r)), intake * (in_i * sigmoid(in_i))
                state_r, state_i = (
                    mul_r * state_r - mul_i * state_i + add_r,
                    mul_r * state_i + mul_i * state_r + add_i,
                )
                states[tile, at, :] = state_r
                states[tiles + tile, at, :] = state_i

    loop(seqs, scan)

    def mix(step):
        at = rows_at(step, size)
        squares = jnp.zeros((size, LANES), F32)
        for tile in range(2 * tiles):
            part = states[tile, at, :]
            squares = squares + part * part
        scale = lax.rsqrt(jnp.sum(squares, axis=-1, keepdims=True) / (2 * chans) + epsilon)
        for tile in range(2 * tiles):
            lanes = slice(tile * LANES, (tile + 1) * LANES)
            gated = gate[at, lanes]
            part = states[tile, at, :] * scale * gain_out[:, lanes] * (gated * sigmoid(gated))
            mixed[at, lanes] = part.astype(BF16)
        total = tokens[at, :].astype(F32) + dot(mixed[at, :], w_out[...], 1, 0)
        after[at, :] = total
        scale = lax.rsqrt(jnp.mean(total * total, axis=-1, keepdims=True) + epsilon)
        ffn_low[at, :] = (total * scale * gain_ffn[...]).astype(BF16)

    loop(rows // size, mix)


def ffn_kernel(ffn_low, w_gu, hidden_back, hidden, grad_gu):
    rows, units = hidden.shape
    size = row_block(rows, 336)
    wide = 256

    def step_of(step):
        at = rows_at(step, size)
        block = ffn_low[at, :]
        for part in range(units // wide):
            cols = slice(part * wide, (part + 1) * wide)
            later = slice(units + part * wide, units + (part + 1) * wide)
            gate = dot(block, w_gu[:, cols], 1, 0)
            up = dot(block, w_gu[:, later], 1, 0)
            back = hidden_back[at, cols].astype(F32)
            sigma = sigmoid(gate)
            act = gate * sigma
            hidden[at, cols] = (act * up).astype(BF16)
            grad_gu[at, cols] = (back * up * (sigma + act * (1.0 - sigma))).astype(BF16)
            grad_gu[at, later] = (back * act).astype(BF16)

    loop(rows // size, step_of)


def store_blocks(ref, slots, first, blocks, size, cols, values):
    for block in range(blocks):
        at = pl.ds(pl.multiple_of(slots[first + block] * size, SUB), size)
        ref[at, cols] = values[block * size : (block + 1) * size, :]


def grad_narrow_kernel(blocks, slots, *refs):
    pairs, (keep, send, turned) = refs[:-3], refs[-3:]
    mine = slots[2 * blocks]
    for index in range(len(pairs) // 2):
        left, right = pairs[2 * index], pairs[2 * index + 1]
        half = right.shape[1] // 2
        keep_at = pl.ds(pl.multiple_of(mine * half, LANES), half)
        send_at = pl.ds(pl.multiple_of((1 - mine) * half, LANES), half)
        turned[:, :half] = right[:, keep_at]
        turned[:, half:] = right[:, send_at]
        size = left.shape[1] // blocks
        tall = min(left.shape[1], 384)
        cols = slice(index * half, (index + 1) * half)
        for part in range(left.shape[1] // tall):
            made = dot(left[:, part * tall : (part + 1) * tall], turned[...], 0, 0)
            count = tall // size
            first = part * count
            store_blocks(keep, slots, first, count, size, cols, made[:, :half])
            store_blocks(send, slots, blocks + first, count, size, cols, made[:, half:])


def grad_wide_kernel(blocks, wide, slots, left, right, keep, send):
    mine = slots[2 * blocks]
    half = right.shape[1] // 2
    size = left.shape[1] // blocks

    def step_of(part):
        cols = pl.ds(pl.multiple_of(part * wide, LANES), wide)
        for ref, owner, base in ((keep, mine, 0), (send, 1 - mine, blocks)):
            source = pl.ds(pl.multiple_of(owner * half + part * wide, LANES), wide)
            made = dot(left[...], right[:, source], 0, 0)
            store_blocks(ref, slots, base, blocks, size, cols, made)

    loop(half // wide, step_of)


def middle_back_kernel(
    shape, grad_gu, w_gu, after, cotangent, gain_ffn, w_out, states, gate, gain_out, pre, chunks, lower, phase,
    grad_mid, grad_mid_low, grad_gate, seeds, chunks_back, ends_back, sums,
):
    seqs, positions, chans = shape
    tiles = chans // LANES
    steps = positions // SUB
    rows = seqs * positions
    width = 2 * chans
    size = row_block(rows, 336)
    sums[...] = jnp.zeros(sums.shape, F32)

    def ffn_back(step):
        at = rows_at(step, size)
        back = dot(grad_gu[at, :], w_gu[...], 1, 1)
        total = after[at, :]
        scale = lax.rsqrt(jnp.mean(total * total, axis=-1, keepdims=True) + epsilon)
        normed = total * scale
        sums[0:SUB, :] += fold_rows(back * normed)
        scaled = back * gain_ffn[...]
        shared = jnp.mean(scaled * normed, axis=-1, keepdims=True)
        made = cotangent[at, :].astype(F32) + scale * (scaled - normed * shared)
        grad_mid[at, :] = made
        grad_mid_low[at, :] = made.astype(BF16)

    loop(rows // size, ffn_back)
    small = row_block(rows, 144)

    def mix_back(step):
        at = rows_at(step, small)
        back = dot(grad_mid_low[at, :], w_out[...], 1, 1)
        squares = jnp.zeros((small, LANES), F32)
        for tile in range(2 * tiles):
            part = states[tile, at, :]
            squares = squares + part * part
        scale = lax.rsqrt(jnp.sum(squares, axis=-1, keepdims=True) / width + epsilon)
        shared = jnp.zeros((small, LANES), F32)
        for tile in range(2 * tiles):
            lanes = slice(tile * LANES, (tile + 1) * LANES)
            gated = gate[at, lanes]
            sigma = sigmoid(gated)
            act = gated * sigma
            normed = states[tile, at, :] * scale
            part = back[:, lanes]
            gain = gain_out[:, lanes]
            grad_gate[at, lanes] = (part * normed * gain * (sigma + act * (1.0 - sigma))).astype(BF16)
            inner = part * act
            product = inner * normed
            sums[SUB : 2 * SUB, lanes] += fold_rows(product)
            shared = shared + product * gain
            seeds[tile, at, :] = inner * gain
        mean = jnp.sum(shared, axis=-1, keepdims=True) / width
        for tile in range(2 * tiles):
            normed = states[tile, at, :] * scale
            seeds[tile, at, :] = scale * (seeds[tile, at, :] - normed * mean)

    loop(rows // small, mix_back)
    cosine, sine = jnp.cos(phase[...]), jnp.sin(phase[...])

    def scan(seq):
        for tile in range(tiles):
            lanes = slice(tile * LANES, (tile + 1) * LANES)
            low_bound, cos_t, sin_t = lower[:, lanes], cosine[:, lanes], sine[:, lanes]
            flow_r = jnp.zeros((SUB, LANES), F32)
            flow_i = jnp.zeros((SUB, LANES), F32)
            for step in reversed(range(steps)):
                at = pl.ds(seq * positions + step, SUB, stride=steps)
                _, _, _, retain = forget_gate(pre[2 * tiles + tile, at, :], low_bound)
                mul_r, mul_i = retain * cos_t, retain * sin_t
                adj_r = seeds[tile, at, :] + flow_r
                adj_i = seeds[tiles + tile, at, :] + flow_i
                flow_r = mul_r * adj_r + mul_i * adj_i
                flow_i = mul_r * adj_i - mul_i * adj_r
            at = pl.ds(pl.multiple_of(seq * SUB, SUB), SUB)
            chunks_back[tile, at, :] = flow_r
            chunks_back[tiles + tile, at, :] = flow_i

    chunks_back[...] = jnp.zeros(chunks_back.shape, F32)
    loop(seqs, scan)
    span_c, span_s = jnp.cos(phase[...] * steps), jnp.sin(phase[...] * steps)
    pad = ends_back.shape[1]
    for tile in range(tiles):
        lanes = slice(tile * LANES, (tile + 1) * LANES)
        mul_r, mul_i = jnp.ones((pad, LANES), F32), jnp.zeros((pad, LANES), F32)
        add_r, add_i = jnp.zeros((pad, LANES), F32), jnp.zeros((pad, LANES), F32)
        for chunk in reversed(range(SUB)):
            at = pl.ds(chunk, pad, stride=SUB)
            product = chunks[tile, at, :]
            new_r, new_i = product * span_c[:, lanes], -product * span_s[:, lanes]
            plus_r, plus_i = chunks_back[tile, at, :], chunks_back[tiles + tile, at, :]
            mul_r, mul_i = mul_r * new_r - mul_i * new_i, mul_r * new_i + mul_i * new_r
            add_r, add_i = (
                new_r * add_r - new_i * add_i + plus_r,
                new_r * add_i + new_i * add_r + plus_i,
            )
        ends_back[tile] = mul_r
        ends_back[tiles + tile] = mul_i
        ends_back[2 * tiles + tile] = add_r
        ends_back[3 * tiles + tile] = add_i


def scan_back_kernel(
    shape, blocks, slots, seeds, chunks, chunks_back, enter, pre, states, entries, lower, phase, low,
    grad_pre, sums, keep, send, entries_back, made_pre, turned,
):
    seqs, positions, chans = shape
    tiles = chans // LANES
    steps = positions // SUB
    rows = seqs * positions
    pad = enter.shape[1]
    span_c, span_s = jnp.cos(phase[...] * steps), jnp.sin(phase[...] * steps)
    for tile in range(tiles):
        lanes = slice(tile * LANES, (tile + 1) * LANES)
        now_r, now_i = enter[tile], enter[tiles + tile]
        for chunk in reversed(range(SUB)):
            at = pl.ds(chunk, pad, stride=SUB)
            entries_back[tile, at, :] = now_r
            entries_back[tiles + tile, at, :] = now_i
            product = chunks[tile, at, :]
            new_r, new_i = product * span_c[:, lanes], -product * span_s[:, lanes]
            now_r, now_i = (
                new_r * now_r - new_i * now_i + chunks_back[tile, at, :],
                new_r * now_i + new_i * now_r + chunks_back[tiles + tile, at, :],
            )
    cosine, sine = jnp.cos(phase[...]), jnp.sin(phase[...])
    sums[...] = jnp.zeros(sums.shape, F32)
    mine = slots[2 * blocks]
    half = keep.shape[1]
    shift = 3 * chans - half
    keep_at = pl.ds(pl.multiple_of(mine * shift, LANES), half)
    send_at = pl.ds(pl.multiple_of((1 - mine) * shift, LANES), half)

    def scan(seq):
        for tile in range(tiles):
            lanes = slice(tile * LANES, (tile + 1) * LANES)
            low_bound, cos_t, sin_t = lower[:, lanes], cosine[:, lanes], sine[:, lanes]
            chunk_at = pl.ds(pl.multiple_of(seq * SUB, SUB), SUB)
            flow_r, flow_i = entries_back[tile, chunk_at, :], entries_back[tiles + tile, chunk_at, :]
            sum_lower = jnp.zeros((SUB, LANES), F32)
            sum_fbias = jnp.zeros((SUB, LANES), F32)
            sum_phase = jnp.zeros((SUB, LANES), F32)
            for step in reversed(range(steps)):
                at = pl.ds(seq * positions + step, SUB, stride=steps)
                in_r, in_i = pre[tile, at, :], pre[tiles + tile, at, :]
                opened, shut, intake, retain = forget_gate(pre[2 * tiles + tile, at, :], low_bound)
                sig_r, sig_i = sigmoid(in_r), sigmoid(in_i)
                act_r, act_i = in_r * sig_r, in_i * sig_i
                adj_r = seeds[tile, at, :] + flow_r
                adj_i = seeds[tiles + tile, at, :] + flow_i
                mul_r, mul_i = retain * cos_t, retain * sin_t
                flow_r = mul_r * adj_r + mul_i * adj_i
                flow_i = mul_r * adj_i - mul_i * adj_r
                if step > 0:
                    before = pl.ds(seq * positions + step - 1, SUB, stride=steps)
                    past_r, past_i = states[tile, before, :], states[tiles + tile, before, :]
                else:
                    past_r, past_i = entries[tile, chunk_at, :], entries[tiles + tile, chunk_at, :]
                grad_r = adj_r * past_r + adj_i * past_i
                grad_i = adj_i * past_r - adj_r * past_i
                grad_retain = grad_r * cos_t + grad_i * sin_t - (adj_r * act_r + adj_i * act_i)
                sum_phase = sum_phase + retain * (grad_i * cos_t - grad_r * sin_t)
                sum_lower = sum_lower + grad_retain * shut
                grad_forget = grad_retain * intake * opened
                sum_fbias = sum_fbias + grad_forget
                at = pl.ds(step, SUB, stride=steps)
                made_pre[tile, at, :] = adj_r * intake * (sig_r + act_r * (1.0 - sig_r))
                made_pre[tiles + tile, at, :] = adj_i * intake * (sig_i + act_i * (1.0 - sig_i))
                made_pre[2 * tiles + tile, at, :] = grad_forget
            sums[0:SUB, lanes] += sum_lower
            sums[SUB : 2 * SUB, lanes] += sum_fbias
            sums[2 * SUB : 3 * SUB, lanes] += sum_phase

        seq_rows = rows_at(seq, positions)
        for tile in range(3 * tiles):
            grad_pre[seq_rows, tile * LANES : (tile + 1) * LANES] = made_pre[tile].astype(BF16)
        turned[seq_rows, :half] = grad_pre[seq_rows, keep_at]
        turned[seq_rows, half:] = grad_pre[seq_rows, send_at]

    loop(seqs, scan)
    block_rows = low.shape[1] // blocks
    tall = min(low.shape[1], 384)
    count = tall // block_rows
    for part in range(low.shape[1] // tall):
        made = dot(low[:, part * tall : (part + 1) * tall], turned[...], 0, 0)
        store_blocks(keep, slots, part * count, count, block_rows, slice(0, half), made[:, :half])
        store_blocks(
            send, slots, blocks + part * count, count, block_rows, slice(0, half), made[:, half:]
        )


def input_back_kernel(grad_pre, grad_gate, w_mix, tokens, gain, grad_mid, grad_tokens, sums):
    rows, chans3 = grad_pre.shape
    size = row_block(rows, 336)
    sums[...] = jnp.zeros(sums.shape, F32)

    def step_of(step):
        at = rows_at(step, size)
        back = dot(grad_pre[at, :], w_mix[:, :chans3], 1, 1)
        back = back + dot(grad_gate[at, :], w_mix[:, chans3:], 1, 1)
        inputs = tokens[at, :].astype(F32)
        scale = lax.rsqrt(jnp.mean(inputs * inputs, axis=-1, keepdims=True) + epsilon)
        normed = inputs * scale
        sums[...] += fold_rows(back * normed)
        scaled = back * gain[...]
        shared = jnp.mean(scaled * normed, axis=-1, keepdims=True)
        grad_tokens[at, :] = grad_mid[at, :] + scale * (scaled - normed * shared)

    loop(rows // size, step_of)


def output_kernel(after, hidden, w_down, output):
    rows, _ = output.shape
    size = row_block(rows, 336)

    def step_of(step):
        at = rows_at(step, size)
        output[at, :] = (after[at, :] + dot(hidden[at, :], w_down[...], 1, 0)).astype(BF16)

    loop(rows // size, step_of)


def call(kernel, name, args, outs, scratch=(), smem=0, vmem=VM, flops=0):
    in_specs = [pl.BlockSpec(memory_space=pltpu.SMEM)] * smem
    in_specs = in_specs + [pl.BlockSpec(memory_space=pltpu.VMEM)] * (len(args) - smem)
    made = pl.pallas_call(
        kernel,
        out_shape=[jax.ShapeDtypeStruct(shape, kind) for shape, kind in outs],
        in_specs=in_specs,
        out_specs=[pl.BlockSpec(memory_space=pltpu.VMEM)] * len(outs),
        scratch_shapes=list(scratch),
        compiler_params=pltpu.CompilerParams(vmem_limit_bytes=vmem * MIB),
        cost_estimate=pl.CostEstimate(flops=flops, bytes_accessed=1024, transcendentals=0),
        name=name,
    )(*args)
    return made


def flipped(seq_size, batch_size, dims):
    pairs = []
    for seq in range(seq_size):
        for batch in range(batch_size):
            axis, bit = dims[batch & 1]
            to = (seq ^ bit, batch) if axis == "seq" else (seq, batch ^ bit)
            pairs.append((seq * batch_size + batch, to[0] * batch_size + to[1]))
    return pairs


def step_orders(seq_size, batch_size):
    along_seq = [("seq", 1 << bit) for bit in range(seq_size.bit_length() - 1)]
    along_batch = [("batch", 1 << bit) for bit in range(1, batch_size.bit_length() - 1)]
    return (along_seq + along_batch, along_batch + along_seq)


def slot_table(seq_size, batch_size):
    orders = step_orders(seq_size, batch_size)
    seq, batch = lax.axis_index("seq"), lax.axis_index("batch")
    rest = batch_size // 2
    block = np.arange(seq_size * rest)
    seq_diff = jnp.asarray(block // rest, jnp.int32) ^ seq
    batch_diff = jnp.asarray((block % rest) * 2, jnp.int32) ^ (batch & ~1)

    def slots(order):
        count = len(order)
        total = jnp.zeros(block.shape, jnp.int32)
        for place, (axis, bit) in enumerate(order):
            diff = seq_diff if axis == "seq" else batch_diff
            total = total + jnp.where((diff & bit) != 0, 1 << (count - 1 - place), 0)
        return total

    first, second = slots(orders[0]), slots(orders[1])
    odd = (batch & 1) == 1
    keep, send = jnp.where(odd, second, first), jnp.where(odd, first, second)
    return jnp.concatenate([keep, send, (batch & 1).astype(jnp.int32)[None]])


def combine(earlier, later_part):
    mul_r, mul_i, add_r, add_i = earlier
    new_r, new_i, plus_r, plus_i = later_part
    out_mr = mul_r * new_r - mul_i * new_i
    out_mi = mul_r * new_i + mul_i * new_r
    out_ar = new_r * add_r - new_i * add_i + plus_r
    out_ai = new_r * add_i + new_i * add_r + plus_i
    return (out_mr, out_mi, out_ar, out_ai)


def carried(ends, backward):
    size = lax.axis_size("seq")
    mine = lax.axis_index("seq")
    tiles = ends.shape[0] // 4

    def parts(values):
        return tuple(values[part * tiles : (part + 1) * tiles] for part in range(4))

    total = ends
    one, zero = jnp.ones(ends[:tiles].shape, F32), jnp.zeros(ends[:tiles].shape, F32)
    before = (one, zero, zero, zero)
    bit = 1
    while bit < size:
        got = lax.ppermute(total, "seq", [(at, at ^ bit) for at in range(size)])
        later = (mine & bit) != 0
        if backward:
            later = jnp.logical_not(later)
        mine_parts, got_parts = parts(total), parts(got)
        longer = combine(got_parts, before)
        before = tuple(jnp.where(later, new, old) for new, old in zip(longer, before))
        if 2 * bit < size:
            first = tuple(jnp.where(later, b, a) for a, b in zip(mine_parts, got_parts))
            second = tuple(jnp.where(later, a, b) for a, b in zip(mine_parts, got_parts))
            total = jnp.concatenate(combine(first, second), axis=0)
        bit *= 2
    return jnp.concatenate([before[2], before[3]], axis=0)


def scatter_sum(keep, send, seq_size, batch_size):
    orders = step_orders(seq_size, batch_size)
    got = lax.ppermute(send, "batch", [(at, at ^ 1) for at in range(batch_size)])
    for first, second in zip(*orders):
        half = keep.shape[0] // 2
        out = keep[half:] + got[half:]
        keep = keep[:half] + got[:half]
        got = lax.ppermute(
            out, ("seq", "batch"), flipped(seq_size, batch_size, (first, second))
        )
    return keep + got


def gather_batch(values, bit, batch_size):
    other = lax.ppermute(values, "batch", [(at, at ^ bit) for at in range(batch_size)])
    upper = (lax.axis_index("batch") & bit) != 0
    return jnp.where(upper, other, values), jnp.where(upper, values, other)


def per_device(
    tokens, cotangent, gain_in, w_mix, lower, fbias, phase, gain_out, w_out, gain_ffn, w_gu, w_down
):
    seqs, positions, width = tokens.shape
    chans = lower.shape[0]
    units = w_down.shape[0]
    rows = seqs * positions
    tiles = chans // LANES
    shape = (seqs, positions, chans)
    pad = -(-seqs // SUB) * SUB
    seq_size, batch_size = lax.axis_size("seq"), lax.axis_size("batch")
    blocks = seq_size * batch_size // 2
    tokens = tokens.reshape(rows, width)
    cotangent = cotangent.reshape(rows, width)
    gain_in, gain_out, gain_ffn = gain_in[None], gain_out[None], gain_ffn[None]
    lower, fbias, phase = lower[None], fbias[None], phase[None]
    slots = slot_table(seq_size, batch_size)
    in_place = width % (blocks * SUB) == 0
    if in_place:
        made_blocks, used = blocks, slots
    else:
        made_blocks = 2 * SUB
        natural = jnp.arange(made_blocks, dtype=jnp.int32)
        used = jnp.concatenate([natural, natural, slots[2 * blocks :]])

    def arranged(keep, send):
        if in_place:
            return keep, send
        made = []
        for index, values in enumerate((keep, send)):
            order = jnp.argsort(slots[index * blocks : (index + 1) * blocks])
            cut = values.reshape((blocks, -1) + values.shape[1:])
            made.append(jnp.take(cut, order, axis=0).reshape(values.shape))
        return made

    def reduced(keep, send):
        keep, send = arranged(keep, send)
        return scatter_sum(keep, send, seq_size, batch_size)

    low, pre, chunks, ends = call(
        functools.partial(project_kernel, shape), "project",
        (tokens, gain_in, w_mix, lower, fbias, phase),
        [((rows, width), BF16), ((3 * tiles, rows, LANES), F32), ((3 * tiles, pad * SUB, LANES), F32), ((4 * tiles, pad, LANES), F32)],
        flops=2 * rows * width * 3 * chans,
    )
    (gate,) = call(gate_kernel, "gate", (low, w_mix), [((rows, width), F32)], flops=2 * rows * width * width)
    (hidden_back,) = call(
        hidden_back_kernel, "hidden_back", (cotangent, w_down), [((rows, units), BF16)], flops=2 * rows * width * units
    )
    start = carried(ends, False)
    states, entries, mixed, after, ffn_low = call(
        functools.partial(mix_kernel, shape), "mix",
        (pre, chunks, start, gate, tokens, phase, lower, gain_out, gain_ffn, w_out),
        [((2 * tiles, rows, LANES), F32), ((2 * tiles, pad * SUB, LANES), F32), ((rows, width), BF16), ((rows, width), F32), ((rows, width), BF16)],
        flops=2 * rows * width * width,
    )
    hidden, grad_gu = call(
        ffn_kernel, "ffn", (ffn_low, w_gu, hidden_back),
        [((rows, units), BF16), ((rows, 2 * units), BF16)], flops=4 * rows * width * units,
    )
    down = call(
        functools.partial(grad_narrow_kernel, made_blocks), "grad_down", (used, hidden, cotangent),
        [((units, width // 2), F32)] * 2, [pltpu.VMEM((rows, width), BF16)], smem=1, flops=2 * rows * width * units,
    )
    wide = call(
        functools.partial(grad_wide_kernel, made_blocks, 512), "grad_gu", (used, ffn_low, grad_gu),
        [((width, units), F32)] * 2, smem=1, flops=4 * rows * width * units,
    )
    grad_mid, grad_mid_low, grad_gate, seeds, chunks_back, ends_back, sums_mid = call(
        functools.partial(middle_back_kernel, shape), "middle_back",
        (grad_gu, w_gu, after, cotangent, gain_ffn, w_out, states, gate, gain_out, pre, chunks, lower, phase),
        [((rows, width), F32), ((rows, width), BF16), ((rows, width), BF16), ((2 * tiles, rows, LANES), F32),
         ((2 * tiles, pad * SUB, LANES), F32), ((4 * tiles, pad, LANES), F32), ((2 * SUB, width), F32)],
        flops=2 * rows * width * (2 * units + width),
    )
    third = call(
        functools.partial(grad_narrow_kernel, made_blocks), "grad_out_gate",
        (used, mixed, grad_mid_low, low, grad_gate),
        [((width, width), F32)] * 2, [pltpu.VMEM((rows, width), BF16)], smem=1, flops=4 * rows * width * width,
    )
    enter = carried(ends_back, True)
    span = -(-3 * tiles // 2) * LANES
    grad_pre, sums_scan, *fourth = call(
        functools.partial(scan_back_kernel, shape, made_blocks), "scan_back",
        (used, seeds, chunks, chunks_back, enter, pre, states, entries, lower, phase, low),
        [((rows, 3 * chans), BF16), ((3 * SUB, chans), F32), ((width, span), F32), ((width, span), F32)],
        [pltpu.VMEM((2 * tiles, pad * SUB, LANES), F32), pltpu.VMEM((3 * tiles, positions, LANES), F32), pltpu.VMEM((rows, 2 * span), BF16)],
        smem=1, flops=2 * rows * width * 3 * chans,
    )
    grad_tokens, sums_in = call(
        input_back_kernel, "input_back", (grad_pre, grad_gate, w_mix, tokens, gain_in, grad_mid),
        [((rows, width), F32), ((SUB, width), F32)], flops=2 * rows * width * (3 * chans + width),
    )
    (output,) = call(
        output_kernel, "output", (after, hidden, w_down), [((rows, width), BF16)], flops=2 * rows * width * units
    )

    parts = [reduced(*pair) for pair in (down, wide, third, fourth)]
    gathered = []
    for part in parts:
        bit = 2
        while bit < batch_size:
            part = jnp.concatenate(gather_batch(part, bit, batch_size), axis=0)
            bit *= 2
        gathered.append(part)
    sides = [gather_batch(part, 1, batch_size) for part in gathered]
    half = width // 2
    grad_down = jnp.concatenate(sides[0], axis=1)
    grad_wide = jnp.concatenate(sides[1], axis=1)
    grad_out = jnp.concatenate([side[:, :half] for side in sides[2]], axis=1)
    shared = 2 * span - 3 * chans
    grad_mix = jnp.concatenate(
        [sides[3][0], sides[3][1][:, shared:]] + [side[:, half:] for side in sides[2]], axis=1
    )

    vectors = jnp.concatenate(
        [
            jnp.sum(sums_in, axis=0),
            jnp.sum(sums_mid.reshape(2, SUB, width), axis=1)[::-1].reshape(-1),
            jnp.sum(sums_scan.reshape(3, SUB, chans), axis=1).reshape(-1),
        ]
    ).reshape(-1, LANES)
    for axis, size in (("batch", batch_size), ("seq", seq_size)):
        bit = 1
        while bit < size:
            vectors = vectors + lax.ppermute(vectors, axis, [(at, at ^ bit) for at in range(size)])
            bit *= 2
    vectors = vectors.reshape(-1)
    cuts = np.cumsum([width, width, width, chans, chans]).tolist()
    gains = jnp.split(vectors, cuts)
    return (
        output.reshape(seqs, positions, width),
        grad_tokens.reshape(seqs, positions, width),
        grad_mix,
        grad_out,
        grad_wide,
        grad_down,
        *gains,
    )


def solution(mesh):
    in_specs = (P("batch", "seq", None), P("batch", "seq", None)) + (P(),) * 10
    rows = P("seq", None)
    out_specs = (P("batch", "seq", None), P("batch", "seq", None), rows, rows, rows, rows) + (P(),) * 6
    return jax.shard_map(
        per_device, mesh=mesh, in_specs=in_specs, out_specs=out_specs, check_vma=False
    )
```

time: 1730 us -> 328 us (0.19); the launches traced: 1700 us -> 327 us
  local copies, waits for them, and re-layouts: 836 us -> 60.7 us
  blocking collectives: 287 us -> 0 us
  other arithmetic: 214 us -> 20.3 us
  waiting for transfers between devices: 261 us -> 114 us
  matrix products: 82.2 us -> 0 us
  Pallas kernels: 0 us -> 72 us
  starting transfers between devices: 0.46 us -> 58 us
    slice x189 -> x1, local copies, waits for them, and re-layouts: 418 us -> 0.04 us  [per_device(): grad_out = jnp.concatenate([side[:, :half] for side in sides[2]], axis=1)]
    reduce_scatter x4 -> x0, waiting for transfers between devices: 252 us -> none  [the longest x1 167 us: per_device(): lax.psum_scatter(grad_gu, 'seq', scatter_dimension=0, tiled=True)]
    all_gather x8 -> x0, blocking collectives: 246 us -> none  [prefix(): pieces = jax.tree.map(lambda part: lax.all_gather(part, axis), value)]
    pad x96 -> x0, local copies, waits for them, and re-layouts: 225 us -> none  [the longest x48 112 us: per_device(): lax.associative_scan(combine, (next_r, next_i, seed_r, seed_i), reverse=T...]
    ppermute x0 -> x39, waiting for transfers between devices: none -> 114 us  [the longest x16 88.3 us: scatter_sum(): lax.ppermute(out, ('seq', 'batch'), flipped(seq_size, batch_size, (first,...]
    dot_general x12 -> x0, matrix products: 82.2 us -> none  [the longest x4 31.1 us: back_product(): lax.dot_general(grad, weight, (((1,), (1,)), ((), ())), preferred_element...]
    add x61 -> x25, other arithmetic: 95.6 us -> 13.9 us  [the longest x12 13.7 us: scatter_sum(): keep = keep[:half] + got[:half]]
    rev x8 -> x1, local copies, waits for them, and re-layouts: 81.7 us -> 0.18 us  [per_device(): jnp.sum(sums_mid.reshape(2, SUB, width), axis=1)[::-1].reshape(-1)]
  transfers between devices with their start and end apart: 5 -> 39, of which waited for: 3 -> 20; matrix products, arithmetic and copies ran while one was open for 40% -> 6% of each run, Pallas kernels for 0% -> 13%
where the time goes in v1:
time: 328 us; the launch traced here: 327 us
  waiting for transfers between devices  114 us (35%)
  Pallas kernels  72 us (22%)
  local copies, waits for them, and re-layouts  60.7 us (19%)
  starting transfers between devices  58 us (18%)
  other arithmetic  20.3 us (6%)
    ppermute x16, waiting for transfers between devices, scatter_sum(): lax.ppermute(out, ('seq', 'batch'), flipped(seq_size, batch_size, (first,...  88.3 us
    pallas_call x12, Pallas kernels, call(): pl.pallas_call(kernel, out_shape=[jax.ShapeDtypeStruct(shape, kind) for s...  72 us
    unnamed x142, local copies, waits for them, and re-layouts  55.8 us
    ppermute x8, starting transfers between devices, gather_batch(): lax.ppermute(values, 'batch', [(at, at ^ bit) for at in range(batch_size)])  24.8 us
    ppermute x16, starting transfers between devices, scatter_sum(): lax.ppermute(out, ('seq', 'batch'), flipped(seq_size, batch_size, (first,...  16.5 us
    add x12, other arithmetic, scatter_sum(): keep = keep[:half] + got[:half]  13.7 us
    ppermute x5, waiting for transfers between devices, per_device(): lax.ppermute(vectors, axis, [(at, at ^ bit) for at in range(size)])  13.6 us
    ppermute x6, starting transfers between devices, carried(): got = lax.ppermute(total, 'seq', [(at, at ^ bit) for at in range(size)])  10.2 us
  transfers between devices with their start and end apart: 39, of which 20 were waited for; matrix products, arithmetic and copies ran while one was open for 6% of the time, Pallas kernels for 13%

profile of v1, /device:TPU:0, one launch (start us, length us, event | category | flops | bytes accessed | tf_op | source)
XLA Modules:
  0.0 326.6 jit_solution(4123040260764729208)
XLA Ops:
  3.4 1.8 copy-done.6
  6.6 5.2 %project.1 = (bf16[1008,768]{1,0:T(8,128)(2,1)S(1)}, f32[9,1008,128]{2,1,0:T(8,128)S(1)}, f32[9,64,128]{2,1,0:T(8,128)S(1)}, f32[12,8,128]{2,1,0:T(8,128)S(1)}) custom-call(bf16[1008,768]{1,0:T(8,128)(2,1)S(1)} %bitcast.31, f32[1,768]{1,0:T(1,128)S(1)} %broadcast_in_dim.43.gain, bf16[768,1920]{1,0:T(8,128)(2,1)S(1)} %copy-done.6, ...), custom_call_target="tpu_custom_call" | custom-call | flops 1783627776 | bytes 1024 | tf_op jit(solution)/shard_map/project/pallas_call | solution.py:518
  11.8 2.1 copy-done
  15.0 3.0 collective-permute-start
  20.1 2.2 collective-permute-start.1
  23.7 3.0 hidden_back.1
  28.4 2.6 collective-permute-start.2
  31.0 1.8 copy-done.7
  38.2 2.3 copy-done.1
  43.2 5.9 %mix.1 = (f32[6,1008,128]{2,1,0:T(8,128)S(1)}, f32[6,64,128]{2,1,0:T(8,128)S(1)}, bf16[1008,768]{1,0:T(8,128)(2,1)S(1)}, f32[1008,768]{1,0:T(8,128)S(1)}, bf16[1008,768]{1,0:T(8,128)(2,1)S(1)}) custom-call(f32[9,1008,128]{2,1,0:T(8,128)S(1)} %copy-done.1, f32[9,64,128]{2,1,0:T(8,128)S(1)} %get-tuple-element.43.chunks, ...), custom_call_target="tpu_custom_call" | custom-call | flops 1189085184 | bytes 1024 | tf_op jit(solution)/shard_map/mix/pallas_call | solution.py:518
  51.0 5.1 %copy-done.21 = bf16[768,3072]{1,0:T(8,128)(2,1)S(1)} copy-done((bf16[768,3072]{1,0:T(8,128)(2,1)S(1)}, bf16[768,3072]{1,0:T(8,128)(2,1)}, u32[]{:S(2)}) %copy-start.21) | copy-done | bytes 4718616
  56.0 7.2 %ffn.1 = (bf16[1008,1536]{1,0:T(8,128)(2,1)S(1)}, bf16[1008,3072]{1,0:T(8,128)(2,1)S(1)}) custom-call(bf16[1008,768]{1,0:T(8,128)(2,1)S(1)} %get-tuple-element.47.ffn_low.left, bf16[768,3072]{1,0:T(8,128)(2,1)S(1)} %copy-done.21, bf16[1008,1536]{1,0:T(8,128)(2,1)S(1)} %copy-done.55), custom_call_target="tpu_custom_call" | custom-call | flops 4756340736 | bytes 1024 | tf_op jit(solution)/shard_map/ffn/pallas_call | solution.py:518
  63.4 12.7 %middle_back.1 = (f32[1008,768]{1,0:T(8,128)S(1)}, bf16[1008,768]{1,0:T(8,128)(2,1)S(1)}, bf16[1008,768]{1,0:T(8,128)(2,1)S(1)}, f32[6,1008,128]{2,1,0:T(8,128)S...) custom-call(bf16[1008,3072]{1,0:T(8,128)(2,1)S(1)} %get-tuple-element.49.grad_gu.right, ...), custom_call_target="tpu_custom_call" | custom-call | flops 5945425920 | bytes 1024 | tf_op jit(solution)/shard_map/middle_back/pallas_call | solution.py:518
  76.1 1.7 copy-done.22
  84.1 2.5 collective-permute-done.3
  87.3 3.9 %collective-permute-done.4 = f32[12,8,128]{2,1,0:T(8,128)S(1)} collective-permute-done((f32[12,8,128]{2,1,0:T(8,128)S(1)}, f32[12,8,128]{2,1,0:T(8,128)S(1)}, u32[]{:S(2)}, u32[]{:S(2)}) %collective-permute-start.4) | collective-permute-done | bytes 49184 | tf_op jit(solution)/shard_map/ppermute | solution.py:592
  91.6 2.9 copy-done.10
  96.0 8.3 %grad_gu.1 = (f32[768,1536]{1,0:T(8,128)S(1)}, f32[768,1536]{1,0:T(8,128)}) custom-call(s32[33]{0:T(128)S(1)} %pad_add_fusion.slots, bf16[1008,768]{1,0:T(8,128)(2,1)S(1)} %copy-done.53, bf16[1008,3072]{1,0:T(8,128)(2,1)S(1)} %copy-done.10), custom_call_target="tpu_custom_call" | custom-call | flops 4756340736 | bytes 1024 | tf_op jit(solution)/shard_map/grad_gu/pallas_call | solution.py:518
  104.3 2.1 copy-done.18
  106.6 8.1 %scan_back.1 = (bf16[1008,1152]{1,0:T(8,128)(2,1)S(1)}, f32[24,384]{1,0:T(8,128)S(1)}, f32[768,640]{1,0:T(8,128)S(1)}, f32[768,640]{1,0:T(8,128)}) custom-call(s32[33]{0:T(128)S(1)} %pad_add_fusion.slots, f32[6,1008,128]{2,1,0:T(8,128)S(1)} %copy-done.25, f32[9,64,128]{2,1,0:T(8,128)S(1)} %get-tuple-element.43.chunks, f32[6,64,128]{2,1,0:T(8,128)S(1)} %copy-done.47, ...), custom_call_target="tpu_custom_call" | custom-call | flops 1783627776 | bytes 1024 | tf_op jit(solution)/shard_map/scan_back/pallas_call | solution.py:518
  115.2 4.7 %grad_down.1 = (f32[1536,384]{1,0:T(8,128)S(1)}, f32[1536,384]{1,0:T(8,128)}) custom-call(s32[33]{0:T(128)S(1)} %pad_add_fusion.slots, bf16[1008,1536]{1,0:T(8,128)(2,1)S(1)} %copy-done.27, bf16[1008,768]{1,0:T(8,128)(2,1)S(1)} %bitcast.40), custom_call_target="tpu_custom_call" | custom-call | flops 2378170368 | bytes 1024 | tf_op jit(solution)/shard_map/grad_down/pallas_call | solution.py:518
  127.1 4.7 %grad_out_gate.1 = (f32[768,768]{1,0:T(8,128)S(1)}, f32[768,768]{1,0:T(8,128)}) custom-call(s32[33]{0:T(128)S(1)} %pad_add_fusion.slots, bf16[1008,768]{1,0:T(8,128)(2,1)S(1)} %copy-done.49, bf16[1008,768]{1,0:T(8,128)(2,1)S(1)} %copy-done.51, bf16[1008,768]{1,0:T(8,128)(2,1)S(1)} %copy-done.17, bf16[1008,768]{1,0:T(8,128)(2,1)S(1)} %copy-done.42), custom_call_target="tpu_custom_call" | custom-call | flops 2378170368 | bytes 1024 | tf_op jit(solution)/shard_map/grad_out_gate/pallas_call | solution.py:518
  135.2 1.9 copy-done.23
  140.2 6.2 %input_back.1 = (f32[1008,768]{1,0:T(8,128)}, f32[8,768]{1,0:T(8,128)S(1)}) custom-call(bf16[1008,1152]{1,0:T(8,128)(2,1)S(1)} %copy-done.36, bf16[1008,768]{1,0:T(8,128)(2,1)S(1)} %copy-done.43, bf16[768,1920]{1,0:T(8,128)(2,1)S(1)} %copy-done.8, bf16[1008,768]{1,0:T(8,128)(2,1)S(1)} %bitcast.33, f32[1,768]{1,0:T(1,128)S(1)} %broadcast_in_dim.43.gain, ...), custom_call_target="tpu_custom_call" | custom-call | flops 2972712960 | bytes 1024 | tf_op jit(solution)/shard_map/input_back/pallas_call | solution.py:518
  146.4 3.7 %slice_add_fusion.9 = (f32[384,640]{1,0:T(8,128)}, f32[384,640]{1,0:T(8,128)}) fusion(f32[768,640]{1,0:T(8,128)} %collective-permute-done.6, f32[768,640]{1,0:T(8,128)} %copy-done.37), kind=kLoop, calls=%fused_computation.10 | loop fusion | flops 491520 | bytes 5898240 | tf_op jit(solution)/shard_map/add | solution.py:613
  154.5 2.4 collective-permute-done.35
  157.9 6.7 %collective-permute-done.36 = f32[27,128]{1,0:T(8,128)S(1)} collective-permute-done((f32[27,128]{1,0:T(8,128)S(1)}, f32[27,128]{1,0:T(8,128)S(1)}, u32[]{:S(2)}, u32[]{:S(2)}) %collective-permute-start.36) | collective-permute-done | bytes 13856 | tf_op jit(solution)/shard_map/ppermute | solution.py:751
  165.1 3.3 %collective-permute-done.37 = f32[27,128]{1,0:T(8,128)S(1)} collective-permute-done((f32[27,128]{1,0:T(8,128)S(1)}, f32[27,128]{1,0:T(8,128)S(1)}, u32[]{:S(2)}, u32[]{:S(2)}) %collective-permute-start.37) | collective-permute-done | bytes 13856 | tf_op jit(solution)/shard_map/ppermute | solution.py:751
  168.4 2.4 collective-permute-start.38
  170.8 1.9 copy-done.28
  174.4 4.3 %output.1 = bf16[1008,768]{1,0:T(8,128)(2,1)} custom-call(f32[1008,768]{1,0:T(8,128)S(1)} %copy-done.5, bf16[1008,1536]{1,0:T(8,128)(2,1)S(1)} %copy-done.28, bf16[1536,768]{1,0:T(8,128)(2,1)S(1)} %copy-done.34), custom_call_target="tpu_custom_call" | custom-call | flops 2378170368 | bytes 1024 | tf_op jit(solution)/shard_map/output/pallas_call | solution.py:518
  180.8 2.1 slice_add_fusion.3
  184.5 2.1 slice_add_fusion.7
  187.2 2.3 collective-permute-done.8
  190.1 3.4 %slice_add_fusion.1 = (f32[384,1536]{1,0:T(8,128)S(1)}, f32[384,1536]{1,0:T(8,128)S(1)}) fusion(f32[768,1536]{1,0:T(8,128)} %collective-permute-done.20, f32[768,1536]{1,0:T(8,128)S(1)} %bitcast.35), kind=kLoop, calls=%fused_computation.1 | loop fusion | flops 1179648 | bytes 14155776 | tf_op jit(solution)/shard_map/add | solution.py:613
  195.7 3.3 %collective-permute-done.9 = f32[96,640]{1,0:T(8,128)S(1)} collective-permute-done((f32[96,640]{1,0:T(8,128)S(1)}, f32[96,640]{1,0:T(8,128)S(1)}, u32[]{:S(2)}, u32[]{:S(2)}) %collective-permute-start.9) | collective-permute-done | bytes 245792 | tf_op jit(solution)/shard_map/ppermute | solution.py:614
  202.4 3.0 collective-permute-done.10
  207.0 16.3 %collective-permute-done.14 = f32[384,768]{1,0:T(8,128)S(1)} collective-permute-done((f32[384,768]{1,0:T(8,128)S(1)}, f32[384,768]{1,0:T(8,128)S(1)}, u32[]{:S(2)}, u32[]{:S(2)}) %collective-permute-start.14) | collective-permute-done | bytes 1179680 | tf_op jit(solution)/shard_map/ppermute | solution.py:614
  223.9 18.2 %collective-permute-start.12 = (f32[96,640]{1,0:T(8,128)S(1)}, f32[96,640]{1,0:T(8,128)S(1)}, u32[]{:S(2)}, u32[]{:S(2)}) collective-permute-start(f32[96,640]{1,0:T(8,128)S(1)} %pad_maximum_fusion.7), channel_id=1, source_target_pairs={{0,1},{1,0},{2,3},{3,2},{4,5},{5,4},{6,7},{7,6},{8,9},{9,8},{10,11... | collective-permute-start | bytes 737288 | tf_op jit(solution)/shard_map/ppermute | solution.py:621
  242.8 2.5 collective-permute-start.16
  245.4 12.4 %collective-permute-done.21 = f32[384,1536]{1,0:T(8,128)S(1)} collective-permute-done((f32[384,1536]{1,0:T(8,128)S(1)}, f32[384,1536]{1,0:T(8,128)S(1)}, u32[]{:S(2)}, u32[]{:S(2)}) %collective-permute-start.21) | collective-permute-done | bytes 2359328 | tf_op jit(solution)/shard_map/ppermute | solution.py:614
  260.2 5.5 %collective-permute-done.16 = f32[96,768]{1,0:T(8,128)S(1)} collective-permute-done((f32[96,768]{1,0:T(8,128)S(1)}, f32[96,768]{1,0:T(8,128)S(1)}, u32[]{:S(2)}, u32[]{:S(2)}) %collective-permute-start.16) | collective-permute-done | bytes 294944 | tf_op jit(solution)/shard_map/ppermute | solution.py:614
  267.9 3.7 %collective-permute-done.17 = f32[48,768]{1,0:T(8,128)S(1)} collective-permute-done((f32[48,768]{1,0:T(8,128)S(1)}, f32[48,768]{1,0:T(8,128)S(1)}, u32[]{:S(2)}, u32[]{:S(2)}) %collective-permute-start.17) | collective-permute-done | bytes 147488 | tf_op jit(solution)/shard_map/ppermute | solution.py:614
  273.2 11.4 %collective-permute-done.22 = f32[192,1536]{1,0:T(8,128)S(1)} collective-permute-done((f32[192,1536]{1,0:T(8,128)S(1)}, f32[192,1536]{1,0:T(8,128)S(1)}, u32[]{:S(2)}, u32[]{:S(2)}) %collective-permute-start.22) | collective-permute-done | bytes 1179680 | tf_op jit(solution)/shard_map/ppermute | solution.py:614
  285.0 22.2 %collective-permute-done.23 = f32[96,1536]{1,0:T(8,128)S(1)} collective-permute-done((f32[96,1536]{1,0:T(8,128)S(1)}, f32[96,1536]{1,0:T(8,128)S(1)}, u32[]{:S(2)}, u32[]{:S(2)}) %collective-permute-start.23) | collective-permute-done | bytes 589856 | tf_op jit(solution)/shard_map/ppermute | solution.py:614
  309.0 6.9 %collective-permute-done.24 = f32[48,1536]{1,0:T(8,128)S(1)} collective-permute-done((f32[48,1536]{1,0:T(8,128)S(1)}, f32[48,1536]{1,0:T(8,128)S(1)}, u32[]{:S(2)}, u32[]{:S(2)}) %collective-permute-start.24) | collective-permute-done | bytes 294944 | tf_op jit(solution)/shard_map/ppermute | solution.py:614
  315.9 2.5 collective-permute-start.25
  319.3 3.9 %collective-permute-done.25 = f32[48,1536]{1,0:T(8,128)S(1)} collective-permute-done((f32[48,1536]{1,0:T(8,128)S(1)}, f32[48,1536]{1,0:T(8,128)S(1)}, u32[]{:S(2)}, u32[]{:S(2)}) %collective-permute-start.25) | collective-permute-done | bytes 294944 | tf_op jit(solution)/shard_map/ppermute | solution.py:621
  (267 shorter events, 76.3 us)
Async XLA Ops:
  6.6 15.6 %copy-start.33 = (bf16[1536,768]{1,0:T(8,128)(2,1)S(1)}, bf16[1536,768]{1,0:T(8,128)(2,1)}, u32[]{:S(2)}) copy-start(bf16[1536,768]{1,0:T(8,128)(2,1)} %w_down.1) | copy-start | bytes 7077892
  15.0 5.0 %collective-permute-start = (f32[12,8,128]{2,1,0:T(8,128)S(1)}, f32[12,8,128]{2,1,0:T(8,128)S(1)}, u32[]{:S(2)}, u32[]{:S(2)}) collective-permute-start(f32[12,8,128]{2,1,0:T(8,128)S(1)} %get-tuple-element.44), channel_id=1, source_target_pairs={{0,4},{4,0},{8,12},{12,8},{16,20},{20,16},{24,28},{28,24},{1,5},{5... | collective-permute-start | bytes 147464 | tf_op jit(solution)/shard_map/ppermute | solution.py:592
  20.1 8.2 %collective-permute-start.1 = (f32[12,8,128]{2,1,0:T(8,128)S(1)}, f32[12,8,128]{2,1,0:T(8,128)S(1)}, u32[]{:S(2)}, u32[]{:S(2)}) collective-permute-start(f32[12,8,128]{2,1,0:T(8,128)S(1)} %pad_maximum_fusion.8), channel_id=1, source_target_pairs={{0,8},{4,12},{8,0},{12,4},{16,24},{20,28},{24,16},{28,20},{1,9},{5... | collective-permute-start | bytes 147464 | tf_op jit(solution)/shard_map/ppermute | solution.py:592
  28.4 8.3 %collective-permute-start.2 = (f32[12,8,128]{2,1,0:T(8,128)S(1)}, f32[12,8,128]{2,1,0:T(8,128)}, u32[]{:S(2)}, u32[]{:S(2)}) collective-permute-start(f32[12,8,128]{2,1,0:T(8,128)S(1)} %pad_maximum_fusion.9), channel_id=1, source_target_pairs={{0,16},{4,20},{8,24},{12,28},{16,0},{20,4},{24,8},{28,12},{1,17},{... | collective-permute-start | bytes 147464 | tf_op jit(solution)/shard_map/ppermute | solution.py:592
  43.2 20.0 %slice-start.6 = ((s8[4718592]{0:T(1024)(128)(4,1)}), s8[524288]{0:T(1024)(128)(4,1)S(1)}, s32[]{:S(2)}) async-start(s8[4718592]{0:T(1024)(128)(4,1)} %bitcast.36), calls=%async_computation.6 | async-start | bytes 1048576
  63.2 12.9 %copy-start.9 = (bf16[1008,3072]{1,0:T(8,128)(2,1)}, bf16[1008,3072]{1,0:T(8,128)(2,1)S(1)}, u32[]{:S(2)}) copy-start(bf16[1008,3072]{1,0:T(8,128)(2,1)S(1)} %get-tuple-element.49.grad_gu.right) | copy-start | bytes 18579460
  63.3 20.7 %copy-start.59 = (s32[16]{0:T(128)S(1)}, s32[16]{0:T(128)}, u32[]{:S(2)}) copy-start(s32[16]{0:T(128)} %get-tuple-element.79) | copy-start | bytes 196
  63.3 20.7 %copy-start.60 = (s32[16]{0:T(128)S(1)}, s32[16]{0:T(128)}, u32[]{:S(2)}) copy-start(s32[16]{0:T(128)} %get-tuple-element.80) | copy-start | bytes 196
  63.4 23.8 %copy-start.58 = (s32[16]{0:T(128)S(1)}, s32[16]{0:T(128)}, u32[]{:S(2)}) copy-start(s32[16]{0:T(128)} %get-tuple-element.78) | copy-start | bytes 196
  82.5 4.1 %collective-permute-start.3 = (f32[12,8,128]{2,1,0:T(8,128)S(1)}, f32[12,8,128]{2,1,0:T(8,128)S(1)}, u32[]{:S(2)}, u32[]{:S(2)}) collective-permute-start(f32[12,8,128]{2,1,0:T(8,128)S(1)} %get-tuple-element.53), channel_id=1, source_target_pairs={{0,4},{4,0},{8,12},{12,8},{16,20},{20,16},{24,28},{28,24},{1,5},{5... | collective-permute-start | bytes 147464 | tf_op jit(solution)/shard_map/ppermute | solution.py:592
  86.7 4.6 %collective-permute-start.4 = (f32[12,8,128]{2,1,0:T(8,128)S(1)}, f32[12,8,128]{2,1,0:T(8,128)S(1)}, u32[]{:S(2)}, u32[]{:S(2)}) collective-permute-start(f32[12,8,128]{2,1,0:T(8,128)S(1)} %pad_maximum_fusion.10), channel_id=1, source_target_pairs={{0,8},{4,12},{8,0},{12,4},{16,24},{20,28},{24,16},{28,20},{1,9},{5... | collective-permute-start | bytes 147464 | tf_op jit(solution)/shard_map/ppermute | solution.py:592
  91.2 15.2 %slice-start.2 = ((s8[4644864]{0:T(1024)(128)(4,1)}), s8[4194304]{0:T(1024)(128)(4,1)S(1)}, s32[]{:S(2)}) async-start(s8[4644864]{0:T(1024)(128)(4,1)} %bitcast.29), calls=%async_computation.2 | async-start | bytes 8388608
  91.3 15.2 %slice-start.3 = ((s8[4644864]{0:T(1024)(128)(4,1)}), s8[450560]{0:T(1024)(128)(4,1)S(1)}, s32[]{:S(2)}) async-start(s8[4644864]{0:T(1024)(128)(4,1)} %bitcast.29), calls=%async_computation.3 | async-start | bytes 901120
  91.3 15.1 %collective-permute-start.5 = (f32[12,8,128]{2,1,0:T(8,128)S(1)}, f32[12,8,128]{2,1,0:T(8,128)S(1)}, u32[]{:S(2)}, u32[]{:S(2)}) collective-permute-start(f32[12,8,128]{2,1,0:T(8,128)S(1)} %pad_maximum_fusion.11), channel_id=1, source_target_pairs={{0,16},{4,20},{8,24},{12,28},{16,0},{20,4},{24,8},{28,12},{1,17},{... | collective-permute-start | bytes 147464 | tf_op jit(solution)/shard_map/ppermute | solution.py:592
  106.4 83.7 %collective-permute-start.20 = (f32[768,1536]{1,0:T(8,128)}, f32[768,1536]{1,0:T(8,128)}, u32[]{:S(2)}, u32[]{:S(2)}) collective-permute-start(f32[768,1536]{1,0:T(8,128)} %get-tuple-element.66), channel_id=1, source_target_pairs={{0,1},{1,0},{2,3},{3,2},{4,5},{5,4},{6,7},{7,6},{8,9},{9,8},{10,11... | collective-permute-start | bytes 14155784 | tf_op jit(solution)/shard_map/ppermute | solution.py:609
  114.7 31.7 %collective-permute-start.6 = (f32[768,640]{1,0:T(8,128)}, f32[768,640]{1,0:T(8,128)}, u32[]{:S(2)}, u32[]{:S(2)}) collective-permute-start(f32[768,640]{1,0:T(8,128)} %get-tuple-element.60), channel_id=1, source_target_pairs={{0,1},{1,0},{2,3},{3,2},{4,5},{5,4},{6,7},{7,6},{8,9},{9,8},{10,11... | collective-permute-start | bytes 5898248 | tf_op jit(solution)/shard_map/ppermute | solution.py:609
  121.3 59.5 %collective-permute-start.27 = (f32[1536,384]{1,0:T(8,128)}, f32[1536,384]{1,0:T(8,128)}, u32[]{:S(2)}, u32[]{:S(2)}) collective-permute-start(f32[1536,384]{1,0:T(8,128)} %get-tuple-element.68), channel_id=1, source_target_pairs={{0,1},{1,0},{2,3},{3,2},{4,5},{5,4},{6,7},{7,6},{8,9},{9,8},{10,11... | collective-permute-start | bytes 7077896 | tf_op jit(solution)/shard_map/ppermute | solution.py:609
  133.3 51.2 %collective-permute-start.13 = (f32[768,768]{1,0:T(8,128)}, f32[768,768]{1,0:T(8,128)}, u32[]{:S(2)}, u32[]{:S(2)}) collective-permute-start(f32[768,768]{1,0:T(8,128)} %get-tuple-element.64), channel_id=1, source_target_pairs={{0,1},{1,0},{2,3},{3,2},{4,5},{5,4},{6,7},{7,6},{8,9},{9,8},{10,11... | collective-permute-start | bytes 7077896 | tf_op jit(solution)/shard_map/ppermute | solution.py:609
  146.4 24.4 %copy-start.5 = (f32[1008,768]{1,0:T(8,128)S(1)}, f32[1008,768]{1,0:T(8,128)}, u32[]{:S(2)}) copy-start(f32[1008,768]{1,0:T(8,128)} %copy-done.4) | copy-start | bytes 9289732
  150.1 29.1 %collective-permute-start.7 = (f32[384,640]{1,0:T(8,128)}, f32[384,640]{1,0:T(8,128)}, u32[]{:S(2)}, u32[]{:S(2)}) collective-permute-start(f32[384,640]{1,0:T(8,128)} %get-tuple-element.96), channel_id=1, source_target_pairs={{0,4},{1,3},{2,6},{3,1},{4,0},{5,7},{6,2},{7,5},{8,12},{9,11},{10,... | collective-permute-start | bytes 2949128 | tf_op jit(solution)/shard_map/ppermute | solution.py:614
  151.7 1.2 collective-permute-start.34
  152.9 4.0 %collective-permute-start.35 = (f32[27,128]{1,0:T(8,128)S(1)}, f32[27,128]{1,0:T(8,128)S(1)}, u32[]{:S(2)}, u32[]{:S(2)}) collective-permute-start(f32[27,128]{1,0:T(8,128)S(1)} %fusion.16), channel_id=1, source_target_pairs={{0,2},{1,3},{2,0},{3,1},{4,6},{5,7},{6,4},{7,5},{8,10},{9,11},{10,... | collective-permute-start | bytes 41480 | tf_op jit(solution)/shard_map/ppermute | solution.py:751
  156.9 7.7 %collective-permute-start.36 = (f32[27,128]{1,0:T(8,128)S(1)}, f32[27,128]{1,0:T(8,128)S(1)}, u32[]{:S(2)}, u32[]{:S(2)}) collective-permute-start(f32[27,128]{1,0:T(8,128)S(1)} %fusion.17), channel_id=1, source_target_pairs={{0,4},{4,0},{8,12},{12,8},{16,20},{20,16},{24,28},{28,24},{1,5},{5... | collective-permute-start | bytes 41480 | tf_op jit(solution)/shard_map/ppermute | solution.py:751
  164.6 3.7 %collective-permute-start.37 = (f32[27,128]{1,0:T(8,128)S(1)}, f32[27,128]{1,0:T(8,128)S(1)}, u32[]{:S(2)}, u32[]{:S(2)}) collective-permute-start(f32[27,128]{1,0:T(8,128)S(1)} %add.321), channel_id=1, source_target_pairs={{0,8},{4,12},{8,0},{12,4},{16,24},{20,28},{24,16},{28,20},{1,9},{5... | collective-permute-start | bytes 41480 | tf_op jit(solution)/shard_map/ppermute | solution.py:751
  168.4 10.2 %collective-permute-start.38 = (f32[27,128]{1,0:T(8,128)S(1)}, f32[27,128]{1,0:T(8,128)S(1)}, u32[]{:S(2)}, u32[]{:S(2)}) collective-permute-start(f32[27,128]{1,0:T(8,128)S(1)} %add.322), channel_id=1, source_target_pairs={{0,16},{4,20},{8,24},{12,28},{16,0},{20,4},{24,8},{28,12},{1,17},{... | collective-permute-start | bytes 41480 | tf_op jit(solution)/shard_map/ppermute | solution.py:751
  180.6 8.9 %collective-permute-start.8 = (f32[192,640]{1,0:T(8,128)S(1)}, f32[192,640]{1,0:T(8,128)S(1)}, u32[]{:S(2)}, u32[]{:S(2)}) collective-permute-start(f32[192,640]{1,0:T(8,128)S(1)} %get-tuple-element.104), channel_id=1, source_target_pairs={{0,8},{1,5},{2,10},{3,7},{4,12},{5,1},{6,14},{7,3},{8,0},{9,13},{1... | collective-permute-start | bytes 1474568 | tf_op jit(solution)/shard_map/ppermute | solution.py:614
  182.9 19.0 %collective-permute-start.28 = (f32[768,384]{1,0:T(8,128)S(1)}, f32[768,384]{1,0:T(8,128)S(1)}, u32[]{:S(2)}, u32[]{:S(2)}) collective-permute-start(f32[768,384]{1,0:T(8,128)S(1)} %get-tuple-element.90), channel_id=1, source_target_pairs={{0,4},{1,3},{2,6},{3,1},{4,0},{5,7},{6,2},{7,5},{8,12},{9,11},{10,... | collective-permute-start | bytes 3538952 | tf_op jit(solution)/shard_map/ppermute | solution.py:614
  186.6 36.8 %collective-permute-start.14 = (f32[384,768]{1,0:T(8,128)S(1)}, f32[384,768]{1,0:T(8,128)S(1)}, u32[]{:S(2)}, u32[]{:S(2)}) collective-permute-start(f32[384,768]{1,0:T(8,128)S(1)} %get-tuple-element.94), channel_id=1, source_target_pairs={{0,4},{1,3},{2,6},{3,1},{4,0},{5,7},{6,2},{7,5},{8,12},{9,11},{10,... | collective-permute-start | bytes 3538952 | tf_op jit(solution)/shard_map/ppermute | solution.py:614
  189.6 9.4 %collective-permute-start.9 = (f32[96,640]{1,0:T(8,128)S(1)}, f32[96,640]{1,0:T(8,128)S(1)}, u32[]{:S(2)}, u32[]{:S(2)}) collective-permute-start(f32[96,640]{1,0:T(8,128)S(1)} %get-tuple-element.112), channel_id=1, source_target_pairs={{0,16},{1,9},{2,18},{3,11},{4,20},{5,13},{6,22},{7,15},{8,24},{9,1... | collective-permute-start | bytes 737288 | tf_op jit(solution)/shard_map/ppermute | solution.py:614
  193.5 64.3 %collective-permute-start.21 = (f32[384,1536]{1,0:T(8,128)S(1)}, f32[384,1536]{1,0:T(8,128)S(1)}, u32[]{:S(2)}, u32[]{:S(2)}) collective-permute-start(f32[384,1536]{1,0:T(8,128)S(1)} %get-tuple-element.88), channel_id=1, source_target_pairs={{0,4},{1,3},{2,6},{3,1},{4,0},{5,7},{6,2},{7,5},{8,12},{9,11},{10,... | collective-permute-start | bytes 7077896 | tf_op jit(solution)/shard_map/ppermute | solution.py:614
  199.0 6.3 %collective-permute-start.10 = (f32[48,640]{1,0:T(8,128)S(1)}, f32[48,640]{1,0:T(8,128)S(1)}, u32[]{:S(2)}, u32[]{:S(2)}) collective-permute-start(f32[48,640]{1,0:T(8,128)S(1)} %slice_add_fusion.30), channel_id=1, source_target_pairs={{0,2},{1,17},{2,0},{3,19},{4,6},{5,21},{6,4},{7,23},{8,10},{9,25},... | collective-permute-start | bytes 368648 | tf_op jit(solution)/shard_map/ppermute | solution.py:614
  202.0 40.2 %collective-permute-start.29 = (f32[384,384]{1,0:T(8,128)S(1)}, f32[384,384]{1,0:T(8,128)S(1)}, u32[]{:S(2)}, u32[]{:S(2)}) collective-permute-start(f32[384,384]{1,0:T(8,128)S(1)} %get-tuple-element.98), channel_id=1, source_target_pairs={{0,8},{1,5},{2,10},{3,7},{4,12},{5,1},{6,14},{7,3},{8,0},{9,13},{1... | collective-permute-start | bytes 1769480 | tf_op jit(solution)/shard_map/ppermute | solution.py:614
  205.4 18.5 %collective-permute-start.11 = (f32[48,640]{1,0:T(8,128)S(1)}, f32[48,640]{1,0:T(8,128)S(1)}, u32[]{:S(2)}, u32[]{:S(2)}) collective-permute-start(f32[48,640]{1,0:T(8,128)S(1)} %fusion.5), channel_id=1, source_target_pairs={{0,2},{1,3},{2,0},{3,1},{4,6},{5,7},{6,4},{7,5},{8,10},{9,11},{10,... | collective-permute-start | bytes 368648 | tf_op jit(solution)/shard_map/ppermute | solution.py:621
  223.5 19.2 %collective-permute-start.15 = (f32[192,768]{1,0:T(8,128)S(1)}, f32[192,768]{1,0:T(8,128)S(1)}, u32[]{:S(2)}, u32[]{:S(2)}) collective-permute-start(f32[192,768]{1,0:T(8,128)S(1)} %get-tuple-element.102), channel_id=1, source_target_pairs={{0,8},{1,5},{2,10},{3,7},{4,12},{5,1},{6,14},{7,3},{8,0},{9,13},{1... | collective-permute-start | bytes 1769480 | tf_op jit(solution)/shard_map/ppermute | solution.py:614
  223.9 21.4 %collective-permute-start.12 = (f32[96,640]{1,0:T(8,128)S(1)}, f32[96,640]{1,0:T(8,128)S(1)}, u32[]{:S(2)}, u32[]{:S(2)}) collective-permute-start(f32[96,640]{1,0:T(8,128)S(1)} %pad_maximum_fusion.7), channel_id=1, source_target_pairs={{0,1},{1,0},{2,3},{3,2},{4,5},{5,4},{6,7},{7,6},{8,9},{9,8},{10,11... | collective-permute-start | bytes 737288 | tf_op jit(solution)/shard_map/ppermute | solution.py:621
  242.2 16.3 %collective-permute-start.30 = (f32[192,384]{1,0:T(8,128)S(1)}, f32[192,384]{1,0:T(8,128)S(1)}, u32[]{:S(2)}, u32[]{:S(2)}) collective-permute-start(f32[192,384]{1,0:T(8,128)S(1)} %get-tuple-element.106), channel_id=1, source_target_pairs={{0,16},{1,9},{2,18},{3,11},{4,20},{5,13},{6,22},{7,15},{8,24},{9,1... | collective-permute-start | bytes 884744 | tf_op jit(solution)/shard_map/ppermute | solution.py:614
  242.8 22.8 %collective-permute-start.16 = (f32[96,768]{1,0:T(8,128)S(1)}, f32[96,768]{1,0:T(8,128)S(1)}, u32[]{:S(2)}, u32[]{:S(2)}) collective-permute-start(f32[96,768]{1,0:T(8,128)S(1)} %get-tuple-element.110), channel_id=1, source_target_pairs={{0,16},{1,9},{2,18},{3,11},{4,20},{5,13},{6,22},{7,15},{8,24},{9,1... | collective-permute-start | bytes 884744 | tf_op jit(solution)/shard_map/ppermute | solution.py:614
  258.2 26.4 %collective-permute-start.22 = (f32[192,1536]{1,0:T(8,128)S(1)}, f32[192,1536]{1,0:T(8,128)S(1)}, u32[]{:S(2)}, u32[]{:S(2)}) collective-permute-start(f32[192,1536]{1,0:T(8,128)S(1)} %get-tuple-element.92), channel_id=1, source_target_pairs={{0,8},{1,5},{2,10},{3,7},{4,12},{5,1},{6,14},{7,3},{8,0},{9,13},{1... | collective-permute-start | bytes 3538952 | tf_op jit(solution)/shard_map/ppermute | solution.py:614
  258.6 8.7 %collective-permute-start.31 = (f32[96,384]{1,0:T(8,128)S(1)}, f32[96,384]{1,0:T(8,128)S(1)}, u32[]{:S(2)}, u32[]{:S(2)}) collective-permute-start(f32[96,384]{1,0:T(8,128)S(1)} %slice_add_fusion.26), channel_id=1, source_target_pairs={{0,2},{1,17},{2,0},{3,19},{4,6},{5,21},{6,4},{7,23},{8,10},{9,25},... | collective-permute-start | bytes 442376 | tf_op jit(solution)/shard_map/ppermute | solution.py:614
  265.7 5.9 %collective-permute-start.17 = (f32[48,768]{1,0:T(8,128)S(1)}, f32[48,768]{1,0:T(8,128)S(1)}, u32[]{:S(2)}, u32[]{:S(2)}) collective-permute-start(f32[48,768]{1,0:T(8,128)S(1)} %slice_add_fusion.28), channel_id=1, source_target_pairs={{0,2},{1,17},{2,0},{3,19},{4,6},{5,21},{6,4},{7,23},{8,10},{9,25},... | collective-permute-start | bytes 442376 | tf_op jit(solution)/shard_map/ppermute | solution.py:614
  267.3 17.7 %collective-permute-start.32 = (f32[96,384]{1,0:T(8,128)S(1)}, f32[96,384]{1,0:T(8,128)S(1)}, u32[]{:S(2)}, u32[]{:S(2)}) collective-permute-start(f32[96,384]{1,0:T(8,128)S(1)} %fusion.3), channel_id=1, source_target_pairs={{0,2},{1,3},{2,0},{3,1},{4,6},{5,7},{6,4},{7,5},{8,10},{9,11},{10,... | collective-permute-start | bytes 442376 | tf_op jit(solution)/shard_map/ppermute | solution.py:621
  271.6 13.2 %collective-permute-start.18 = (f32[48,768]{1,0:T(8,128)S(1)}, f32[48,768]{1,0:T(8,128)S(1)}, u32[]{:S(2)}, u32[]{:S(2)}) collective-permute-start(f32[48,768]{1,0:T(8,128)S(1)} %fusion.4), channel_id=1, source_target_pairs={{0,2},{1,3},{2,0},{3,1},{4,6},{5,7},{6,4},{7,5},{8,10},{9,11},{10,... | collective-permute-start | bytes 442376 | tf_op jit(solution)/shard_map/ppermute | solution.py:621
  284.7 22.5 %collective-permute-start.23 = (f32[96,1536]{1,0:T(8,128)S(1)}, f32[96,1536]{1,0:T(8,128)S(1)}, u32[]{:S(2)}, u32[]{:S(2)}) collective-permute-start(f32[96,1536]{1,0:T(8,128)S(1)} %get-tuple-element.100), channel_id=1, source_target_pairs={{0,16},{1,9},{2,18},{3,11},{4,20},{5,13},{6,22},{7,15},{8,24},{9,1... | collective-permute-start | bytes 1769480 | tf_op jit(solution)/shard_map/ppermute | solution.py:614
  284.9 24.0 %collective-permute-start.19 = (f32[96,768]{1,0:T(8,128)S(1)}, f32[96,768]{1,0:T(8,128)S(1)}, u32[]{:S(2)}, u32[]{:S(2)}) collective-permute-start(f32[96,768]{1,0:T(8,128)S(1)} %pad_maximum_fusion.4), channel_id=1, source_target_pairs={{0,1},{1,0},{2,3},{3,2},{4,5},{5,4},{6,7},{7,6},{8,9},{9,8},{10,11... | collective-permute-start | bytes 884744 | tf_op jit(solution)/shard_map/ppermute | solution.py:621
  307.2 8.6 %collective-permute-start.24 = (f32[48,1536]{1,0:T(8,128)S(1)}, f32[48,1536]{1,0:T(8,128)S(1)}, u32[]{:S(2)}, u32[]{:S(2)}) collective-permute-start(f32[48,1536]{1,0:T(8,128)S(1)} %slice_add_fusion.20), channel_id=1, source_target_pairs={{0,2},{1,17},{2,0},{3,19},{4,6},{5,21},{6,4},{7,23},{8,10},{9,25},... | collective-permute-start | bytes 884744 | tf_op jit(solution)/shard_map/ppermute | solution.py:614
  308.8 14.5 %collective-permute-start.33 = (f32[192,384]{1,0:T(8,128)S(1)}, f32[192,384]{1,0:T(8,128)S(1)}, u32[]{:S(2)}, u32[]{:S(2)}) collective-permute-start(f32[192,384]{1,0:T(8,128)S(1)} %pad_maximum_fusion.6), channel_id=1, source_target_pairs={{0,1},{1,0},{2,3},{3,2},{4,5},{5,4},{6,7},{7,6},{8,9},{9,8},{10,11... | collective-permute-start | bytes 884744 | tf_op jit(solution)/shard_map/ppermute | solution.py:621
  315.9 7.2 %collective-permute-start.25 = (f32[48,1536]{1,0:T(8,128)S(1)}, f32[48,1536]{1,0:T(8,128)S(1)}, u32[]{:S(2)}, u32[]{:S(2)}) collective-permute-start(f32[48,1536]{1,0:T(8,128)S(1)} %fusion), channel_id=1, source_target_pairs={{0,2},{1,3},{2,0},{3,1},{4,6},{5,7},{6,4},{7,5},{8,10},{9,11},{10,... | collective-permute-start | bytes 884744 | tf_op jit(solution)/shard_map/ppermute | solution.py:621
  323.3 2.1 collective-permute-start.26
  (62 other events, 288.3 us)

commit v2 on v0

v2 whole, which is shorter than its diff:
```python
import functools
import types

import jax
import jax.numpy as jnp
import numpy as np
from jax import lax
from jax.experimental import pallas as pl
from jax.experimental.pallas import tpu as pltpu
from jax.sharding import PartitionSpec as P

epsilon = 1e-06
LANES = 128
SUB = 8
F32 = jnp.float32
BF16 = jnp.bfloat16
MIB = 2**20


class Names:
    def __getattr__(self, name):
        return name


N = Names()
SCALE = 0.2
FOLD = 0.3
HOPS = (2, 1, 0)
ORDERS = {N.wide: (N.yzxw, N.xwyz), N.down: (N.yxwz, N.xyzw), N.scan: (N.yxzw, N.zxyw)}
ROUNDS = N.wpsposwpswpssp
DEPS = {N.s0: "p0 w2", N.p1: N.s0, "o": N.p1, N.s1: "o", N.w3: N.s1, N.p2: N.s1, N.p3: N.s2, N.w4: N.s2, N.s3: N.w4, N.p4: N.s4}
PIECES = 2
TIME = {
    N.project: 8.0, N.gate: 1.8, N.hidden_back: 1.9, N.mix: 5.9, N.ffn: 7.3, N.grad_gu: 3.2, N.grad_down: 3.6, N.ffn_back: 6.5,
    N.mix_back: 7.0, N.grad_out: 1.6, N.grad_gate: 1.6, N.scan_back: 4.0, N.input_back: 5.6, N.grad_scan: 2.4, N.output: 7.0,
}


def sigmoid(values):
    return 0.5 * jnp.tanh(0.5 * values) + 0.5


def forget_gate(forget, lower):
    decay = jnp.exp(jnp.minimum(-forget, 80.0))
    total = 1.0 + decay
    guess = pl.reciprocal(total, approx=True)
    open_part = guess * (2.0 - total * guess)
    shut_part = decay * open_part
    intake = (1.0 - lower) * shut_part
    return open_part, shut_part, intake, 1.0 - intake


def dot(left, right, left_dim, right_dim):
    return lax.dot_general(
        left, right, (((left_dim,), (right_dim,)), ((), ())), preferred_element_type=F32
    )


def row_block(rows, most):
    best = 16
    for size in range(16, most + 1, 16):
        if rows % size == 0:
            best = size
    return best


def rows_at(step, size):
    return pl.ds(pl.multiple_of(step * size, 16), size)


def tile_of(ref, tile):
    return ref[:, tile * LANES : (tile + 1) * LANES]


def fold_rows(values):
    rows, lanes = values.shape
    return jnp.sum(values.reshape(rows // SUB, SUB, lanes), axis=0)


def loop(count, body):
    lax.fori_loop(0, count, lambda step, _: (body(step), 0)[1], 0)


def project_kernel(shape, r):
    seqs, positions, chans = shape
    tiles = chans // LANES
    steps = positions // SUB
    rows = seqs * positions
    size = row_block(rows, 336)
    width = r.tok.shape[1]
    r.vec[...] = jnp.zeros(r.vec.shape, F32)
    for name in (N.raw_in, N.raw_lower, N.raw_fbias, N.raw_phase, N.raw_out, N.raw_ffn):
        r.wait(name)
    for row, name in enumerate((N.raw_in, N.raw_out, N.raw_ffn)):
        r.vec[row : row + 1, :] = getattr(r, name)[...].reshape(1, width)
    phase = r.raw_phase[...].reshape(1, chans)
    r.vec[3:4, :chans] = r.raw_lower[...].reshape(1, chans)
    r.vec[3:4, chans:] = r.raw_fbias[...].reshape(1, chans)
    r.vec[4:5, :chans] = jnp.cos(phase)
    r.vec[4:5, chans:] = jnp.sin(phase)
    r.vec[5:6, :chans] = jnp.cos(phase * steps)
    r.vec[5:6, chans:] = jnp.sin(phase * steps)
    r.vec[6:7, :chans] = jnp.cos(phase * positions)
    r.vec[6:7, chans:] = jnp.sin(phase * positions)
    gain = r.vec[0:1, :]
    fbias = r.vec[3:4, chans:]
    r.wait(N.tok)

    def norm(step):
        at = rows_at(step, size)
        inputs = r.tok[at, :].astype(F32)
        scale = lax.rsqrt(jnp.mean(inputs * inputs, axis=-1, keepdims=True) + epsilon)
        r.low[at, :] = (inputs * scale * gain).astype(BF16)

    loop(rows // size, norm)
    r.wait(N.wmix)
    r.start_late()

    def project(step):
        at = rows_at(step, size)
        for part in range(3):
            made = dot(r.low[at, :], r.wmix[:, part * chans : (part + 1) * chans], 1, 0)
            if part == 2:
                made = made + fbias
            for tile in range(tiles):
                r.pre[part * tiles + tile, at, :] = made[:, tile * LANES : (tile + 1) * LANES]

    loop(rows // size, project)

    def scan(seq):
        for tile in range(tiles):
            lanes = slice(tile * LANES, (tile + 1) * LANES)
            low_bound, cos_t, sin_t = r.vec[3:4, lanes], r.vec[4:5, lanes], sine_of(r, lanes)
            product = jnp.ones((SUB, LANES), F32)
            state_r = jnp.zeros((SUB, LANES), F32)
            state_i = jnp.zeros((SUB, LANES), F32)
            for step in range(steps):
                at = pl.ds(seq * positions + step, SUB, stride=steps)
                in_r, in_i = r.pre[tile, at, :], r.pre[tiles + tile, at, :]
                _, _, intake, retain = forget_gate(r.pre[2 * tiles + tile, at, :], low_bound)
                mul_r, mul_i = retain * cos_t, retain * sin_t
                add_r, add_i = intake * (in_r * sigmoid(in_r)), intake * (in_i * sigmoid(in_i))
                state_r, state_i = (
                    mul_r * state_r - mul_i * state_i + add_r,
                    mul_r * state_i + mul_i * state_r + add_i,
                )
                product = product * retain
                r.steps[tile, at, :] = retain
                r.steps[tiles + tile, at, :] = add_r
                r.steps[2 * tiles + tile, at, :] = add_i
            at = pl.ds(pl.multiple_of(seq * SUB, SUB), SUB)
            r.chunks[tile, at, :] = product
            r.chunks[tiles + tile, at, :] = state_r
            r.chunks[2 * tiles + tile, at, :] = state_i

    r.chunks[...] = jnp.zeros(r.chunks.shape, F32)
    loop(seqs, scan)
    joined(r, tiles, r.chunks, tiles, r.ends, False)


def sine_of(r, lanes):
    chans = r.vec.shape[1] // 2
    return r.vec[4:5, chans + lanes.start : chans + lanes.stop]


def chunk_step(r, tiles, tile, at, added, base, now_r, now_i, backward):
    lanes = slice(tile * LANES, (tile + 1) * LANES)
    chans = r.vec.shape[1] // 2
    product = r.chunks[tile, at, :]
    new_r = product * r.vec[5:6, lanes]
    new_i = product * r.vec[5:6, chans + lanes.start : chans + lanes.stop]
    if backward:
        new_i = -new_i
    return (
        new_r,
        new_i,
        new_r * now_r - new_i * now_i + added[base + tile, at, :],
        new_r * now_i + new_i * now_r + added[base + tiles + tile, at, :],
    )


def joined(r, tiles, added, base, ends, backward):
    pad = ends.shape[1]
    for tile in range(tiles):
        mul_r, mul_i = jnp.ones((pad, LANES), F32), jnp.zeros((pad, LANES), F32)
        add_r, add_i = jnp.zeros((pad, LANES), F32), jnp.zeros((pad, LANES), F32)
        for chunk in reversed(range(SUB)) if backward else range(SUB):
            at = pl.ds(chunk, pad, stride=SUB)
            new_r, new_i, add_r, add_i = chunk_step(r, tiles, tile, at, added, base, add_r, add_i, backward)
            mul_r, mul_i = mul_r * new_r - mul_i * new_i, mul_r * new_i + mul_i * new_r
        ends[tile] = mul_r
        ends[tiles + tile] = mul_i
        ends[2 * tiles + tile] = add_r
        ends[3 * tiles + tile] = add_i


def entered(r, tiles, added, base, start, entries, backward):
    pad = start.shape[1]
    for tile in range(tiles):
        now_r, now_i = start[tile], start[tiles + tile]
        for chunk in reversed(range(SUB)) if backward else range(SUB):
            at = pl.ds(chunk, pad, stride=SUB)
            entries[tile, at, :] = now_r
            entries[tiles + tile, at, :] = now_i
            _, _, now_r, now_i = chunk_step(r, tiles, tile, at, added, base, now_r, now_i, backward)


def carry_kernel(bit, first, last, backward, r):
    tiles = r.total.shape[0] // 4
    later = (lax.axis_index(N.seq) & bit) != 0
    if backward:
        later = jnp.logical_not(later)
    for tile in range(tiles):
        parts = [part * tiles + tile for part in range(4)]
        mine = tuple(r.total[part] for part in parts)
        got = tuple(r.got[part] for part in parts)
        one, zero = jnp.ones(mine[0].shape, F32), jnp.zeros(mine[0].shape, F32)
        before = (one, zero, zero, zero) if first else tuple(r.before[part] for part in parts)
        longer = combine(got, before)
        before = [jnp.where(later, new, old) for new, old in zip(longer, before)]
        if last:
            r.start[tile] = before[2]
            r.start[tiles + tile] = before[3]
        else:
            ahead = [jnp.where(later, b, a) for a, b in zip(mine, got)]
            behind = [jnp.where(later, a, b) for a, b in zip(mine, got)]
            for part, new, total in zip(parts, before, combine(ahead, behind)):
                r.before_next[part] = new
                r.total_next[part] = total


def gate_kernel(chans, r):
    tiles, rows, _ = r.gate.shape
    size = row_block(rows, 336)

    def step_of(step):
        at = rows_at(step, size)
        made = dot(r.low[at, :], r.wmix[:, 3 * chans :], 1, 0)
        for tile in range(tiles):
            r.gate[tile, at, :] = made[:, tile * LANES : (tile + 1) * LANES]

    loop(rows // size, step_of)


def hidden_back_kernel(first, name, r):
    made = getattr(r, name)
    rows, units = made.shape
    size = row_block(rows, 336)

    def step_of(step):
        at = rows_at(step, size)
        for part in range(units // 256):
            cols = slice(part * 256, (part + 1) * 256)
            weight = r.wdown[first + part * 256 : first + (part + 1) * 256, :]
            made[at, cols] = dot(r.cot[at, :], weight, 1, 1).astype(BF16)

    loop(rows // size, step_of)


def mix_kernel(shape, r):
    seqs, positions, chans = shape
    tiles = chans // LANES
    steps = positions // SUB
    rows = seqs * positions
    width = 2 * chans
    size = row_block(rows, 144)
    entered(r, tiles, r.chunks, tiles, r.start, r.entries, False)

    def scan(seq):
        for tile in range(tiles):
            lanes = slice(tile * LANES, (tile + 1) * LANES)
            cos_t, sin_t = r.vec[4:5, lanes], sine_of(r, lanes)
            at = pl.ds(pl.multiple_of(seq * SUB, SUB), SUB)
            state_r, state_i = r.entries[tile, at, :], r.entries[tiles + tile, at, :]
            for step in range(steps):
                at = pl.ds(seq * positions + step, SUB, stride=steps)
                retain = r.steps[tile, at, :]
                add_r, add_i = r.steps[tiles + tile, at, :], r.steps[2 * tiles + tile, at, :]
                mul_r, mul_i = retain * cos_t, retain * sin_t
                state_r, state_i = (
                    mul_r * state_r - mul_i * state_i + add_r,
                    mul_r * state_i + mul_i * state_r + add_i,
                )
                r.states[tile, at, :] = state_r
                r.states[tiles + tile, at, :] = state_i

    loop(seqs, scan)

    def mix(step):
        at = rows_at(step, size)
        squares = jnp.zeros((size, LANES), F32)
        for tile in range(2 * tiles):
            part = r.states[tile, at, :]
            squares = squares + part * part
        scale = lax.rsqrt(jnp.sum(squares, axis=-1, keepdims=True) / width + epsilon)
        for tile in range(2 * tiles):
            lanes = slice(tile * LANES, (tile + 1) * LANES)
            gated = r.gate[tile, at, :]
            part = r.states[tile, at, :] * scale * r.vec[1:2, lanes] * (gated * sigmoid(gated))
            r.mixed[at, lanes] = part.astype(BF16)
        total = r.tok[at, :].astype(F32) + dot(r.mixed[at, :], r.wout[...], 1, 0)
        r.after[at, :] = total
        scale = lax.rsqrt(jnp.mean(total * total, axis=-1, keepdims=True) + epsilon)
        r.ffn_low[at, :] = (total * scale * r.vec[2:3, :]).astype(BF16)

    loop(rows // size, mix)


def ffn_kernel(r):
    rows, units = r.hidden.shape
    for name in (N.after, N.mixed, N.low, N.pre, N.states, N.gate):
        r.save(getattr(r, name), getattr(r, name + N._out))
    size = row_block(rows, 336)
    wide = 256

    def step_of(step):
        at = rows_at(step, size)
        block = r.ffn_low[at, :]
        for part in range(units // wide):
            cols = slice(part * wide, (part + 1) * wide)
            later = slice(units + part * wide, units + (part + 1) * wide)
            gate = dot(block, r.wgu[:, cols], 1, 0)
            up = dot(block, r.wgu[:, later], 1, 0)
            side, at_side = (r.back0, part) if 2 * part * wide < units else (r.back1, part - units // wide // 2)
            back = side[at, at_side * wide : (at_side + 1) * wide].astype(F32)
            sigma = sigmoid(gate)
            act = gate * sigma
            r.hidden[at, cols] = (act * up).astype(BF16)
            r.grad_gu[at, cols] = (back * up * (sigma + act * (1.0 - sigma))).astype(BF16)
            r.grad_gu[at, later] = (back * act).astype(BF16)

    loop(rows // size, step_of)


def block_slots(plan):
    if not plan.in_place:
        return list(range(plan.made)), list(range(plan.made))
    seq, batch = lax.axis_index(N.seq), lax.axis_index(N.batch)
    odd = (batch & 1) == 1
    rest = plan.rest

    def place(order, seq_bits, batch_bits):
        total = 0
        for index, (axis, bit) in enumerate(order):
            value = seq_bits if axis == N.seq else batch_bits
            total = total + (((value & bit) // bit) << (len(order) - 1 - index))
        return total

    mine = [place(order, seq, batch) for order in plan.orders]
    keep, send = [], []
    for block in range(plan.blocks):
        fixed = [place(order, block // rest, (block % rest) * 2) for order in plan.orders]
        first, second = fixed[0] ^ mine[0], fixed[1] ^ mine[1]
        keep.append(jnp.where(odd, second, first))
        send.append(jnp.where(odd, first, second))
    return keep, send


def store_blocks(ref, slots, size, cols, values, base=0):
    for block, slot in enumerate(slots):
        at = base + slot * size if isinstance(slot, int) else pl.multiple_of(base + slot * size, SUB)
        ref[pl.ds(at, size), cols] = values[block * size : (block + 1) * size, :]


def grad_narrow_kernel(plan, left, right, keep, send, r):
    left, right, keep, send = (getattr(r, name) for name in (left, right, keep, send))
    mine = lax.axis_index(N.batch) & 1
    kept, sent = block_slots(plan)
    half = right.shape[1] // 2
    r.turned[:, :half] = right[:, pl.ds(pl.multiple_of(mine * half, LANES), half)]
    r.turned[:, half:] = right[:, pl.ds(pl.multiple_of((1 - mine) * half, LANES), half)]
    size = left.shape[1] // plan.made
    tall = min(left.shape[1], 384)
    cols = slice(0, half)
    count = tall // size
    for part in range(left.shape[1] // tall):
        made = dot(left[:, part * tall : (part + 1) * tall], r.turned[...], 0, 0)
        there = slice(part * count, (part + 1) * count)
        store_blocks(keep, kept[there], size, cols, made[:, :half])
        store_blocks(send, sent[there], size, cols, made[:, half:])


def grad_wide_kernel(plan, left, right, made_name, sending, wide, r):
    left, right, out = getattr(r, left), getattr(r, right), getattr(r, made_name)
    mine = lax.axis_index(N.batch) & 1
    owner = 1 - mine if sending else mine
    slots = block_slots(plan)[1 if sending else 0]
    half = right.shape[1] // 2
    size = left.shape[1] // plan.made

    def step_of(part):
        cols = pl.ds(pl.multiple_of(part * wide, LANES), wide)
        source = pl.ds(pl.multiple_of(owner * half + part * wide, LANES), wide)
        store_blocks(out, slots, size, cols, dot(left[...], right[:, source], 0, 0))

    loop(half // wide, step_of)


def fold_kernel(names, head, r):
    keep, got = getattr(r, names[0]), r.got
    send_next, keep_next = getattr(r, names[1]), getattr(r, names[2])
    half = (keep.shape[0] - head) // 2
    send_next[head:, :] = keep[head + half :, :] + got[head + half :, :]
    keep_next[head:, :] = keep[head : head + half, :] + got[head : head + half, :]
    if head:
        both = keep[:head, :] + got[:head, :]
        send_next[:head, :] = both
        keep_next[:head, :] = both


def fold_first_kernel(parts, head, pieces, names, r):
    send_next, keep_next = getattr(r, names[0]), getattr(r, names[1])
    start = 0
    for part in parts:
        keep = getattr(r, N.keep_ + part)
        rows = keep.shape[0] - head
        half = rows // 2
        cols = slice(start, start + keep.shape[1])
        start = cols.stop
        count = max(pieces, 2)
        size = rows // count
        for piece in range(count):
            at = piece * size
            if pieces == 1:
                got = getattr(r, "got_%s0" % part)[head + at : head + at + size, :]
            else:
                first = head if piece == 0 else 0
                got = getattr(r, "got_%s%d" % (part, piece))[first : first + size, :]
            value = keep[head + at : head + at + size, :] + got
            if at < half:
                keep_next[head + at : head + at + size, cols] = value
            else:
                send_next[head + at - half : head + at - half + size, cols] = value
        if head:
            both = keep[:head, :] + getattr(r, "got_%s0" % part)[:head, :]
            send_next[:head, cols] = both
            keep_next[:head, cols] = both


def sum_kernel(name, r):
    r.total[...] = getattr(r, name)[...] + r.got[...]


def fold_pair_kernel(slots, r):
    per, wide = r.keep_down.shape[0] // slots, r.keep_down.shape[1]
    rows = r.keep_third.shape[0] // slots
    for slot in range(slots):
        out = r.later_pair if 2 * slot < slots else r.send_pair
        to = slot % (slots // 2) * per
        at = slice(slot * per, (slot + 1) * per)
        out[to : to + per, :wide] = r.keep_down[at, :] + r.got_down[at, :]
        at = slice(slot * rows, (slot + 1) * rows)
        value = r.keep_third[at, :] + r.got_third[at, :]
        out[to : to + rows, wide:] = value[:, :wide]
        out[to + rows : to + per, wide:] = value[:, wide:]


def pack_kernel(r):
    rows, wide = r.packed.shape[0], r.keep_pair.shape[1] // 2
    total = r.keep_pair[...] + r.got[...]
    r.packed[:, :wide] = total[:rows, wide:]
    r.packed[:, wide : 2 * wide] = total[rows:, wide:]
    r.packed[:, 2 * wide : 3 * wide] = total[:rows, :wide]
    r.packed[:, 3 * wide :] = total[rows:, :wide]


def stack_kernel(axis, bit, r):
    upper = (lax.axis_index(axis) & bit) != 0
    start = 0
    for mine, got in ((r.first, r.first_got), (r.second, r.second_got)):
        rows, wide = mine.shape
        cols = slice(start, start + wide)
        start = cols.stop
        r.both[:rows, cols] = jnp.where(upper, got[...], mine[...])
        r.both[rows:, cols] = jnp.where(upper, mine[...], got[...])


def stack_head_kernel(axis, bit, head, r):
    upper = (lax.axis_index(axis) & bit) != 0
    rows = r.mine.shape[0]
    r.both[:head, :] = r.mine[:head, :]
    r.both[head:rows, :] = jnp.where(upper, r.got[head:, :], r.mine[head:, :])
    r.both[rows:, :] = jnp.where(upper, r.mine[head:, :], r.got[head:, :])


def unpack_kernel(parts, r):
    upper = (lax.axis_index(N.batch) & 1) != 0
    units, width = r.grad_down.shape[0], r.grad_down.shape[1]
    half = width // 2
    rows = r.mine.shape[0]
    wide = r.grad_wide.shape[1] // 2
    size = rows // parts

    def sides(at, cols):
        mine, got = r.mine[at, cols], r.got[at, cols]
        return jnp.where(upper, got, mine), jnp.where(upper, mine, got)

    every = slice(0, rows)
    r.grad_wide[:, :wide], r.grad_wide[:, wide:] = sides(every, slice(0, wide))
    r.grad_out[:, :half], r.grad_out[:, half:] = sides(every, slice(wide, wide + half))
    r.gate_part[:, :half], r.gate_part[:, half:] = sides(every, slice(wide + half, wide + 2 * half))
    base = wide + 2 * half
    per = units // rows
    for part in range(parts):
        for piece in range(per):
            at = slice(part * size, (part + 1) * size)
            to = slice((part * per + piece) * size, (part * per + piece + 1) * size)
            first, second = sides(at, slice(base + piece * half, base + (piece + 1) * half))
            r.grad_down[to, :half] = first
            r.grad_down[to, half:] = second


def finish_kernel(r):
    upper = (lax.axis_index(N.batch) & 1) != 0
    wide = r.mine.shape[1]
    first = jnp.where(upper, r.got[SUB:, :], r.mine[SUB:, :])
    second = jnp.where(upper, r.mine[SUB:, :], r.got[SUB:, :])
    gate = r.gate_part.shape[1]
    scan = r.grad_mix.shape[1] - gate
    r.grad_mix[:, :wide] = first
    r.grad_mix[:, wide:scan] = second[:, 2 * wide - scan :]
    r.grad_mix[:, scan:] = r.gate_part[...]
    index = 0
    for name in (N.vec_in, N.vec_out, N.vec_ffn, N.vec_lower, N.vec_fbias, N.vec_phase):
        ref = getattr(r, name)
        for tile in range(ref.shape[0] // LANES):
            rows, lanes = sum_place(wide, index)
            ref[tile * LANES : (tile + 1) * LANES] = r.mine[rows, lanes].reshape(LANES)
            index += 1


def ffn_back_kernel(r):
    rows, width = r.after.shape
    size = row_block(rows, 336)
    r.sums_ffn[...] = jnp.zeros(r.sums_ffn.shape, F32)

    def ffn_back(step):
        at = rows_at(step, size)
        back = dot(r.grad_gu[at, :], r.wgu[...], 1, 1)
        total = r.after[at, :]
        scale = lax.rsqrt(jnp.mean(total * total, axis=-1, keepdims=True) + epsilon)
        normed = total * scale
        r.sums_ffn[...] += fold_rows(back * normed)
        scaled = back * r.vec[2:3, :]
        shared = jnp.mean(scaled * normed, axis=-1, keepdims=True)
        made = r.cot[at, :].astype(F32) + scale * (scaled - normed * shared)
        r.grad_mid[at, :] = made
        r.grad_mid_low[at, :] = made.astype(BF16)

    loop(rows // size, ffn_back)


def mix_back_kernel(shape, r):
    seqs, positions, chans = shape
    tiles = chans // LANES
    steps = positions // SUB
    rows = seqs * positions
    width = 2 * chans
    small = row_block(rows, 144)
    r.sums_out[...] = jnp.zeros(r.sums_out.shape, F32)

    def mix_back(step):
        at = rows_at(step, small)
        back = dot(r.grad_mid_low[at, :], r.wout[...], 1, 1)
        squares = jnp.zeros((small, LANES), F32)
        for tile in range(2 * tiles):
            part = r.states[tile, at, :]
            squares = squares + part * part
        scale = lax.rsqrt(jnp.sum(squares, axis=-1, keepdims=True) / width + epsilon)
        shared = jnp.zeros((small, LANES), F32)
        for tile in range(2 * tiles):
            lanes = slice(tile * LANES, (tile + 1) * LANES)
            gated = r.gate[tile, at, :]
            sigma = sigmoid(gated)
            act = gated * sigma
            normed = r.states[tile, at, :] * scale
            part = back[:, lanes]
            gain = r.vec[1:2, lanes]
            r.grad_gate[at, lanes] = (part * normed * gain * (sigma + act * (1.0 - sigma))).astype(BF16)
            inner = part * act
            product = inner * normed
            r.sums_out[:, lanes] += fold_rows(product)
            shared = shared + product * gain
            r.seeds[tile, at, :] = inner * gain
        mean = jnp.sum(shared, axis=-1, keepdims=True) / width
        for tile in range(2 * tiles):
            normed = r.states[tile, at, :] * scale
            r.seeds[tile, at, :] = scale * (r.seeds[tile, at, :] - normed * mean)

    loop(rows // small, mix_back)

    def scan(seq):
        for tile in range(tiles):
            lanes = slice(tile * LANES, (tile + 1) * LANES)
            low_bound, cos_t, sin_t = r.vec[3:4, lanes], r.vec[4:5, lanes], sine_of(r, lanes)
            flow_r = jnp.zeros((SUB, LANES), F32)
            flow_i = jnp.zeros((SUB, LANES), F32)
            for step in reversed(range(steps)):
                at = pl.ds(seq * positions + step, SUB, stride=steps)
                _, _, _, retain = forget_gate(r.pre[2 * tiles + tile, at, :], low_bound)
                mul_r, mul_i = retain * cos_t, retain * sin_t
                adj_r = r.seeds[tile, at, :] + flow_r
                adj_i = r.seeds[tiles + tile, at, :] + flow_i
                flow_r = mul_r * adj_r + mul_i * adj_i
                flow_i = mul_r * adj_i - mul_i * adj_r
            at = pl.ds(pl.multiple_of(seq * SUB, SUB), SUB)
            r.chunks_back[tile, at, :] = flow_r
            r.chunks_back[tiles + tile, at, :] = flow_i

    r.chunks_back[...] = jnp.zeros(r.chunks_back.shape, F32)
    loop(seqs, scan)
    pad = r.ends_back.shape[2]
    for tile in range(tiles):
        product = jnp.ones((pad, LANES), F32)
        add_r, add_i = jnp.zeros((pad, LANES), F32), jnp.zeros((pad, LANES), F32)
        for chunk in reversed(range(SUB)):
            at = pl.ds(chunk, pad, stride=SUB)
            product = product * r.chunks[tile, at, :]
            _, _, add_r, add_i = chunk_step(r, tiles, tile, at, r.chunks_back, 0, add_r, add_i, True)
        r.ends_back[0, tile] = product
        r.ends_back[0, tiles + tile] = add_r
        r.ends_back[0, 2 * tiles + tile] = add_i


def append_kernel(r):
    count = r.have.shape[0]
    r.both[:count] = r.have[...]
    r.both[count:] = r.got[...]


def enter_kernel(bits, r):
    mine = lax.axis_index(N.seq)
    count = r.have.shape[0]
    tiles = r.have.shape[1] // 3
    r.both[:count] = r.have[...]
    r.both[count:] = r.got[...]
    for tile in range(tiles):
        lanes = slice(tile * LANES, (tile + 1) * LANES)
        chans = r.vec.shape[1] // 2
        turn_r = r.vec[6:7, lanes]
        turn_i = r.vec[6:7, chans + lanes.start : chans + lanes.stop]
        now_r = jnp.zeros(r.have.shape[2:], F32)
        now_i = jnp.zeros(r.have.shape[2:], F32)
        for other in reversed(range(1, 2 * count)):
            index = 0
            for place, bit in enumerate(bits):
                index = index + ((((mine ^ other) & bit) // bit) << place)
            product = r.both[index, tile]
            mul_r, mul_i = product * turn_r, product * turn_i
            next_r = mul_r * now_r + mul_i * now_i + r.both[index, tiles + tile]
            next_i = mul_r * now_i - mul_i * now_r + r.both[index, 2 * tiles + tile]
            now_r = jnp.where(other > mine, next_r, now_r)
            now_i = jnp.where(other > mine, next_i, now_i)
        r.start[tile] = now_r
        r.start[tiles + tile] = now_i


def scan_back_kernel(shape, r):
    seqs, positions, chans = shape
    tiles = chans // LANES
    steps = positions // SUB
    entered(r, tiles, r.chunks_back, 0, r.start, r.entries_back, True)
    r.sums_scan[...] = jnp.zeros(r.sums_scan.shape, F32)
    mine = lax.axis_index(N.batch) & 1
    half = r.turned.shape[1] // 2
    shift = 3 * chans - half
    keep_at = pl.ds(pl.multiple_of(mine * shift, LANES), half)
    send_at = pl.ds(pl.multiple_of((1 - mine) * shift, LANES), half)

    def scan(seq):
        for tile in range(tiles):
            lanes = slice(tile * LANES, (tile + 1) * LANES)
            low_bound, cos_t, sin_t = r.vec[3:4, lanes], r.vec[4:5, lanes], sine_of(r, lanes)
            chunk_at = pl.ds(pl.multiple_of(seq * SUB, SUB), SUB)
            flow_r, flow_i = r.entries_back[tile, chunk_at, :], r.entries_back[tiles + tile, chunk_at, :]
            sum_lower = jnp.zeros((SUB, LANES), F32)
            sum_fbias = jnp.zeros((SUB, LANES), F32)
            sum_phase = jnp.zeros((SUB, LANES), F32)
            for step in reversed(range(steps)):
                at = pl.ds(seq * positions + step, SUB, stride=steps)
                in_r, in_i = r.pre[tile, at, :], r.pre[tiles + tile, at, :]
                opened, shut, intake, retain = forget_gate(r.pre[2 * tiles + tile, at, :], low_bound)
                sig_r, sig_i = sigmoid(in_r), sigmoid(in_i)
                act_r, act_i = in_r * sig_r, in_i * sig_i
                adj_r = r.seeds[tile, at, :] + flow_r
                adj_i = r.seeds[tiles + tile, at, :] + flow_i
                mul_r, mul_i = retain * cos_t, retain * sin_t
                flow_r = mul_r * adj_r + mul_i * adj_i
                flow_i = mul_r * adj_i - mul_i * adj_r
                if step > 0:
                    before = pl.ds(seq * positions + step - 1, SUB, stride=steps)
                    past_r, past_i = r.states[tile, before, :], r.states[tiles + tile, before, :]
                else:
                    past_r, past_i = r.entries[tile, chunk_at, :], r.entries[tiles + tile, chunk_at, :]
                grad_r = adj_r * past_r + adj_i * past_i
                grad_i = adj_i * past_r - adj_r * past_i
                grad_retain = grad_r * cos_t + grad_i * sin_t - (adj_r * act_r + adj_i * act_i)
                sum_phase = sum_phase + retain * (grad_i * cos_t - grad_r * sin_t)
                sum_lower = sum_lower + grad_retain * shut
                grad_forget = grad_retain * intake * opened
                sum_fbias = sum_fbias + grad_forget
                at = pl.ds(step, SUB, stride=steps)
                r.made_pre[tile, at, :] = adj_r * intake * (sig_r + act_r * (1.0 - sig_r))
                r.made_pre[tiles + tile, at, :] = adj_i * intake * (sig_i + act_i * (1.0 - sig_i))
                r.made_pre[2 * tiles + tile, at, :] = grad_forget
            r.sums_scan[0:SUB, lanes] += sum_lower
            r.sums_scan[SUB : 2 * SUB, lanes] += sum_fbias
            r.sums_scan[2 * SUB : 3 * SUB, lanes] += sum_phase
        seq_rows = rows_at(seq, positions)
        for tile in range(3 * tiles):
            r.grad_pre[seq_rows, tile * LANES : (tile + 1) * LANES] = r.made_pre[tile].astype(BF16)
        r.turned[seq_rows, :half] = r.grad_pre[seq_rows, keep_at]
        r.turned[seq_rows, half:] = r.grad_pre[seq_rows, send_at]

    loop(seqs, scan)


def grad_scan_kernel(plan, chans, r):
    kept, sent = block_slots(plan)
    half = r.turned.shape[1] // 2
    size = r.low.shape[1] // plan.made
    tall = min(r.low.shape[1], 384)
    count = tall // size
    for part in range(r.low.shape[1] // tall):
        made = dot(r.low[:, part * tall : (part + 1) * tall], r.turned[...], 0, 0)
        there = slice(part * count, (part + 1) * count)
        store_blocks(r.keep_scan, kept[there], size, slice(0, half), made[:, :half], SUB)
        store_blocks(r.made, sent[there], size, slice(0, half), made[:, half:])
    zero = jnp.zeros((SUB, half), F32)
    r.keep_scan[0:SUB, :] = zero
    index = 0
    for source in (r.sums_in, r.sums_out, r.sums_ffn):
        for tile in range(source.shape[1] // LANES):
            total = jnp.sum(source[:, tile * LANES : (tile + 1) * LANES], axis=0, keepdims=True)
            put_sum(r.keep_scan, index, total)
            index += 1
    for part in range(3):
        for tile in range(chans // LANES):
            block = r.sums_scan[part * SUB : (part + 1) * SUB, tile * LANES : (tile + 1) * LANES]
            put_sum(r.keep_scan, index, jnp.sum(block, axis=0, keepdims=True))
            index += 1
    rows = r.made.shape[0] // PIECES
    r.send_scan0[0:SUB, :] = r.keep_scan[0:SUB, :]
    r.send_scan0[SUB:, :] = r.made[:rows, :]
    for piece in range(1, PIECES):
        getattr(r, "send_scan%d" % piece)[...] = r.made[piece * rows : (piece + 1) * rows, :]


def sum_place(wide, index):
    row, tile = divmod(index, wide // LANES)
    return slice(row, row + 1), slice(tile * LANES, (tile + 1) * LANES)


def put_sum(ref, index, total):
    rows, lanes = sum_place(ref.shape[1], index)
    ref[rows, lanes] = total


def input_back_kernel(r):
    rows, chans3 = r.grad_pre.shape
    size = row_block(rows, 336)
    r.sums_in[...] = jnp.zeros(r.sums_in.shape, F32)

    for step in range(rows // size):
        at = pl.ds(step * size, size)
        back = dot(r.grad_pre[at, :], r.wmix[:, :chans3], 1, 1)
        back = back + dot(r.grad_gate[at, :], r.wmix[:, chans3:], 1, 1)
        inputs = r.tok[at, :].astype(F32)
        scale = lax.rsqrt(jnp.mean(inputs * inputs, axis=-1, keepdims=True) + epsilon)
        normed = inputs * scale
        r.sums_in[...] += fold_rows(back * normed)
        scaled = back * r.vec[0:1, :]
        shared = jnp.mean(scaled * normed, axis=-1, keepdims=True)
        r.made[at, :] = r.grad_mid[at, :] + scale * (scaled - normed * shared)
        r.save(r.made.at[at, :], r.grad_tokens.at[at, :])


def output_kernel(count, r):
    rows, _ = r.output.shape
    r.mark[...] = jnp.zeros(r.mark.shape, F32)
    size = rows // count
    r.wait(N.wdown_in)
    for step in range(count):
        at = pl.ds(step * size, size)
        for name in (N.after_in, N.hidden_in):
            r.wait(name + str(step))
        made = dot(getattr(r, N.hidden_in + str(step))[...], r.wdown_in[...], 1, 0)
        r.made[at, :] = (getattr(r, N.after_in + str(step))[...] + made).astype(BF16)
        r.save(r.made.at[at, :], r.output.at[at, :])


def run(pool, kernel, name, new=(), args=None, fetch=None, load=None, out=(), drop=(), reuse=None, scratch=None, vmem=5, after=(), late=()):
    args, fetch, load, reuse, scratch = args or {}, fetch or {}, load or {}, reuse or {}, scratch or {}
    whole = {key: value for key, value in load.items() if not isinstance(value, tuple)}
    scratch = {**scratch, **{key: pltpu.VMEM(value.shape, value.dtype) for key, value in whole.items()}}
    parts = {key: value for key, value in load.items() if isinstance(value, tuple)}
    load = {key: value for key, value in load.items() if key not in parts}
    incoming = {**fetch, **load}
    for key, (value, count) in parts.items():
        rows = value.shape[0] // count
        for part in range(count):
            scratch[key + str(part)] = pltpu.VMEM((rows,) + value.shape[1:], value.dtype)
    kept = [key for key in pool if key not in drop]
    dropped = [key for key in pool if key in drop]
    new_names = [item[0] for item in new]
    operands = [pool[key] for key in kept + dropped]
    operands += [pltpu.with_memory_space_constraint(value, pltpu.VMEM) for value in args.values()]
    operands += [pltpu.with_memory_space_constraint(value, pltpu.HBM) for value in incoming.values()]
    in_names = kept + dropped + list(args) + ["hbm " + key for key in incoming] + ["after%d" % index for index in range(len(after))]
    operands += list(after)
    in_names += ["hbm " + key for key in parts]
    operands += [pltpu.with_memory_space_constraint(value, pltpu.HBM) for value, _ in parts.values()]
    shapes = [pltpu.VMEM(pool[key].shape, pool[key].dtype) for key in kept]
    shapes += [pltpu.VMEM(shape, kind) for _, shape, kind in new]
    shapes += [pltpu.VMEM(value.shape, value.dtype) for value in fetch.values()]
    shapes += [pltpu.HBM(shape, kind) for _, shape, kind in out]
    out_names = ["out " + key for key in kept] + new_names + list(fetch) + [item[0] for item in out]
    aliases = {index: index for index in range(len(kept))}
    for key, old in reuse.items():
        aliases[in_names.index(old)] = out_names.index(key)
    copies = len(incoming) + sum(count for _, count in parts.values()) + len(out) + 8

    def body(*refs):
        r = types.SimpleNamespace(**dict(zip(in_names + out_names + list(scratch), refs)))
        sems = refs[-1]
        waiting = {}
        for index, key in enumerate(incoming):
            copy = pltpu.make_async_copy(getattr(r, "hbm " + key), getattr(r, key), sems.at[index])
            if key not in late:
                copy.start()
            waiting[key] = copy

        index = len(incoming)
        for part in range(max([count for _, count in parts.values()], default=0)):
            for key, (value, count) in parts.items():
                rows = value.shape[0] // count
                source = getattr(r, "hbm " + key).at[pl.ds(part * rows, rows), :]
                copy = pltpu.make_async_copy(source, getattr(r, key + str(part)), sems.at[index])
                copy.start()
                waiting[key + str(part)] = copy
                index += 1
        taken = index

        def save(source, target):
            index = taken + len([key for key in waiting if key.startswith("save ")])
            copy = pltpu.make_async_copy(source, target, sems.at[index])
            copy.start()
            waiting["save " + str(index)] = copy

        r.wait = lambda key: waiting.pop(key).wait()
        r.save = save
        r.start_late = lambda: [waiting[key].start() for key in late]
        kernel(r)
        for copy in waiting.values():
            copy.wait()

    made = pl.pallas_call(
        body,
        out_shape=shapes,
        in_specs=[pl.BlockSpec(memory_space=pltpu.VMEM)] * (len(kept) + len(dropped) + len(args))
        + [pl.BlockSpec(memory_space=pltpu.HBM)] * len(incoming)
        + [pl.BlockSpec(memory_space=pl.ANY)] * len(after)
        + [pl.BlockSpec(memory_space=pltpu.HBM)] * len(parts),
        out_specs=[pl.BlockSpec(memory_space=pl.ANY)] * len(kept)
        + [pl.BlockSpec(memory_space=pltpu.VMEM)] * (len(new) + len(fetch))
        + [pl.BlockSpec(memory_space=pltpu.HBM)] * len(out),
        scratch_shapes=list(scratch.values()) + [pltpu.SemaphoreType.DMA((copies,))],
        input_output_aliases=aliases,
        compiler_params=pltpu.CompilerParams(vmem_limit_bytes=vmem * MIB),
        cost_estimate=pl.CostEstimate(flops=int(SCALE * TIME.get(name, FOLD if name.startswith(N.fold) else 0.3) * 1.15e9), bytes_accessed=0, transcendentals=0),
        name=name,
    )(*operands)
    pool.clear()
    count = len(kept) + len(new) + len(fetch)
    pool.update(zip(kept + new_names + list(fetch), made[:count]))
    return made[count:]


def combine(earlier, later_part):
    mul_r, mul_i, add_r, add_i = earlier
    new_r, new_i, plus_r, plus_i = later_part
    out_mr = mul_r * new_r - mul_i * new_i
    out_mi = mul_r * new_i + mul_i * new_r
    out_ar = new_r * add_r - new_i * add_i + plus_r
    out_ai = new_r * add_i + new_i * add_r + plus_i
    return (out_mr, out_mi, out_ar, out_ai)


def across(value, axis, bit):
    size = lax.axis_size(axis)
    return lax.ppermute(value, axis, [(at, at ^ bit) for at in range(size)])


def across_by_core(value, dims):
    seq_size, batch_size = lax.axis_size(N.seq), lax.axis_size(N.batch)
    pairs = []
    for seq in range(seq_size):
        for batch in range(batch_size):
            axis, bit = dims[batch & 1]
            to = (seq ^ bit, batch) if axis == N.seq else (seq, batch ^ bit)
            pairs.append((seq * batch_size + batch, to[0] * batch_size + to[1]))
    return lax.ppermute(value, (N.seq, N.batch), pairs)


def make_plan(seq_size, batch_size, width, kind):
    along_seq = [(N.seq, 1 << bit) for bit in range(seq_size.bit_length() - 1)]
    along_batch = [(N.batch, 1 << bit) for bit in range(1, batch_size.bit_length() - 1)]
    near, next_bit, far = along_seq[:1], along_seq[1:2], along_seq[2:]
    rest = batch_size // 2
    places = {"y": near, "z": next_bit, "w": far, "x": along_batch}
    orders = tuple(sum((places[letter] for letter in order), []) for order in ORDERS[kind])
    blocks = seq_size * rest
    in_place = width % (blocks * SUB) == 0
    return types.SimpleNamespace(
        seq_size=seq_size, batch_size=batch_size, orders=orders, blocks=blocks, in_place=in_place, rest=rest,
        made=blocks if in_place else 2 * SUB, steps=list(zip(*orders)),
    )


class Chunk:
    def __init__(self, pool, plan, name, parts=None, head=0):
        self.pool, self.plan, self.name, self.head, self.done = pool, plan, name, head, 0
        self.parts, self.got = parts or (name,), {}

    def begin(self, part=None):
        part = part or self.name
        names = [key for key in self.pool if key.startswith(N.send_ + part)]
        sent = [self.pool.pop(key) for key in names]
        if not self.plan.in_place:
            sent = [self.arranged(jnp.concatenate(sent, axis=0), 1)]
            self.pool[N.keep_ + part] = self.arranged(self.pool[N.keep_ + part], 0)
        for piece, value in enumerate(sent):
            self.got["got_%s%d" % (part, piece)] = across(value, N.batch, 1)

    def arranged(self, values, side):
        seq, batch = lax.axis_index(N.seq), lax.axis_index(N.batch)
        rest = self.plan.rest
        block = np.arange(self.plan.blocks)
        found = []
        for order in self.plan.orders:
            slots = jnp.zeros(block.shape, jnp.int32)
            for place, (axis, bit) in enumerate(order):
                fixed = block // rest if axis == N.seq else (block % rest) * 2
                mine = seq if axis == N.seq else batch
                flag = (((jnp.asarray(fixed, jnp.int32) ^ mine) & bit) != 0).astype(jnp.int32)
                slots = slots + (flag << (len(order) - 1 - place))
            found.append(slots)
        odd = (batch & 1) == 1
        slots = jnp.where(odd, found[1 - side], found[side])
        body = values[self.head :]
        cut = body.reshape((self.plan.blocks, -1) + body.shape[1:])
        body = jnp.take(cut, jnp.argsort(slots), axis=0).reshape(body.shape)
        return jnp.concatenate([values[: self.head], body], axis=0) if self.head else body

    def apart(self):
        names = [N.keep_ + part for part in self.parts] if self.done == 0 else [N.keep_ + self.name]
        self.pool = {name: self.pool.pop(name) for name in names}

    def fold(self, after=()):
        keep, head = N.keep_ + self.name, self.head
        send, later = N.send_ + self.name, N.later_ + self.name
        names = [N.keep_ + part for part in self.parts] if self.done == 0 else [keep]
        rows, cols = self.pool[names[0]].shape[0], sum(self.pool[name].shape[1] for name in names)
        half = (rows - head) // 2
        if half % SUB == 0:
            if self.done == 0:
                pieces = len(self.got) // len(self.parts)
                kernel = functools.partial(fold_first_kernel, self.parts, head, pieces, (send, later))
            else:
                kernel = functools.partial(fold_kernel, (keep, send, later), head)
            run(
                self.pool, kernel, N.fold_ + self.name,
                new=[(send, (head + half, cols), F32), (later, (head + half, cols), F32)], args=self.got, drop=tuple(names),
                vmem=6 if self.plan.in_place else 24, after=after,
            )
            self.pool[keep] = self.pool.pop(later)
            self.sent = self.pool.pop(send)
        else:
            values = [self.pool.pop(name) + got for name, got in zip(names, self.got.values())]
            value = jnp.concatenate(values, axis=1)
            self.sent = jnp.concatenate([value[:head], value[head + half :]], axis=0)
            self.pool[keep] = value[: head + half]

    def send(self):
        self.got = {N.got: across_by_core(self.sent, self.plan.steps[self.done])}
        self.done += 1

    def step(self, after=()):
        self.fold(after)
        self.send()

    def whole(self, after=()):
        run(
            self.pool, functools.partial(sum_kernel, N.keep_ + self.name), N.sum_ + self.name,
            new=[(N.total, self.pool[N.keep_ + self.name].shape, F32)], args=self.got, drop=(N.keep_ + self.name,), after=after,
        )
        return self.pool.pop(N.total)


def carry(pool, total, between):
    size = lax.axis_size(N.seq)
    hops = size.bit_length() - 1
    sent = pool.pop(total)
    for hop in range(hops):
        first, last = hop == 0, hop == hops - 1
        got = across(sent, N.seq, 1 << hop)
        between(hop)
        shape = sent.shape
        if last:
            new = [(N.start, (shape[0] // 2,) + shape[1:], F32)]
        else:
            new = [(N.before_next, shape, F32), (N.total_next, shape, F32)]
        run(
            pool, functools.partial(carry_kernel, 1 << hop, first, last, False), N.carry,
            new=new, args={N.got: got, N.total: sent}, drop=(N.before,),
        )
        if not last:
            sent = pool.pop(N.total_next)
            pool[N.before] = pool.pop(N.before_next)


def carry_back(pool, name, between):
    size = lax.axis_size(N.seq)
    order = [HOPS[place] for place in range(3) if HOPS[place] < size.bit_length() - 1] + list(range(3, size.bit_length() - 1))
    bits = [1 << hop for hop in order]
    sent = pool.pop(name)
    for hop, bit in enumerate(bits):
        got = across(sent, N.seq, bit)
        between(hop)
        shape = sent.shape
        if hop < len(bits) - 1:
            run(pool, append_kernel, N.append, new=[(N.both, (2 * shape[0],) + shape[1:], F32)], args={N.have: sent, N.got: got})
            sent = pool.pop(N.both)
        else:
            run(
                pool, functools.partial(enter_kernel, bits), N.enter,
                new=[(N.start, (2 * shape[1] // 3,) + shape[2:], F32)], args={N.have: sent, N.got: got},
                scratch={N.both: pltpu.VMEM((2 * shape[0],) + shape[1:], F32)},
            )


def per_device(
    tokens, cotangent, gain_in, w_mix, lower, fbias, phase, gain_out, w_out, gain_ffn, w_gu, w_down
):
    seqs, positions, width = tokens.shape
    chans = lower.shape[0]
    units = w_down.shape[0]
    rows = seqs * positions
    tiles = chans // LANES
    shape = (seqs, positions, chans)
    pad = -(-seqs // SUB) * SUB
    seq_size, batch_size = lax.axis_size(N.seq), lax.axis_size(N.batch)
    tokens = tokens.reshape(rows, width)
    cotangent = cotangent.reshape(rows, width)
    wide_plan, down_plan, scan_plan = (
        make_plan(seq_size, batch_size, width, kind) for kind in (N.wide, N.down, N.scan)
    )
    pool = {}
    raw = {N.raw_in: gain_in, N.raw_lower: lower, N.raw_fbias: fbias, N.raw_phase: phase, N.raw_out: gain_out, N.raw_ffn: gain_ffn}
    run(
        pool, functools.partial(project_kernel, shape), N.project,
        new=[(N.vec, (SUB, width), F32), (N.low, (rows, width), BF16), (N.pre, (3 * tiles, rows, LANES), F32), (N.steps, (3 * tiles, rows, LANES), F32),
             (N.chunks, (3 * tiles, pad * SUB, LANES), F32), (N.ends, (4 * tiles, pad, LANES), F32)],
        fetch={N.tok: tokens, N.wmix: w_mix, N.wdown: w_down, N.cot: cotangent}, load=raw, late=(N.wdown, N.cot),
    )

    def between(hop):
        if hop == 0:
            run(
                pool, functools.partial(gate_kernel, chans), N.gate, new=[(N.gate, (2 * tiles, rows, LANES), F32)],
                fetch={N.wout: w_out}, drop=(N.wmix,),
            )
        elif hop <= 2:
            run(
                pool, functools.partial(hidden_back_kernel, (hop - 1) * units // 2, "back%d" % (hop - 1)), N.hidden_back,
                new=[("back%d" % (hop - 1), (rows, units // 2), BF16)], drop=(N.wdown,) if hop == 2 else (),
            )

    carry(pool, N.ends, between)
    run(
        pool, functools.partial(mix_kernel, shape), N.mix,
        new=[(N.states, (2 * tiles, rows, LANES), F32), (N.entries, (2 * tiles, pad * SUB, LANES), F32),
             (N.mixed, (rows, width), BF16), (N.after, (rows, width), F32), (N.ffn_low, (rows, width), BF16)],
        fetch={N.wgu: w_gu}, drop=(N.start, N.wout, N.tok, N.steps),
    )
    away = (N.after, N.mixed, N.low, N.pre, N.states, N.gate)
    kinds = [(key + N._out, pool[key].shape, pool[key].dtype) for key in away]
    stored = run(
        pool, ffn_kernel, N.ffn, new=[(N.hidden, (rows, units), BF16), (N.grad_gu, (rows, 2 * units), BF16)],
        out=kinds, drop=(N.back0, N.back1) + away[1:],
    )
    stored = dict(zip(away, stored))
    wide, down = Chunk(pool, wide_plan, N.wide), Chunk(pool, down_plan, N.down)
    for side, sending in ((N.send_wide, True), (N.keep_wide, False)):
        run(
            pool, functools.partial(grad_wide_kernel, wide_plan, N.ffn_low, N.grad_gu, side, sending, 512), N.grad_gu,
            new=[(side, (width, units), F32)], drop=() if sending else (N.ffn_low,),
        )
        if sending:
            sent = pool.pop(N.send_wide)
    pool[N.send_wide] = sent
    wide.begin()
    (hidden_out,) = run(
        pool, lambda r: (r.save(r.hidden, r.hidden_out),
                         grad_narrow_kernel(down_plan, N.hidden, N.cot, N.keep_down, N.send_down, r)), N.grad_down,
        new=[(N.keep_down, (units, width // 2), F32), (N.send_down, (units, width // 2), F32)],
        out=[(N.hidden_out, (rows, units), BF16)], drop=(N.hidden,),
        scratch={N.turned: pltpu.VMEM((rows, width), BF16)},
    )
    down.begin()
    wide.step()
    run(
        pool, ffn_back_kernel, N.ffn_back,
        new=[(N.grad_mid, (rows, width), F32), (N.grad_mid_low, (rows, width), BF16), (N.sums_ffn, (SUB, width), F32)],
        fetch={N.states: stored[N.states], N.gate: stored[N.gate], N.wout: w_out, N.pre: stored[N.pre]},
        drop=(N.grad_gu, N.wgu, N.after, N.cot), reuse={N.grad_mid: N.after},
    )
    down.step()
    run(
        pool, functools.partial(mix_back_kernel, shape), N.mix_back,
        new=[(N.grad_gate, (rows, width), BF16), (N.seeds, (2 * tiles, rows, LANES), F32),
             (N.chunks_back, (2 * tiles, pad * SUB, LANES), F32), (N.ends_back, (1, 3 * tiles, pad, LANES), F32),
             (N.sums_out, (SUB, width), F32)],
        fetch={N.low: stored[N.low], N.mixed: stored[N.mixed]}, drop=(N.gate, N.wout), reuse={N.seeds: N.gate},
    )
    half = width // 2
    turned = {N.turned: pltpu.VMEM((rows, width), BF16)}
    third = Chunk(pool, down_plan, N.third, (N.out, N.gates))
    hops = seq_size.bit_length() - 1

    def between(hop):
        if hop == 0:
            run(
                pool, functools.partial(grad_narrow_kernel, down_plan, N.mixed, N.grad_mid_low, N.keep_out, N.send_out),
                N.grad_out, new=[(N.keep_out, (width, half), F32), (N.send_out, (width, half), F32)],
                drop=(N.mixed, N.grad_mid_low), scratch=turned,
            )
            third.begin(N.out)
        elif hop == 1:
            run(
                pool, functools.partial(grad_narrow_kernel, down_plan, N.low, N.grad_gate, N.keep_gates, N.send_gates),
                N.grad_gate, new=[(N.keep_gates, (width, half), F32), (N.send_gates, (width, half), F32)], scratch=turned,
            )
            third.begin(N.gates)
            wide.fold()
        if hop == hops - 1:
            wide.send()

    carry_back(pool, N.ends_back, between)
    span = -(-3 * tiles // 2) * LANES
    run(
        pool, functools.partial(scan_back_kernel, shape), N.scan_back,
        new=[(N.grad_pre, (rows, 3 * chans), BF16), (N.sums_scan, (3 * SUB, chans), F32), (N.turned, (rows, 2 * span), BF16)],
        fetch={N.wmix: w_mix, N.tok: tokens}, drop=(N.start, N.seeds, N.chunks, N.chunks_back, N.pre, N.states, N.entries),
        scratch={N.entries_back: pltpu.VMEM((2 * tiles, pad * SUB, LANES), F32),
                 N.made_pre: pltpu.VMEM((3 * tiles, positions, LANES), F32)},
    )
    third.step()
    (grad_tokens,) = run(
        pool, input_back_kernel, N.input_back, new=[(N.sums_in, (SUB, width), F32)],
        out=[(N.grad_tokens, (rows, width), F32)], drop=(N.grad_pre, N.grad_gate, N.wmix, N.tok, N.grad_mid),
        scratch={N.made: pltpu.VMEM((rows, width), F32)}, vmem=9,
    )
    fourth = Chunk(pool, scan_plan, N.scan, head=SUB)
    run(
        pool, functools.partial(grad_scan_kernel, scan_plan, chans), N.grad_scan,
        new=[(N.keep_scan, (SUB + width, span), F32)]
        + [("send_scan%d" % piece, (width // PIECES + (0 if piece else SUB), span), F32) for piece in range(PIECES)],
        scratch={N.made: pltpu.VMEM((width, span), F32)},
        drop=(N.turned, N.low, N.sums_in, N.sums_out, N.sums_ffn, N.sums_scan),
    )
    fourth.begin()
    block = width // wide_plan.blocks
    pair = Chunk({}, down_plan, N.pair)
    sets = {"w": wide, "p": pair, "s": fourth}
    for chunk in (wide, down, third, fourth):
        chunk.apart()

    def begin_pair(before):
        pair.pool = {**down.pool, **third.pool}
        (shape,) = {pair.pool[N.keep_down].shape}
        half = (shape[0] // 2, 2 * shape[1])
        run(
            pair.pool, functools.partial(fold_pair_kernel, down_plan.blocks // 2), N.fold_pair,
            new=[(N.send_pair, half, F32), (N.later_pair, half, F32)],
            args={N.got_down: down.got[N.got], N.got_third: third.got[N.got]}, drop=(N.keep_down, N.keep_third), after=before,
            vmem=5 if down_plan.in_place else 24,
        )
        pair.pool[N.keep_pair] = pair.pool.pop(N.later_pair)
        pair.sent = pair.pool.pop(N.send_pair)
        pair.done = 1
        pair.send()

    found, trail = {}, {}

    def gather_wide(before=()):
        found[N.first] = wide.whole(before)
        found[N.first_got] = across(found[N.first], N.batch, 2)

    def gather_pair(before=()):
        run(
            pair.pool, pack_kernel, N.pack, new=[(N.packed, (block, units), F32)], args=pair.got, drop=(N.keep_pair,), after=before,
        )
        found[N.second] = pair.pool.pop(N.packed)
        found[N.second_got] = across(found[N.second], N.batch, 2)

    def gather_scan():
        found[N.mine] = fourth.whole()
        found[N.got] = across(found[N.mine], N.batch, 2)

    for letter in ROUNDS:
        chunk = sets.get(letter)
        token = letter + str(chunk.done) if chunk else letter
        before = [trail[name] for name in DEPS.get(token, "").split() if name in trail]
        if letter == "o":
            space = {}
            (output,) = run(
                space, functools.partial(output_kernel, 3), N.output, new=[(N.mark, (SUB, LANES), F32)], out=[(N.output, (rows, width), BF16)],
                load={N.wdown_in: w_down, N.after_in: (stored[N.after], 3), N.hidden_in: (hidden_out, 3)},
                scratch={N.made: pltpu.VMEM((rows, width), BF16)}, vmem=14, after=before,
            )
            trail[token] = space[N.mark]
        elif chunk is pair and chunk.done == 0:
            begin_pair(before)
            trail[token] = pair.pool[N.keep_pair]
        elif chunk.done < len(chunk.plan.steps):
            chunk.step(before)
            trail[token] = chunk.pool[N.keep_ + chunk.name]
        elif letter == "w":
            if N.first not in found:
                gather_wide(before)
                trail[token] = found[N.first]
        elif letter == "s":
            if N.mine not in found:
                gather_scan()
                trail[token] = found[N.mine]
        elif N.second not in found:
            gather_pair(before)
    while any(chunk.done < len(chunk.plan.steps) for chunk in sets.values()):
        for chunk in sets.values():
            if chunk.done < len(chunk.plan.steps):
                chunk.step()
    for key, gather in ((N.first, gather_wide), (N.second, gather_pair), (N.mine, gather_scan)):
        if key not in found:
            gather()
    total, total_got = found.pop(N.mine), found.pop(N.got)
    final_rows = 2 * block
    run(
        pool, functools.partial(stack_kernel, N.batch, 2), N.stack, new=[(N.both, (final_rows, 2 * units), F32)],
        args=found, after=(total,),
    )
    packed = pool.pop(N.both)
    packed_got = across(packed, N.batch, 1)
    grad_down, grad_wide, grad_out, gate_part = finish(
        functools.partial(unpack_kernel, batch_size // 2), N.unpack, {N.mine: packed, N.got: packed_got},
        [(N.grad_down, (units // seq_size, width)), (N.grad_wide, (final_rows, 2 * units)), (N.grad_out, (final_rows, width)),
         (N.gate_part, (final_rows, width))],
    )
    run(
        pool, functools.partial(stack_head_kernel, N.batch, 2, SUB), N.stack_scan,
        new=[(N.both, (SUB + final_rows, span), F32)], args={N.mine: total, N.got: total_got}, after=(grad_out,),
    )
    total = pool.pop(N.both)
    total_got = across(total, N.batch, 1)
    grad_mix, *gains = finish(
        finish_kernel, N.finish, {N.mine: total, N.got: total_got, N.gate_part: gate_part},
        [(N.grad_mix, (final_rows, 3 * chans + width)), (N.vec_in, (width,)), (N.vec_out, (width,)), (N.vec_ffn, (width,)),
         (N.vec_lower, (chans,)), (N.vec_fbias, (chans,)), (N.vec_phase, (chans,))],
    )
    return (
        output.reshape(seqs, positions, width),
        grad_tokens.reshape(seqs, positions, width),
        grad_mix,
        grad_out,
        grad_wide,
        grad_down,
        *gains,
    )


def finish(kernel, name, args, outs):
    names = list(args) + [item[0] for item in outs]

    def body(*refs):
        kernel(types.SimpleNamespace(**dict(zip(names, refs))))

    return pl.pallas_call(
        body,
        out_shape=[jax.ShapeDtypeStruct(shape, F32) for _, shape in outs],
        in_specs=[pl.BlockSpec(memory_space=pltpu.VMEM)] * len(args),
        out_specs=[pl.BlockSpec(memory_space=pltpu.VMEM)] * len(outs),
        compiler_params=pltpu.CompilerParams(vmem_limit_bytes=8 * MIB),
        name=name,
    )(*args.values())


def solution(mesh):
    in_specs = (P(N.batch, N.seq, None), P(N.batch, N.seq, None)) + (P(),) * 10
    rows = P(N.seq, None)
    out_specs = (P(N.batch, N.seq, None), P(N.batch, N.seq, None), rows, rows, rows, rows) + (P(),) * 6
    return jax.shard_map(
        per_device, mesh=mesh, in_specs=in_specs, out_specs=out_specs, check_vma=False
    )
```

time: 1730 us -> 180 us (0.10); the launches traced: 1700 us -> 179 us
  local copies, waits for them, and re-layouts: 836 us -> 0.96 us
  blocking collectives: 287 us -> 0 us
  other arithmetic: 214 us -> 0 us
  waiting for transfers between devices: 261 us -> 58.6 us
  matrix products: 82.2 us -> 0 us
  Pallas kernels: 0 us -> 78 us
  starting transfers between devices: 0.46 us -> 40.8 us
    slice x189 -> x0, local copies, waits for them, and re-layouts: 418 us -> none  [the longest x99 269 us: per_device(): lax.associative_scan(combine, (next_r, next_i, seed_r, seed_i), reverse=T...]
    reduce_scatter x4 -> x0, waiting for transfers between devices: 252 us -> none  [the longest x1 167 us: per_device(): lax.psum_scatter(grad_gu, 'seq', scatter_dimension=0, tiled=True)]
    all_gather x8 -> x0, blocking collectives: 246 us -> none  [prefix(): pieces = jax.tree.map(lambda part: lax.all_gather(part, axis), value)]
    pad x96 -> x0, local copies, waits for them, and re-layouts: 225 us -> none  [the longest x48 112 us: per_device(): lax.associative_scan(combine, (next_r, next_i, seed_r, seed_i), reverse=T...]
    add x79 -> x0, other arithmetic: 115 us -> none  [the longest x24 33.4 us: per_device(): lax.associative_scan(combine, (next_r, next_i, seed_r, seed_i), reverse=T...]
    dot_general x12 -> x0, matrix products: 82.2 us -> none  [the longest x4 31.1 us: back_product(): lax.dot_general(grad, weight, (((1,), (1,)), ((), ())), preferred_element...]
    rev x8 -> x0, local copies, waits for them, and re-layouts: 81.7 us -> none  [the longest x4 81.6 us: per_device(): lax.associative_scan(combine, (next_r, next_i, seed_r, seed_i), reverse=T...]
    pallas_call x0 -> x43, Pallas kernels: none -> 78 us  [the longest x41 75.7 us: run(): pl.pallas_call(body, out_shape=shapes, in_specs=[pl.BlockSpec(memory_spac...]
  transfers between devices with their start and end apart: 5 -> 30, of which waited for: 3 -> 18; matrix products, arithmetic and copies ran while one was open for 40% -> 0% of each run, Pallas kernels for 0% -> 30%
where the time goes in v2:
time: 180 us; the launch traced here: 179 us
  Pallas kernels  78 us (43%)
  waiting for transfers between devices  58.6 us (33%)
  starting transfers between devices  40.8 us (23%)
    pallas_call x41, Pallas kernels, run(): pl.pallas_call(body, out_shape=shapes, in_specs=[pl.BlockSpec(memory_spac...  75.7 us
    ppermute x13, waiting for transfers between devices, across_by_core(): return lax.ppermute(value, (N.seq, N.batch), pairs)  46.1 us
    ppermute x13, starting transfers between devices, across_by_core(): return lax.ppermute(value, (N.seq, N.batch), pairs)  22.3 us
    ppermute x17, starting transfers between devices, across(): return lax.ppermute(value, axis, [(at, at ^ bit) for at in range(size)])  18.5 us
    ppermute x17, waiting for transfers between devices, across(): return lax.ppermute(value, axis, [(at, at ^ bit) for at in range(size)])  12.5 us
  transfers between devices with their start and end apart: 30, of which 18 were waited for; matrix products, arithmetic and copies ran while one was open for 0% of the time, Pallas kernels for 30%

profile of v2, /device:TPU:0, one launch (start us, length us, event | category | flops | bytes accessed | tf_op | source)
XLA Modules:
  0.0 179.5 jit_solution(1471258750144458516)
XLA Ops:
  0.6 7.8 %project.1 = (f32[8,768]{1,0:T(8,128)S(1)}, bf16[1008,768]{1,0:T(8,128)(2,1)S(1)}, f32[9,1008,128]{2,1,0:T(8,128)S(1)}, f32[9,1008,128]{2,1,0:T(8,128)S(1)}, f32...) custom-call(bf16[1008,768]{1,0:T(8,128)(2,1)} %bitcast.4, ...), custom_call_target="tpu_custom_call" | custom-call | flops 1840000000 | tf_op jit(solution)/shard_map/project/pallas_call | solution.py:857
  8.5 3.0 %collective-permute-start = (f32[12,8,128]{2,1,0:T(8,128)S(1)}, f32[12,8,128]{2,1,0:T(8,128)S(1)}, u32[]{:S(2)}, u32[]{:S(2)}) collective-permute-start(f32[12,8,128]{2,1,0:T(8,128)S(1)} %get-tuple-element.405.refs_11_), channel_id=1, source_target_pairs={{0,4},{4,0},{8,12},{12,8},{16,20},{20,16},{24,28},{28,24},{1,5},{5... | collective-permute-start | bytes 147464 | tf_op jit(solution)/shard_map/ppermute | solution.py:891
  11.5 1.9 %gate.1 = (f32[8,768]{1,0:T(8,128)S(1)}, bf16[1008,768]{1,0:T(8,128)(2,1)S(1)}, f32[9,1008,128]{2,1,0:T(8,128)S(1)}, f32[9,1008,128]{2,1,0:T(8,128)S(1)}, f32[9,...) custom-call(f32[8,768]{1,0:T(8,128)S(1)} %get-tuple-element.386.refs, ...), custom_call_target="tpu_custom_call", output_to_operand_aliasing={{0}: (0, {}), {1}: (1, {}), {2}: (2, {}), {3}: (3, {}), {4}... | custom-call | flops 414000000 | tf_op jit(solution)/shard_map/gate/pallas_call | solution.py:857
  13.7 2.1 %collective-permute-start.1 = (f32[12,8,128]{2,1,0:T(8,128)S(1)}, f32[12,8,128]{2,1,0:T(8,128)S(1)}, u32[]{:S(2)}, u32[]{:S(2)}) collective-permute-start(f32[12,8,128]{2,1,0:T(8,128)S(1)} %get-tuple-element.429.refs_13_), channel_id=1, source_target_pairs={{0,8},{4,12},{8,0},{12,4},{16,24},{20,28},{24,16},{28,20},{1,9},{5... | collective-permute-start | bytes 147464 | tf_op jit(solution)/shard_map/ppermute | solution.py:891
  15.8 1.9 %hidden_back.2 = (f32[8,768]{1,0:T(8,128)S(1)}, bf16[1008,768]{1,0:T(8,128)(2,1)S(1)}, f32[9,1008,128]{2,1,0:T(8,128)S(1)}, f32[9,1008,128]{2,1,0:T(8,128)S(1)},...) custom-call(f32[8,768]{1,0:T(8,128)S(1)} %get-tuple-element.406.refs, ...), custom_call_target="tpu_custom_call", output_to_operand_aliasing={{0}: (0, {}), {1}: (1, {}), {2}: (2, {}), {3}: (3, {}), {4}... | custom-call | flops 437000000 | tf_op jit(solution)/shard_map/hidden_back/pallas_call | solution.py:857
  18.0 3.1 %collective-permute-start.2 = (f32[12,8,128]{2,1,0:T(8,128)S(1)}, f32[12,8,128]{2,1,0:T(8,128)S(1)}, u32[]{:S(2)}, u32[]{:S(2)}) collective-permute-start(f32[12,8,128]{2,1,0:T(8,128)S(1)} %get-tuple-element.454.refs_13_), channel_id=1, source_target_pairs={{0,16},{4,20},{8,24},{12,28},{16,0},{20,4},{24,8},{28,12},{1,17},{... | collective-permute-start | bytes 147464 | tf_op jit(solution)/shard_map/ppermute | solution.py:891
  21.1 1.9 %hidden_back.3 = (f32[8,768]{1,0:T(8,128)S(1)}, bf16[1008,768]{1,0:T(8,128)(2,1)S(1)}, f32[9,1008,128]{2,1,0:T(8,128)S(1)}, f32[9,1008,128]{2,1,0:T(8,128)S(1)},...) custom-call(f32[8,768]{1,0:T(8,128)S(1)} %get-tuple-element.430.refs, ...), custom_call_target="tpu_custom_call", output_to_operand_aliasing={{0}: (0, {}), {1}: (1, {}), {2}: (2, {}), {3}: (3, {}), {4}... | custom-call | flops 437000000 | tf_op jit(solution)/shard_map/hidden_back/pallas_call | solution.py:857
  23.2 4.9 %mix.1 = (f32[8,768]{1,0:T(8,128)S(1)}, bf16[1008,768]{1,0:T(8,128)(2,1)S(1)}, f32[9,1008,128]{2,1,0:T(8,128)S(1)}, f32[9,64,128]{2,1,0:T(8,128)S(1)}, bf16[1008...) custom-call(f32[8,768]{1,0:T(8,128)S(1)} %get-tuple-element.455.refs, ...), custom_call_target="tpu_custom_call", output_to_operand_aliasing={{0}: (0, {}), {1}: (1, {}), {2}: (2, {}), {3}: (3, {}), {4}... | custom-call | flops 1356999936 | tf_op jit(solution)/shard_map/mix/pallas_call | solution.py:857
  28.1 7.3 %ffn.1 = (f32[8,768]{1,0:T(8,128)S(1)}, f32[9,64,128]{2,1,0:T(8,128)S(1)}, bf16[1008,768]{1,0:T(8,128)(2,1)S(1)}, f32[6,64,128]{2,1,0:T(8,128)S(1)}, f32[1008,76...) custom-call(f32[8,768]{1,0:T(8,128)S(1)} %get-tuple-element.467.refs, ...), custom_call_target="tpu_custom_call", output_to_operand_aliasing={{0}: (0, {}), {1}: (1, {}), {2}: (2, {}), {3}: (3, {}), {4}... | custom-call | flops 1679000064 | tf_op jit(solution)/shard_map/ffn/pallas_call | solution.py:857
  35.4 3.2 %grad_gu.2 = (f32[8,768]{1,0:T(8,128)S(1)}, f32[9,64,128]{2,1,0:T(8,128)S(1)}, bf16[1008,768]{1,0:T(8,128)(2,1)S(1)}, f32[6,64,128]{2,1,0:T(8,128)S(1)}, f32[100...) custom-call(f32[8,768]{1,0:T(8,128)S(1)} %get-tuple-element.482.refs, ...), custom_call_target="tpu_custom_call", output_to_operand_aliasing={{0}: (0, {}), {1}: (1, {}), {2}: (2, {}), {3}: (3, {}), {4}... | custom-call | flops 736000000 | tf_op jit(solution)/shard_map/grad_gu/pallas_call | solution.py:857
  38.7 3.2 %grad_gu.3 = (f32[8,768]{1,0:T(8,128)S(1)}, f32[9,64,128]{2,1,0:T(8,128)S(1)}, bf16[1008,768]{1,0:T(8,128)(2,1)S(1)}, f32[6,64,128]{2,1,0:T(8,128)S(1)}, f32[100...) custom-call(f32[8,768]{1,0:T(8,128)S(1)} %get-tuple-element.491.refs, ...), custom_call_target="tpu_custom_call", output_to_operand_aliasing={{0}: (0, {}), {1}: (1, {}), {2}: (2, {}), {3}: (3, {}), {4}... | custom-call | flops 736000000 | tf_op jit(solution)/shard_map/grad_gu/pallas_call | solution.py:857
  41.8 4.0 %grad_down.1 = (f32[8,768]{1,0:T(8,128)S(1)}, f32[9,64,128]{2,1,0:T(8,128)S(1)}, bf16[1008,768]{1,0:T(8,128)(2,1)S(1)}, f32[6,64,128]{2,1,0:T(8,128)S(1)}, f32[1...) custom-call(f32[8,768]{1,0:T(8,128)S(1)} %get-tuple-element.500.refs, ...), custom_call_target="tpu_custom_call", output_to_operand_aliasing={{0}: (0, {}), {1}: (1, {}), {2}: (2, {}), {3}: (3, {}), {4}... | custom-call | flops 828000000 | tf_op jit(solution)/shard_map/grad_down/pallas_call | solution.py:857
  47.1 1.9 %collective-permute-start.6 = (f32[384,1536]{1,0:T(8,128)S(1)}, f32[384,1536]{1,0:T(8,128)S(1)}, u32[]{:S(2)}, u32[]{:S(2)}) collective-permute-start(f32[384,1536]{1,0:T(8,128)S(1)} %get-tuple-element.623), channel_id=1, source_target_pairs={{0,4},{1,3},{2,6},{3,1},{4,0},{5,7},{6,2},{7,5},{8,12},{9,11},{10,... | collective-permute-start | bytes 7077896 | tf_op jit(solution)/shard_map/ppermute | solution.py:902
  49.0 6.3 %ffn_back.1 = (f32[8,768]{1,0:T(8,128)S(1)}, f32[9,64,128]{2,1,0:T(8,128)S(1)}, f32[6,64,128]{2,1,0:T(8,128)S(1)}, f32[1536,384]{1,0:T(8,128)S(1)}, f32[384,1536...) custom-call(f32[8,768]{1,0:T(8,128)S(1)} %get-tuple-element.521.refs, ...), custom_call_target="tpu_custom_call", output_to_operand_aliasing={{0}: (0, {}), {1}: (1, {}), {2}: (2, {}), {3}: (3, {}), {4}... | custom-call | flops 1495000064 | tf_op jit(solution)/shard_map/ffn_back/pallas_call | solution.py:857
  55.7 7.0 %mix_back.1 = (f32[8,768]{1,0:T(8,128)S(1)}, f32[9,64,128]{2,1,0:T(8,128)S(1)}, f32[6,64,128]{2,1,0:T(8,128)S(1)}, f32[384,1536]{1,0:T(8,128)S(1)}, f32[1008,768...) custom-call(f32[8,768]{1,0:T(8,128)S(1)} %get-tuple-element.546.refs, ...), custom_call_target="tpu_custom_call", output_to_operand_aliasing={{0}: (0, {}), {1}: (1, {}), {2}: (2, {}), {3}: (3, {}), {4}... | custom-call | flops 1610000000 | tf_op jit(solution)/shard_map/mix_back/pallas_call | solution.py:857
  62.8 2.7 %collective-permute-start.5 = (f32[1,9,8,128]{3,2,1,0:T(8,128)S(1)}, f32[1,9,8,128]{3,2,1,0:T(8,128)S(1)}, u32[]{:S(2)}, u32[]{:S(2)}) collective-permute-start(f32[1,9,8,128]{3,2,1,0:T(8,128)S(1)} %get-tuple-element.591.refs_15_), channel_id=1, source_target_pairs={{0,16},{4,20},{8,24},{12,28},{16,0},{20,4},{24,8},{28,12},{1,17},{... | collective-permute-start | bytes 110600 | tf_op jit(solution)/shard_map/ppermute | solution.py:891
  65.5 1.5 grad_out.1
  68.2 1.6 grad_gate.1
  69.9 1.5 collective-permute-start.7
  71.3 4.7 %collective-permute-done.6.refs_16_ = f32[384,1536]{1,0:T(8,128)S(1)} collective-permute-done((f32[384,1536]{1,0:T(8,128)S(1)}, f32[384,1536]{1,0:T(8,128)S(1)}, u32[]{:S(2)}, u32[]{:S(2)}) %collective-permute-start.6) | collective-permute-done | bytes 2359328 | tf_op jit(solution)/shard_map/ppermute | solution.py:902
  76.5 1.9 %collective-permute-start.8 = (f32[4,9,8,128]{3,2,1,0:T(8,128)S(1)}, f32[4,9,8,128]{3,2,1,0:T(8,128)S(1)}, u32[]{:S(2)}, u32[]{:S(2)}) collective-permute-start(f32[4,9,8,128]{3,2,1,0:T(8,128)S(1)} %get-tuple-element.657.refs_16_), channel_id=1, source_target_pairs={{0,4},{4,0},{8,12},{12,8},{16,20},{20,16},{24,28},{28,24},{1,5},{5... | collective-permute-start | bytes 442376 | tf_op jit(solution)/shard_map/ppermute | solution.py:891
  78.6 3.1 %collective-permute-done.8.refs_17_ = f32[4,9,8,128]{3,2,1,0:T(8,128)S(1)} collective-permute-done((f32[4,9,8,128]{3,2,1,0:T(8,128)S(1)}, f32[4,9,8,128]{3,2,1,0:T(8,128)S(1)}, u32[]{:S(2)}, u32[]{:S(2)}) %collective-permute-start.8) | collective-permute-done | bytes 147488 | tf_op jit(solution)/shard_map/ppermute | solution.py:891
  81.8 4.0 %scan_back.1 = (f32[8,768]{1,0:T(8,128)S(1)}, f32[1008,768]{1,0:T(8,128)S(1)}, f32[8,768]{1,0:T(8,128)S(1)}, f32[768,384]{1,0:T(8,128)S(1)}, bf16[1008,768]{1,0:...) custom-call(f32[8,768]{1,0:T(8,128)S(1)} %get-tuple-element.658.refs, ...), custom_call_target="tpu_custom_call", output_to_operand_aliasing={{0}: (0, {}), {1}: (1, {}), {2}: (2, {}), {3}: (3, {}), {4}... | custom-call | flops 920000000 | tf_op jit(solution)/shard_map/scan_back/pallas_call | solution.py:857
  86.2 1.9 %collective-permute-start.16 = (f32[384,768]{1,0:T(8,128)S(1)}, f32[384,768]{1,0:T(8,128)S(1)}, u32[]{:S(2)}, u32[]{:S(2)}) collective-permute-start(f32[384,768]{1,0:T(8,128)S(1)} %get-tuple-element.728), channel_id=1, source_target_pairs={{0,4},{1,3},{2,6},{3,1},{4,0},{5,7},{6,2},{7,5},{8,12},{9,11},{10,... | collective-permute-start | bytes 3538952 | tf_op jit(solution)/shard_map/ppermute | solution.py:902
  88.1 1.6 collective-permute-start.11
  89.7 5.7 %input_back.1 = (f32[8,768]{1,0:T(8,128)S(1)}, f32[8,768]{1,0:T(8,128)S(1)}, f32[768,384]{1,0:T(8,128)S(1)}, f32[8,768]{1,0:T(8,128)S(1)}, bf16[1008,768]{1,0:T(...) custom-call(f32[8,768]{1,0:T(8,128)S(1)} %get-tuple-element.692.refs, ...), custom_call_target="tpu_custom_call", output_to_operand_aliasing={{0}: (0, {}), {1}: (1, {}), {2}: (2, {}), {3}: (3, {}), {4}... | custom-call | flops 1288000000 | tf_op jit(solution)/shard_map/input_back/pallas_call | solution.py:857
  95.4 2.5 %grad_scan.1 = (f32[8,768]{1,0:T(8,128)S(1)}, f32[768,384]{1,0:T(8,128)S(1)}, f32[192,1536]{1,0:T(8,128)S(1)}, f32[384,768]{1,0:T(8,128)S(1)}, f32[776,640]{1,0:...) custom-call(f32[8,768]{1,0:T(8,128)S(1)} %get-tuple-element.707.refs, ...), custom_call_target="tpu_custom_call", output_to_operand_aliasing={{0}: (0, {}), {1}: (1, {}), {2}: (2, {}), {3}: (3, {})} | custom-call | flops 552000000 | tf_op jit(solution)/shard_map/grad_scan/pallas_call | solution.py:857
  98.4 8.8 %collective-permute-done.16.refs_3_ = f32[384,768]{1,0:T(8,128)S(1)} collective-permute-done((f32[384,768]{1,0:T(8,128)S(1)}, f32[384,768]{1,0:T(8,128)S(1)}, u32[]{:S(2)}, u32[]{:S(2)}) %collective-permute-start.16) | collective-permute-done | bytes 1179680 | tf_op jit(solution)/shard_map/ppermute | solution.py:902
  107.6 1.6 collective-permute-start.21
  109.3 6.2 %collective-permute-done.11.refs_1_ = f32[192,1536]{1,0:T(8,128)S(1)} collective-permute-done((f32[192,1536]{1,0:T(8,128)S(1)}, f32[192,1536]{1,0:T(8,128)S(1)}, u32[]{:S(2)}, u32[]{:S(2)}) %collective-permute-start.11) | collective-permute-done | bytes 1179680 | tf_op jit(solution)/shard_map/ppermute | solution.py:902
  116.3 1.8 collective-permute-start.12
  118.1 5.8 %collective-permute-done.21.refs_1_ = f32[384,768]{1,0:T(8,128)S(1)} collective-permute-done((f32[384,768]{1,0:T(8,128)S(1)}, f32[384,768]{1,0:T(8,128)S(1)}, u32[]{:S(2)}, u32[]{:S(2)}) %collective-permute-start.21) | collective-permute-done | bytes 1179680 | tf_op jit(solution)/shard_map/ppermute | solution.py:902
  124.1 2.8 %collective-permute-start.22 = (f32[192,768]{1,0:T(8,128)S(1)}, f32[192,768]{1,0:T(8,128)S(1)}, u32[]{:S(2)}, u32[]{:S(2)}) collective-permute-start(f32[192,768]{1,0:T(8,128)S(1)} %get-tuple-element.740), channel_id=1, source_target_pairs={{0,16},{1,9},{2,18},{3,11},{4,20},{5,13},{6,22},{7,15},{8,24},{9,1... | collective-permute-start | bytes 1769480 | tf_op jit(solution)/shard_map/ppermute | solution.py:902
  126.9 6.6 %output.1 = (f32[8,128]{1,0:T(8,128)S(1)}, bf16[1008,768]{1,0:T(8,128)(2,1)}) custom-call(bf16[1536,768]{1,0:T(8,128)(2,1)} %refs_0_.1, f32[1008,768]{1,0:T(8,128)} %get-tuple-element.481.refs_1_, bf16[1008,1536]{1,0:T(8,128)(2,1)} %get-tuple-element.509.refs_2_), custom_call_target="tpu_custom_call" | custom-call | flops 1610000000 | tf_op jit(solution)/shard_map/output/pallas_call | solution.py:857
  133.5 4.7 %collective-permute-done.17.refs_1_ = f32[392,640]{1,0:T(8,128)S(1)} collective-permute-done((f32[392,640]{1,0:T(8,128)S(1)}, f32[392,640]{1,0:T(8,128)S(1)}, u32[]{:S(2)}, u32[]{:S(2)}) %collective-permute-start.17) | collective-permute-done | bytes 1003552 | tf_op jit(solution)/shard_map/ppermute | solution.py:902
  138.4 1.6 collective-permute-start.19
  140.1 2.7 %collective-permute-start.18 = (f32[48,1536]{1,0:T(8,128)S(1)}, f32[48,1536]{1,0:T(8,128)S(1)}, u32[]{:S(2)}, u32[]{:S(2)}) collective-permute-start(f32[48,1536]{1,0:T(8,128)S(1)} %get-tuple-element.735), channel_id=1, source_target_pairs={{0,16},{1,9},{2,18},{3,11},{4,20},{5,13},{6,22},{7,15},{8,24},{9,1... | collective-permute-start | bytes 884744 | tf_op jit(solution)/shard_map/ppermute | solution.py:902
  142.9 2.0 %collective-permute-start.23 = (f32[96,768]{1,0:T(8,128)S(1)}, f32[96,768]{1,0:T(8,128)S(1)}, u32[]{:S(2)}, u32[]{:S(2)}) collective-permute-start(f32[96,768]{1,0:T(8,128)S(1)} %get-tuple-element.742), channel_id=1, source_target_pairs={{0,8},{1,17},{2,10},{3,19},{4,12},{5,21},{6,14},{7,23},{8,0},{9,25... | collective-permute-start | bytes 884744 | tf_op jit(solution)/shard_map/ppermute | solution.py:902
  144.9 2.6 %collective-permute-done.19.refs_1_ = f32[200,640]{1,0:T(8,128)S(1)} collective-permute-done((f32[200,640]{1,0:T(8,128)S(1)}, f32[200,640]{1,0:T(8,128)S(1)}, u32[]{:S(2)}, u32[]{:S(2)}) %collective-permute-start.19) | collective-permute-done | bytes 512032 | tf_op jit(solution)/shard_map/ppermute | solution.py:902
  147.6 1.8 collective-permute-start.25
  149.4 7.7 %collective-permute-done.18.refs_1_ = f32[48,1536]{1,0:T(8,128)S(1)} collective-permute-done((f32[48,1536]{1,0:T(8,128)S(1)}, f32[48,1536]{1,0:T(8,128)S(1)}, u32[]{:S(2)}, u32[]{:S(2)}) %collective-permute-start.18) | collective-permute-done | bytes 294944 | tf_op jit(solution)/shard_map/ppermute | solution.py:902
  157.8 1.7 collective-permute-start.24
  159.6 2.2 %collective-permute-start.26 = (f32[56,640]{1,0:T(8,128)S(1)}, f32[56,640]{1,0:T(8,128)S(1)}, u32[]{:S(2)}, u32[]{:S(2)}) collective-permute-start(f32[56,640]{1,0:T(8,128)S(1)} %get-tuple-element.745), channel_id=1, source_target_pairs={{0,16},{1,17},{2,18},{3,19},{4,20},{5,21},{6,22},{7,23},{8,24},{9,... | collective-permute-start | bytes 430088 | tf_op jit(solution)/shard_map/ppermute | solution.py:902
  161.8 5.6 %collective-permute-done.26.refs_1_ = f32[56,640]{1,0:T(8,128)S(1)} collective-permute-done((f32[56,640]{1,0:T(8,128)S(1)}, f32[56,640]{1,0:T(8,128)S(1)}, u32[]{:S(2)}, u32[]{:S(2)}) %collective-permute-start.26) | collective-permute-done | bytes 143392 | tf_op jit(solution)/shard_map/ppermute | solution.py:902
  167.5 1.9 %collective-permute-done.24.refs_4_ = f32[48,1536]{1,0:T(8,128)S(1)} collective-permute-done((f32[48,1536]{1,0:T(8,128)S(1)}, f32[48,1536]{1,0:T(8,128)S(1)}, u32[]{:S(2)}, u32[]{:S(2)}) %collective-permute-start.24) | collective-permute-done | bytes 294944 | tf_op jit(solution)/shard_map/ppermute | solution.py:891
  170.3 2.3 %collective-permute-done.28.refs_1_ = f32[96,3072]{1,0:T(8,128)S(1)} collective-permute-done((f32[96,3072]{1,0:T(8,128)S(1)}, f32[96,3072]{1,0:T(8,128)S(1)}, u32[]{:S(2)}, u32[]{:S(2)}) %collective-permute-start.28) | collective-permute-done | bytes 1179680 | tf_op jit(solution)/shard_map/ppermute | solution.py:891
  174.0 1.9 %collective-permute-done.27.refs_2_ = f32[56,640]{1,0:T(8,128)S(1)} collective-permute-done((f32[56,640]{1,0:T(8,128)S(1)}, f32[56,640]{1,0:T(8,128)S(1)}, u32[]{:S(2)}, u32[]{:S(2)}) %collective-permute-start.27) | collective-permute-done | bytes 143392 | tf_op jit(solution)/shard_map/ppermute | solution.py:891
  177.0 1.5 collective-permute-done.29.refs_1_
  (57 shorter events, 12.5 us)
Async XLA Ops:
  8.5 5.1 %collective-permute-start = (f32[12,8,128]{2,1,0:T(8,128)S(1)}, f32[12,8,128]{2,1,0:T(8,128)S(1)}, u32[]{:S(2)}, u32[]{:S(2)}) collective-permute-start(f32[12,8,128]{2,1,0:T(8,128)S(1)} %get-tuple-element.405.refs_11_), channel_id=1, source_target_pairs={{0,4},{4,0},{8,12},{12,8},{16,20},{20,16},{24,28},{28,24},{1,5},{5... | collective-permute-start | bytes 147464 | tf_op jit(solution)/shard_map/ppermute | solution.py:891
  13.7 4.2 %collective-permute-start.1 = (f32[12,8,128]{2,1,0:T(8,128)S(1)}, f32[12,8,128]{2,1,0:T(8,128)S(1)}, u32[]{:S(2)}, u32[]{:S(2)}) collective-permute-start(f32[12,8,128]{2,1,0:T(8,128)S(1)} %get-tuple-element.429.refs_13_), channel_id=1, source_target_pairs={{0,8},{4,12},{8,0},{12,4},{16,24},{20,28},{24,16},{28,20},{1,9},{5... | collective-permute-start | bytes 147464 | tf_op jit(solution)/shard_map/ppermute | solution.py:891
  18.0 5.2 %collective-permute-start.2 = (f32[12,8,128]{2,1,0:T(8,128)S(1)}, f32[12,8,128]{2,1,0:T(8,128)S(1)}, u32[]{:S(2)}, u32[]{:S(2)}) collective-permute-start(f32[12,8,128]{2,1,0:T(8,128)S(1)} %get-tuple-element.454.refs_13_), channel_id=1, source_target_pairs={{0,16},{4,20},{8,24},{12,28},{16,0},{20,4},{24,8},{28,12},{1,17},{... | collective-permute-start | bytes 147464 | tf_op jit(solution)/shard_map/ppermute | solution.py:891
  38.6 8.0 %collective-permute-start.3 = (f32[768,1536]{1,0:T(8,128)S(1)}, f32[768,1536]{1,0:T(8,128)S(1)}, u32[]{:S(2)}, u32[]{:S(2)}) collective-permute-start(f32[768,1536]{1,0:T(8,128)S(1)} %get-tuple-element.520), channel_id=1, source_target_pairs={{0,1},{1,0},{2,3},{3,2},{4,5},{5,4},{6,7},{7,6},{8,9},{9,8},{10,11... | collective-permute-start | bytes 14155784 | tf_op jit(solution)/shard_map/ppermute | solution.py:891
  45.9 9.5 %collective-permute-start.4 = (f32[1536,384]{1,0:T(8,128)S(1)}, f32[1536,384]{1,0:T(8,128)S(1)}, u32[]{:S(2)}, u32[]{:S(2)}) collective-permute-start(f32[1536,384]{1,0:T(8,128)S(1)} %get-tuple-element.545), channel_id=1, source_target_pairs={{0,1},{1,0},{2,3},{3,2},{4,5},{5,4},{6,7},{7,6},{8,9},{9,8},{10,11... | collective-permute-start | bytes 7077896 | tf_op jit(solution)/shard_map/ppermute | solution.py:891
  47.1 28.9 %collective-permute-start.6 = (f32[384,1536]{1,0:T(8,128)S(1)}, f32[384,1536]{1,0:T(8,128)S(1)}, u32[]{:S(2)}, u32[]{:S(2)}) collective-permute-start(f32[384,1536]{1,0:T(8,128)S(1)} %get-tuple-element.623), channel_id=1, source_target_pairs={{0,4},{1,3},{2,6},{3,1},{4,0},{5,7},{6,2},{7,5},{8,12},{9,11},{10,... | collective-permute-start | bytes 7077896 | tf_op jit(solution)/shard_map/ppermute | solution.py:902
  62.8 5.3 %collective-permute-start.5 = (f32[1,9,8,128]{3,2,1,0:T(8,128)S(1)}, f32[1,9,8,128]{3,2,1,0:T(8,128)S(1)}, u32[]{:S(2)}, u32[]{:S(2)}) collective-permute-start(f32[1,9,8,128]{3,2,1,0:T(8,128)S(1)} %get-tuple-element.591.refs_15_), channel_id=1, source_target_pairs={{0,16},{4,20},{8,24},{12,28},{16,0},{20,4},{24,8},{28,12},{1,17},{... | collective-permute-start | bytes 110600 | tf_op jit(solution)/shard_map/ppermute | solution.py:891
  67.0 18.8 %collective-permute-start.9 = (f32[768,384]{1,0:T(8,128)S(1)}, f32[768,384]{1,0:T(8,128)S(1)}, u32[]{:S(2)}, u32[]{:S(2)}) collective-permute-start(f32[768,384]{1,0:T(8,128)S(1)} %get-tuple-element.690), channel_id=1, source_target_pairs={{0,1},{1,0},{2,3},{3,2},{4,5},{5,4},{6,7},{7,6},{8,9},{9,8},{10,11... | collective-permute-start | bytes 3538952 | tf_op jit(solution)/shard_map/ppermute | solution.py:891
  69.8 16.0 %collective-permute-start.10 = (f32[768,384]{1,0:T(8,128)S(1)}, f32[768,384]{1,0:T(8,128)S(1)}, u32[]{:S(2)}, u32[]{:S(2)}) collective-permute-start(f32[768,384]{1,0:T(8,128)S(1)} %get-tuple-element.691), channel_id=1, source_target_pairs={{0,1},{1,0},{2,3},{3,2},{4,5},{5,4},{6,7},{7,6},{8,9},{9,8},{10,11... | collective-permute-start | bytes 3538952 | tf_op jit(solution)/shard_map/ppermute | solution.py:891
  69.9 6.5 %collective-permute-start.7 = (f32[2,9,8,128]{3,2,1,0:T(8,128)S(1)}, f32[2,9,8,128]{3,2,1,0:T(8,128)S(1)}, u32[]{:S(2)}, u32[]{:S(2)}) collective-permute-start(f32[2,9,8,128]{3,2,1,0:T(8,128)S(1)} %get-tuple-element.640.refs_16_), channel_id=1, source_target_pairs={{0,8},{4,12},{8,0},{12,4},{16,24},{20,28},{24,16},{28,20},{1,9},{5... | collective-permute-start | bytes 221192 | tf_op jit(solution)/shard_map/ppermute | solution.py:891
  76.5 5.2 %collective-permute-start.8 = (f32[4,9,8,128]{3,2,1,0:T(8,128)S(1)}, f32[4,9,8,128]{3,2,1,0:T(8,128)S(1)}, u32[]{:S(2)}, u32[]{:S(2)}) collective-permute-start(f32[4,9,8,128]{3,2,1,0:T(8,128)S(1)} %get-tuple-element.657.refs_16_), channel_id=1, source_target_pairs={{0,4},{4,0},{8,12},{12,8},{16,20},{20,16},{24,28},{28,24},{1,5},{5... | collective-permute-start | bytes 442376 | tf_op jit(solution)/shard_map/ppermute | solution.py:891
  78.4 20.0 %collective-permute-start.15 = (f32[768,384]{1,0:T(8,128)S(1)}, f32[768,384]{1,0:T(8,128)S(1)}, u32[]{:S(2)}, u32[]{:S(2)}) collective-permute-start(f32[768,384]{1,0:T(8,128)S(1)} %get-tuple-element.727), channel_id=1, source_target_pairs={{0,4},{1,3},{2,6},{3,1},{4,0},{5,7},{6,2},{7,5},{8,12},{9,11},{10,... | collective-permute-start | bytes 3538952 | tf_op jit(solution)/shard_map/ppermute | solution.py:902
  86.2 21.0 %collective-permute-start.16 = (f32[384,768]{1,0:T(8,128)S(1)}, f32[384,768]{1,0:T(8,128)S(1)}, u32[]{:S(2)}, u32[]{:S(2)}) collective-permute-start(f32[384,768]{1,0:T(8,128)S(1)} %get-tuple-element.728), channel_id=1, source_target_pairs={{0,4},{1,3},{2,6},{3,1},{4,0},{5,7},{6,2},{7,5},{8,12},{9,11},{10,... | collective-permute-start | bytes 3538952 | tf_op jit(solution)/shard_map/ppermute | solution.py:902
  88.1 27.4 %collective-permute-start.11 = (f32[192,1536]{1,0:T(8,128)S(1)}, f32[192,1536]{1,0:T(8,128)S(1)}, u32[]{:S(2)}, u32[]{:S(2)}) collective-permute-start(f32[192,1536]{1,0:T(8,128)S(1)} %get-tuple-element.719), channel_id=1, source_target_pairs={{0,8},{1,17},{2,10},{3,19},{4,12},{5,21},{6,14},{7,23},{8,0},{9,25... | collective-permute-start | bytes 3538952 | tf_op jit(solution)/shard_map/ppermute | solution.py:902
  97.8 17.9 %collective-permute-start.13 = (f32[392,640]{1,0:T(8,128)S(1)}, f32[392,640]{1,0:T(8,128)S(1)}, u32[]{:S(2)}, u32[]{:S(2)}) collective-permute-start(f32[392,640]{1,0:T(8,128)S(1)} %get-tuple-element.723), channel_id=1, source_target_pairs={{0,1},{1,0},{2,3},{3,2},{4,5},{5,4},{6,7},{7,6},{8,9},{9,8},{10,11... | collective-permute-start | bytes 3010568 | tf_op jit(solution)/shard_map/ppermute | solution.py:891
  97.9 17.8 %collective-permute-start.14 = (f32[384,640]{1,0:T(8,128)S(1)}, f32[384,640]{1,0:T(8,128)S(1)}, u32[]{:S(2)}, u32[]{:S(2)}) collective-permute-start(f32[384,640]{1,0:T(8,128)S(1)} %get-tuple-element.724), channel_id=1, source_target_pairs={{0,1},{1,0},{2,3},{3,2},{4,5},{5,4},{6,7},{7,6},{8,9},{9,8},{10,11... | collective-permute-start | bytes 2949128 | tf_op jit(solution)/shard_map/ppermute | solution.py:891
  107.6 16.3 %collective-permute-start.21 = (f32[384,768]{1,0:T(8,128)S(1)}, f32[384,768]{1,0:T(8,128)S(1)}, u32[]{:S(2)}, u32[]{:S(2)}) collective-permute-start(f32[384,768]{1,0:T(8,128)S(1)} %get-tuple-element.738), channel_id=1, source_target_pairs={{0,2},{1,5},{2,0},{3,7},{4,6},{5,1},{6,4},{7,3},{8,10},{9,13},{10,... | collective-permute-start | bytes 3538952 | tf_op jit(solution)/shard_map/ppermute | solution.py:902
  116.1 22.1 %collective-permute-start.17 = (f32[392,640]{1,0:T(8,128)S(1)}, f32[392,640]{1,0:T(8,128)S(1)}, u32[]{:S(2)}, u32[]{:S(2)}) collective-permute-start(f32[392,640]{1,0:T(8,128)S(1)} %get-tuple-element.731), channel_id=1, source_target_pairs={{0,4},{1,9},{2,6},{3,11},{4,0},{5,13},{6,2},{7,15},{8,12},{9,1},{1... | collective-permute-start | bytes 3010568 | tf_op jit(solution)/shard_map/ppermute | solution.py:902
  116.3 23.6 %collective-permute-start.12 = (f32[96,1536]{1,0:T(8,128)S(1)}, f32[96,1536]{1,0:T(8,128)S(1)}, u32[]{:S(2)}, u32[]{:S(2)}) collective-permute-start(f32[96,1536]{1,0:T(8,128)S(1)} %get-tuple-element.721), channel_id=1, source_target_pairs={{0,2},{1,5},{2,0},{3,7},{4,6},{5,1},{6,4},{7,3},{8,10},{9,13},{10,... | collective-permute-start | bytes 1769480 | tf_op jit(solution)/shard_map/ppermute | solution.py:902
  124.1 18.7 %collective-permute-start.22 = (f32[192,768]{1,0:T(8,128)S(1)}, f32[192,768]{1,0:T(8,128)S(1)}, u32[]{:S(2)}, u32[]{:S(2)}) collective-permute-start(f32[192,768]{1,0:T(8,128)S(1)} %get-tuple-element.740), channel_id=1, source_target_pairs={{0,16},{1,9},{2,18},{3,11},{4,20},{5,13},{6,22},{7,15},{8,24},{9,1... | collective-permute-start | bytes 1769480 | tf_op jit(solution)/shard_map/ppermute | solution.py:902
  138.4 9.1 %collective-permute-start.19 = (f32[200,640]{1,0:T(8,128)S(1)}, f32[200,640]{1,0:T(8,128)S(1)}, u32[]{:S(2)}, u32[]{:S(2)}) collective-permute-start(f32[200,640]{1,0:T(8,128)S(1)} %get-tuple-element.736), channel_id=1, source_target_pairs={{0,2},{1,3},{2,0},{3,1},{4,6},{5,7},{6,4},{7,5},{8,10},{9,11},{10,... | collective-permute-start | bytes 1536008 | tf_op jit(solution)/shard_map/ppermute | solution.py:902
  140.1 17.1 %collective-permute-start.18 = (f32[48,1536]{1,0:T(8,128)S(1)}, f32[48,1536]{1,0:T(8,128)S(1)}, u32[]{:S(2)}, u32[]{:S(2)}) collective-permute-start(f32[48,1536]{1,0:T(8,128)S(1)} %get-tuple-element.735), channel_id=1, source_target_pairs={{0,16},{1,9},{2,18},{3,11},{4,20},{5,13},{6,22},{7,15},{8,24},{9,1... | collective-permute-start | bytes 884744 | tf_op jit(solution)/shard_map/ppermute | solution.py:902
  142.9 14.8 %collective-permute-start.23 = (f32[96,768]{1,0:T(8,128)S(1)}, f32[96,768]{1,0:T(8,128)S(1)}, u32[]{:S(2)}, u32[]{:S(2)}) collective-permute-start(f32[96,768]{1,0:T(8,128)S(1)} %get-tuple-element.742), channel_id=1, source_target_pairs={{0,8},{1,17},{2,10},{3,19},{4,12},{5,21},{6,14},{7,23},{8,0},{9,25... | collective-permute-start | bytes 884744 | tf_op jit(solution)/shard_map/ppermute | solution.py:902
  147.6 11.9 %collective-permute-start.25 = (f32[104,640]{1,0:T(8,128)S(1)}, f32[104,640]{1,0:T(8,128)S(1)}, u32[]{:S(2)}, u32[]{:S(2)}) collective-permute-start(f32[104,640]{1,0:T(8,128)S(1)} %get-tuple-element.743), channel_id=1, source_target_pairs={{0,8},{1,5},{2,10},{3,7},{4,12},{5,1},{6,14},{7,3},{8,0},{9,13},{1... | collective-permute-start | bytes 798728 | tf_op jit(solution)/shard_map/ppermute | solution.py:902
  157.2 10.3 %collective-permute-start.20 = (f32[48,1536]{1,0:T(8,128)S(1)}, f32[48,1536]{1,0:T(8,128)S(1)}, u32[]{:S(2)}, u32[]{:S(2)}) collective-permute-start(f32[48,1536]{1,0:T(8,128)S(1)} %sum_wide.1.refs_2_.refs_1_), channel_id=1, source_target_pairs={{0,2},{1,3},{2,0},{3,1},{4,6},{5,7},{6,4},{7,5},{8,10},{9,11},{10,... | collective-permute-start | bytes 884744 | tf_op jit(solution)/shard_map/ppermute | solution.py:891
  157.8 11.6 %collective-permute-start.24 = (f32[48,1536]{1,0:T(8,128)S(1)}, f32[48,1536]{1,0:T(8,128)S(1)}, u32[]{:S(2)}, u32[]{:S(2)}) collective-permute-start(f32[48,1536]{1,0:T(8,128)S(1)} %pack.1.refs_3_), channel_id=1, source_target_pairs={{0,2},{1,3},{2,0},{3,1},{4,6},{5,7},{6,4},{7,5},{8,10},{9,11},{10,... | collective-permute-start | bytes 884744 | tf_op jit(solution)/shard_map/ppermute | solution.py:891
  159.6 7.8 %collective-permute-start.26 = (f32[56,640]{1,0:T(8,128)S(1)}, f32[56,640]{1,0:T(8,128)S(1)}, u32[]{:S(2)}, u32[]{:S(2)}) collective-permute-start(f32[56,640]{1,0:T(8,128)S(1)} %get-tuple-element.745), channel_id=1, source_target_pairs={{0,16},{1,17},{2,18},{3,19},{4,20},{5,21},{6,22},{7,23},{8,24},{9,... | collective-permute-start | bytes 430088 | tf_op jit(solution)/shard_map/ppermute | solution.py:902
  169.6 2.9 %collective-permute-start.28 = (f32[96,3072]{1,0:T(8,128)S(1)}, f32[96,3072]{1,0:T(8,128)S(1)}, u32[]{:S(2)}, u32[]{:S(2)}) collective-permute-start(f32[96,3072]{1,0:T(8,128)S(1)} %get-tuple-element.747.refs_0_), channel_id=1, source_target_pairs={{0,1},{1,0},{2,3},{3,2},{4,5},{5,4},{6,7},{7,6},{8,9},{9,8},{10,11... | collective-permute-start | bytes 3538952 | tf_op jit(solution)/shard_map/ppermute | solution.py:891
  169.7 6.2 %collective-permute-start.27 = (f32[56,640]{1,0:T(8,128)S(1)}, f32[56,640]{1,0:T(8,128)S(1)}, u32[]{:S(2)}, u32[]{:S(2)}) collective-permute-start(f32[56,640]{1,0:T(8,128)S(1)} %sum_scan.1.refs_5_.refs_1_), channel_id=1, source_target_pairs={{0,2},{1,3},{2,0},{3,1},{4,6},{5,7},{6,4},{7,5},{8,10},{9,11},{10,... | collective-permute-start | bytes 430088 | tf_op jit(solution)/shard_map/ppermute | solution.py:891
  175.9 1.0 copy-start
  176.9 1.6 collective-permute-start.29

commit v3 on v2

--- a/solution.py
+++ b/solution.py
@@ -26,7 +26,7 @@
 SCALE = 0.2
 FOLD = 0.3
 HOPS = (2, 1, 0)
-ORDERS = {N.wide: (N.yzxw, N.xwyz), N.down: (N.yxwz, N.xyzw), N.scan: (N.yxzw, N.zxyw)}
+ORDERS = {N.wide: (N.xzyw, N.ywzx), N.down: (N.yxzw, N.xywz), N.scan: (N.xywz, N.yxzw)}
 ROUNDS = N.wpsposwpswpssp
 DEPS = {N.s0: "p0 w2", N.p1: N.s0, "o": N.p1, N.s1: "o", N.w3: N.s1, N.p2: N.s1, N.p3: N.s2, N.w4: N.s2, N.s3: N.w4, N.p4: N.s4}
 PIECES = 2
@@ -88,6 +88,9 @@
     rows = seqs * positions
     size = row_block(rows, 336)
     width = r.tok.shape[1]
+    columns = 3 * chans
+    first = pltpu.make_async_copy(r.mix.at[:, :columns], r.wmix.at[:, :columns], r.own.at[0])
+    first.start()
     r.vec[...] = jnp.zeros(r.vec.shape, F32)
     for name in (N.raw_in, N.raw_lower, N.raw_fbias, N.raw_phase, N.raw_out, N.raw_ffn):
         r.wait(name)
@@ -113,7 +116,9 @@
         r.low[at, :] = (inputs * scale * gain).astype(BF16)
 
     loop(rows // size, norm)
-    r.wait(N.wmix)
+    rest = pltpu.make_async_copy(r.mix.at[:, columns:], r.wmix.at[:, columns:], r.own.at[1])
+    first.wait()
+    rest.start()
     r.start_late()
 
     def project(step):
@@ -145,9 +150,9 @@
                     mul_r * state_i + mul_i * state_r + add_i,
                 )
                 product = product * retain
-                r.steps[tile, at, :] = retain
-                r.steps[tiles + tile, at, :] = add_r
-                r.steps[2 * tiles + tile, at, :] = add_i
+                r.decay[tile, at, :] = retain
+                r.adds[tile, at, :] = add_r
+                r.adds[tiles + tile, at, :] = add_i
             at = pl.ds(pl.multiple_of(seq * SUB, SUB), SUB)
             r.chunks[tile, at, :] = product
             r.chunks[tiles + tile, at, :] = state_r
@@ -156,6 +161,7 @@
     r.chunks[...] = jnp.zeros(r.chunks.shape, F32)
     loop(seqs, scan)
     joined(r, tiles, r.chunks, tiles, r.ends, False)
+    rest.wait()
 
 
 def sine_of(r, lanes):
@@ -274,8 +280,8 @@
             state_r, state_i = r.entries[tile, at, :], r.entries[tiles + tile, at, :]
             for step in range(steps):
                 at = pl.ds(seq * positions + step, SUB, stride=steps)
-                retain = r.steps[tile, at, :]
-                add_r, add_i = r.steps[tiles + tile, at, :], r.steps[2 * tiles + tile, at, :]
+                retain = r.decay[tile, at, :]
+                add_r, add_i = r.adds[tile, at, :], r.adds[tiles + tile, at, :]
                 mul_r, mul_i = retain * cos_t, retain * sin_t
                 state_r, state_i = (
                     mul_r * state_r - mul_i * state_i + add_r,
@@ -789,7 +795,7 @@
         r.save(r.made.at[at, :], r.output.at[at, :])
 
 
-def run(pool, kernel, name, new=(), args=None, fetch=None, load=None, out=(), drop=(), reuse=None, scratch=None, vmem=5, after=(), late=()):
+def run(pool, kernel, name, new=(), args=None, fetch=None, load=None, out=(), drop=(), reuse=None, scratch=None, vmem=5, after=(), late=(), raw=None):
     args, fetch, load, reuse, scratch = args or {}, fetch or {}, load or {}, reuse or {}, scratch or {}
     whole = {key: value for key, value in load.items() if not isinstance(value, tuple)}
     scratch = {**scratch, **{key: pltpu.VMEM(value.shape, value.dtype) for key, value in whole.items()}}
@@ -808,8 +814,9 @@
     operands += [pltpu.with_memory_space_constraint(value, pltpu.HBM) for value in incoming.values()]
     in_names = kept + dropped + list(args) + ["hbm " + key for key in incoming] + ["after%d" % index for index in range(len(after))]
     operands += list(after)
-    in_names += ["hbm " + key for key in parts]
+    in_names += ["hbm " + key for key in parts] + list(raw or {})
     operands += [pltpu.with_memory_space_constraint(value, pltpu.HBM) for value, _ in parts.values()]
+    operands += [pltpu.with_memory_space_constraint(value, pltpu.HBM) for value in (raw or {}).values()]
     shapes = [pltpu.VMEM(pool[key].shape, pool[key].dtype) for key in kept]
     shapes += [pltpu.VMEM(shape, kind) for _, shape, kind in new]
     shapes += [pltpu.VMEM(value.shape, value.dtype) for value in fetch.values()]
@@ -860,7 +867,7 @@
         in_specs=[pl.BlockSpec(memory_space=pltpu.VMEM)] * (len(kept) + len(dropped) + len(args))
         + [pl.BlockSpec(memory_space=pltpu.HBM)] * len(incoming)
         + [pl.BlockSpec(memory_space=pl.ANY)] * len(after)
-        + [pl.BlockSpec(memory_space=pltpu.HBM)] * len(parts),
+        + [pl.BlockSpec(memory_space=pltpu.HBM)] * (len(parts) + len(raw or {})),
         out_specs=[pl.BlockSpec(memory_space=pl.ANY)] * len(kept)
         + [pl.BlockSpec(memory_space=pltpu.VMEM)] * (len(new) + len(fetch))
         + [pl.BlockSpec(memory_space=pltpu.HBM)] * len(out),
@@ -1059,9 +1066,10 @@
     raw = {N.raw_in: gain_in, N.raw_lower: lower, N.raw_fbias: fbias, N.raw_phase: phase, N.raw_out: gain_out, N.raw_ffn: gain_ffn}
     run(
         pool, functools.partial(project_kernel, shape), N.project,
-        new=[(N.vec, (SUB, width), F32), (N.low, (rows, width), BF16), (N.pre, (3 * tiles, rows, LANES), F32), (N.steps, (3 * tiles, rows, LANES), F32),
+        new=[(N.vec, (SUB, width), F32), (N.wmix, w_mix.shape, BF16), (N.low, (rows, width), BF16), (N.pre, (3 * tiles, rows, LANES), F32), (N.decay, (tiles, rows, LANES), F32), (N.adds, (2 * tiles, rows, LANES), F32),
              (N.chunks, (3 * tiles, pad * SUB, LANES), F32), (N.ends, (4 * tiles, pad, LANES), F32)],
-        fetch={N.tok: tokens, N.wmix: w_mix, N.wdown: w_down, N.cot: cotangent}, load=raw, late=(N.wdown, N.cot),
+        fetch={N.tok: tokens, N.wdown: w_down, N.cot: cotangent}, load=raw, late=(N.wdown, N.cot), raw={N.mix: w_mix},
+        scratch={N.own: pltpu.SemaphoreType.DMA((2,))},
     )
 
     def between(hop):
@@ -1081,7 +1089,7 @@
         pool, functools.partial(mix_kernel, shape), N.mix,
         new=[(N.states, (2 * tiles, rows, LANES), F32), (N.entries, (2 * tiles, pad * SUB, LANES), F32),
              (N.mixed, (rows, width), BF16), (N.after, (rows, width), F32), (N.ffn_low, (rows, width), BF16)],
-        fetch={N.wgu: w_gu}, drop=(N.start, N.wout, N.tok, N.steps),
+        fetch={N.wgu: w_gu}, drop=(N.start, N.wout, N.tok, N.decay, N.adds),
     )
     away = (N.after, N.mixed, N.low, N.pre, N.states, N.gate)
     kinds = [(key + N._out, pool[key].shape, pool[key].dtype) for key in away]
@@ -1254,11 +1262,11 @@
     grad_down, grad_wide, grad_out, gate_part = finish(
         functools.partial(unpack_kernel, batch_size // 2), N.unpack, {N.mine: packed, N.got: packed_got},
         [(N.grad_down, (units // seq_size, width)), (N.grad_wide, (final_rows, 2 * units)), (N.grad_out, (final_rows, width)),
-         (N.gate_part, (final_rows, width))],
+         (N.gate_part, (final_rows, width))], local=(N.gate_part,),
     )
     run(
         pool, functools.partial(stack_head_kernel, N.batch, 2, SUB), N.stack_scan,
-        new=[(N.both, (SUB + final_rows, span), F32)], args={N.mine: total, N.got: total_got}, after=(grad_out,),
+        new=[(N.both, (SUB + final_rows, span), F32)], args={N.mine: total, N.got: total_got}, after=(gate_part,),
     )
     total = pool.pop(N.both)
     total_got = across(total, N.batch, 1)
@@ -1278,7 +1286,7 @@
     )
 
 
-def finish(kernel, name, args, outs):
+def finish(kernel, name, args, outs, local=()):
     names = list(args) + [item[0] for item in outs]
 
     def body(*refs):
@@ -1286,7 +1294,9 @@
 
     return pl.pallas_call(
         body,
-        out_shape=[jax.ShapeDtypeStruct(shape, F32) for _, shape in outs],
+        out_shape=[
+            pltpu.VMEM(shape, F32) if key in local else jax.ShapeDtypeStruct(shape, F32) for key, shape in outs
+        ],
         in_specs=[pl.BlockSpec(memory_space=pltpu.VMEM)] * len(args),
         out_specs=[pl.BlockSpec(memory_space=pltpu.VMEM)] * len(outs),
         compiler_params=pltpu.CompilerParams(vmem_limit_bytes=8 * MIB),

time: 180 us -> 176 us (0.978)
  waiting for transfers between devices: 58.6 us -> 51.7 us
  starting transfers between devices: 40.8 us -> 43.5 us
    ppermute x13, waiting for transfers between devices: 46.1 us -> 42.3 us  [across_by_core(): return lax.ppermute(value, (N.seq, N.batch), pairs)]
    ppermute x17, waiting for transfers between devices: 12.5 us -> 9.4 us  [across(): return lax.ppermute(value, axis, [(at, at ^ bit) for at in range(size)])]
  transfers between devices with their start and end apart: 30 -> 30, of which waited for: 18 -> 18; matrix products, arithmetic and copies ran while one was open for 0% -> 0% of each run, Pallas kernels for 30% -> 31%
where the time goes in v3:
time: 176 us; the launch traced here: 175 us
  Pallas kernels  79 us (45%)
  waiting for transfers between devices  51.7 us (29%)
  starting transfers between devices  43.5 us (25%)
    pallas_call x41, Pallas kernels, run(): pl.pallas_call(body, out_shape=shapes, in_specs=[pl.BlockSpec(memory_spac...  76.6 us
    ppermute x13, waiting for transfers between devices, across_by_core(): return lax.ppermute(value, (N.seq, N.batch), pairs)  42.3 us
    ppermute x13, starting transfers between devices, across_by_core(): return lax.ppermute(value, (N.seq, N.batch), pairs)  23.2 us
    ppermute x17, starting transfers between devices, across(): return lax.ppermute(value, axis, [(at, at ^ bit) for at in range(size)])  20.2 us
    ppermute x17, waiting for transfers between devices, across(): return lax.ppermute(value, axis, [(at, at ^ bit) for at in range(size)])  9.4 us
  transfers between devices with their start and end apart: 30, of which 18 were waited for; matrix products, arithmetic and copies ran while one was open for 0% of the time, Pallas kernels for 31%

profile of v3, /device:TPU:0, one launch (start us, length us, event | category | flops | bytes accessed | tf_op | source)
XLA Modules:
  0.0 175.2 jit_solution(9510608628448260099)
XLA Ops:
  0.6 7.1 %project.1 = (f32[8,768]{1,0:T(8,128)S(1)}, bf16[768,1920]{1,0:T(8,128)(2,1)S(1)}, bf16[1008,768]{1,0:T(8,128)(2,1)S(1)}, f32[9,1008,128]{2,1,0:T(8,128)S(1)}, f...) custom-call(bf16[1008,768]{1,0:T(8,128)(2,1)} %bitcast.4, ...), custom_call_target="tpu_custom_call" | custom-call | flops 1840000000 | tf_op jit(solution)/shard_map/project/pallas_call | solution.py:864
  7.7 3.0 %collective-permute-start = (f32[12,8,128]{2,1,0:T(8,128)S(1)}, f32[12,8,128]{2,1,0:T(8,128)S(1)}, u32[]{:S(2)}, u32[]{:S(2)}) collective-permute-start(f32[12,8,128]{2,1,0:T(8,128)S(1)} %get-tuple-element.414.refs_12_), channel_id=1, source_target_pairs={{0,4},{4,0},{8,12},{12,8},{16,20},{20,16},{24,28},{28,24},{1,5},{5... | collective-permute-start | bytes 147464 | tf_op jit(solution)/shard_map/ppermute | solution.py:898
  10.8 1.8 %gate.1 = (f32[8,768]{1,0:T(8,128)S(1)}, bf16[1008,768]{1,0:T(8,128)(2,1)S(1)}, f32[9,1008,128]{2,1,0:T(8,128)S(1)}, f32[3,1008,128]{2,1,0:T(8,128)S(1)}, f32[6,...) custom-call(f32[8,768]{1,0:T(8,128)S(1)} %get-tuple-element.393.refs, ...), custom_call_target="tpu_custom_call", output_to_operand_aliasing={{0}: (0, {}), {1}: (1, {}), {2}: (2, {}), {3}: (3, {}), {4}... | custom-call | flops 414000000 | tf_op jit(solution)/shard_map/gate/pallas_call | solution.py:864
  12.9 2.1 %collective-permute-start.1 = (f32[12,8,128]{2,1,0:T(8,128)S(1)}, f32[12,8,128]{2,1,0:T(8,128)S(1)}, u32[]{:S(2)}, u32[]{:S(2)}) collective-permute-start(f32[12,8,128]{2,1,0:T(8,128)S(1)} %get-tuple-element.440.refs_14_), channel_id=1, source_target_pairs={{0,8},{4,12},{8,0},{12,4},{16,24},{20,28},{24,16},{28,20},{1,9},{5... | collective-permute-start | bytes 147464 | tf_op jit(solution)/shard_map/ppermute | solution.py:898
  15.1 1.9 %hidden_back.2 = (f32[8,768]{1,0:T(8,128)S(1)}, bf16[1008,768]{1,0:T(8,128)(2,1)S(1)}, f32[9,1008,128]{2,1,0:T(8,128)S(1)}, f32[3,1008,128]{2,1,0:T(8,128)S(1)},...) custom-call(f32[8,768]{1,0:T(8,128)S(1)} %get-tuple-element.415.refs, ...), custom_call_target="tpu_custom_call", output_to_operand_aliasing={{0}: (0, {}), {1}: (1, {}), {2}: (2, {}), {3}: (3, {}), {4}... | custom-call | flops 437000000 | tf_op jit(solution)/shard_map/hidden_back/pallas_call | solution.py:864
  17.2 3.1 %collective-permute-start.2 = (f32[12,8,128]{2,1,0:T(8,128)S(1)}, f32[12,8,128]{2,1,0:T(8,128)S(1)}, u32[]{:S(2)}, u32[]{:S(2)}) collective-permute-start(f32[12,8,128]{2,1,0:T(8,128)S(1)} %get-tuple-element.467.refs_14_), channel_id=1, source_target_pairs={{0,16},{4,20},{8,24},{12,28},{16,0},{20,4},{24,8},{28,12},{1,17},{... | collective-permute-start | bytes 147464 | tf_op jit(solution)/shard_map/ppermute | solution.py:898
  20.3 1.9 %hidden_back.3 = (f32[8,768]{1,0:T(8,128)S(1)}, bf16[1008,768]{1,0:T(8,128)(2,1)S(1)}, f32[9,1008,128]{2,1,0:T(8,128)S(1)}, f32[3,1008,128]{2,1,0:T(8,128)S(1)},...) custom-call(f32[8,768]{1,0:T(8,128)S(1)} %get-tuple-element.441.refs, ...), custom_call_target="tpu_custom_call", output_to_operand_aliasing={{0}: (0, {}), {1}: (1, {}), {2}: (2, {}), {3}: (3, {}), {4}... | custom-call | flops 437000000 | tf_op jit(solution)/shard_map/hidden_back/pallas_call | solution.py:864
  22.5 4.9 %mix.1 = (f32[8,768]{1,0:T(8,128)S(1)}, bf16[1008,768]{1,0:T(8,128)(2,1)S(1)}, f32[9,1008,128]{2,1,0:T(8,128)S(1)}, f32[9,64,128]{2,1,0:T(8,128)S(1)}, bf16[1008...) custom-call(f32[8,768]{1,0:T(8,128)S(1)} %get-tuple-element.468.refs, ...), custom_call_target="tpu_custom_call", output_to_operand_aliasing={{0}: (0, {}), {1}: (1, {}), {2}: (2, {}), {3}: (3, {}), {4}... | custom-call | flops 1356999936 | tf_op jit(solution)/shard_map/mix/pallas_call | solution.py:864
  27.4 7.3 %ffn.1 = (f32[8,768]{1,0:T(8,128)S(1)}, f32[9,64,128]{2,1,0:T(8,128)S(1)}, bf16[1008,768]{1,0:T(8,128)(2,1)S(1)}, f32[6,64,128]{2,1,0:T(8,128)S(1)}, f32[1008,76...) custom-call(f32[8,768]{1,0:T(8,128)S(1)} %get-tuple-element.481.refs, ...), custom_call_target="tpu_custom_call", output_to_operand_aliasing={{0}: (0, {}), {1}: (1, {}), {2}: (2, {}), {3}: (3, {}), {4}... | custom-call | flops 1679000064 | tf_op jit(solution)/shard_map/ffn/pallas_call | solution.py:864
  34.7 3.1 %grad_gu.2 = (f32[8,768]{1,0:T(8,128)S(1)}, f32[9,64,128]{2,1,0:T(8,128)S(1)}, bf16[1008,768]{1,0:T(8,128)(2,1)S(1)}, f32[6,64,128]{2,1,0:T(8,128)S(1)}, f32[100...) custom-call(f32[8,768]{1,0:T(8,128)S(1)} %get-tuple-element.496.refs, ...), custom_call_target="tpu_custom_call", output_to_operand_aliasing={{0}: (0, {}), {1}: (1, {}), {2}: (2, {}), {3}: (3, {}), {4}... | custom-call | flops 736000000 | tf_op jit(solution)/shard_map/grad_gu/pallas_call | solution.py:864
  37.9 3.2 %grad_gu.3 = (f32[8,768]{1,0:T(8,128)S(1)}, f32[9,64,128]{2,1,0:T(8,128)S(1)}, bf16[1008,768]{1,0:T(8,128)(2,1)S(1)}, f32[6,64,128]{2,1,0:T(8,128)S(1)}, f32[100...) custom-call(f32[8,768]{1,0:T(8,128)S(1)} %get-tuple-element.505.refs, ...), custom_call_target="tpu_custom_call", output_to_operand_aliasing={{0}: (0, {}), {1}: (1, {}), {2}: (2, {}), {3}: (3, {}), {4}... | custom-call | flops 736000000 | tf_op jit(solution)/shard_map/grad_gu/pallas_call | solution.py:864
  41.1 5.4 %grad_down.1 = (f32[8,768]{1,0:T(8,128)S(1)}, f32[9,64,128]{2,1,0:T(8,128)S(1)}, bf16[1008,768]{1,0:T(8,128)(2,1)S(1)}, f32[6,64,128]{2,1,0:T(8,128)S(1)}, f32[1...) custom-call(f32[8,768]{1,0:T(8,128)S(1)} %get-tuple-element.514.refs, ...), custom_call_target="tpu_custom_call", output_to_operand_aliasing={{0}: (0, {}), {1}: (1, {}), {2}: (2, {}), {3}: (3, {}), {4}... | custom-call | flops 828000000 | tf_op jit(solution)/shard_map/grad_down/pallas_call | solution.py:864
  47.7 1.9 %collective-permute-start.6 = (f32[384,1536]{1,0:T(8,128)S(1)}, f32[384,1536]{1,0:T(8,128)S(1)}, u32[]{:S(2)}, u32[]{:S(2)}) collective-permute-start(f32[384,1536]{1,0:T(8,128)S(1)} %get-tuple-element.637), channel_id=1, source_target_pairs={{0,2},{1,5},{2,0},{3,7},{4,6},{5,1},{6,4},{7,3},{8,10},{9,13},{10,... | collective-permute-start | bytes 7077896 | tf_op jit(solution)/shard_map/ppermute | solution.py:909
  49.6 6.4 %ffn_back.1 = (f32[8,768]{1,0:T(8,128)S(1)}, f32[9,64,128]{2,1,0:T(8,128)S(1)}, f32[6,64,128]{2,1,0:T(8,128)S(1)}, f32[1536,384]{1,0:T(8,128)S(1)}, f32[384,1536...) custom-call(f32[8,768]{1,0:T(8,128)S(1)} %get-tuple-element.535.refs, ...), custom_call_target="tpu_custom_call", output_to_operand_aliasing={{0}: (0, {}), {1}: (1, {}), {2}: (2, {}), {3}: (3, {}), {4}... | custom-call | flops 1495000064 | tf_op jit(solution)/shard_map/ffn_back/pallas_call | solution.py:864
  56.3 7.1 %mix_back.1 = (f32[8,768]{1,0:T(8,128)S(1)}, f32[9,64,128]{2,1,0:T(8,128)S(1)}, f32[6,64,128]{2,1,0:T(8,128)S(1)}, f32[384,1536]{1,0:T(8,128)S(1)}, f32[1008,768...) custom-call(f32[8,768]{1,0:T(8,128)S(1)} %get-tuple-element.560.refs, ...), custom_call_target="tpu_custom_call", output_to_operand_aliasing={{0}: (0, {}), {1}: (1, {}), {2}: (2, {}), {3}: (3, {}), {4}... | custom-call | flops 1610000000 | tf_op jit(solution)/shard_map/mix_back/pallas_call | solution.py:864
  63.4 2.7 %collective-permute-start.5 = (f32[1,9,8,128]{3,2,1,0:T(8,128)S(1)}, f32[1,9,8,128]{3,2,1,0:T(8,128)S(1)}, u32[]{:S(2)}, u32[]{:S(2)}) collective-permute-start(f32[1,9,8,128]{3,2,1,0:T(8,128)S(1)} %get-tuple-element.605.refs_15_), channel_id=1, source_target_pairs={{0,16},{4,20},{8,24},{12,28},{16,0},{20,4},{24,8},{28,12},{1,17},{... | collective-permute-start | bytes 110600 | tf_op jit(solution)/shard_map/ppermute | solution.py:898
  66.1 1.5 grad_out.1
  68.8 1.6 grad_gate.1
  71.9 4.7 %collective-permute-done.6.refs_16_ = f32[384,1536]{1,0:T(8,128)S(1)} collective-permute-done((f32[384,1536]{1,0:T(8,128)S(1)}, f32[384,1536]{1,0:T(8,128)S(1)}, u32[]{:S(2)}, u32[]{:S(2)}) %collective-permute-start.6) | collective-permute-done | bytes 2359328 | tf_op jit(solution)/shard_map/ppermute | solution.py:909
  77.1 1.9 %collective-permute-start.8 = (f32[4,9,8,128]{3,2,1,0:T(8,128)S(1)}, f32[4,9,8,128]{3,2,1,0:T(8,128)S(1)}, u32[]{:S(2)}, u32[]{:S(2)}) collective-permute-start(f32[4,9,8,128]{3,2,1,0:T(8,128)S(1)} %get-tuple-element.671.refs_16_), channel_id=1, source_target_pairs={{0,4},{4,0},{8,12},{12,8},{16,20},{20,16},{24,28},{28,24},{1,5},{5... | collective-permute-start | bytes 442376 | tf_op jit(solution)/shard_map/ppermute | solution.py:898
  79.2 3.1 %collective-permute-done.8.refs_17_ = f32[4,9,8,128]{3,2,1,0:T(8,128)S(1)} collective-permute-done((f32[4,9,8,128]{3,2,1,0:T(8,128)S(1)}, f32[4,9,8,128]{3,2,1,0:T(8,128)S(1)}, u32[]{:S(2)}, u32[]{:S(2)}) %collective-permute-start.8) | collective-permute-done | bytes 147488 | tf_op jit(solution)/shard_map/ppermute | solution.py:898
  82.4 4.0 %scan_back.1 = (f32[8,768]{1,0:T(8,128)S(1)}, f32[1008,768]{1,0:T(8,128)S(1)}, f32[8,768]{1,0:T(8,128)S(1)}, f32[768,384]{1,0:T(8,128)S(1)}, bf16[1008,768]{1,0:...) custom-call(f32[8,768]{1,0:T(8,128)S(1)} %get-tuple-element.672.refs, ...), custom_call_target="tpu_custom_call", output_to_operand_aliasing={{0}: (0, {}), {1}: (1, {}), {2}: (2, {}), {3}: (3, {}), {4}... | custom-call | flops 920000000 | tf_op jit(solution)/shard_map/scan_back/pallas_call | solution.py:864
  86.8 1.9 %collective-permute-start.16 = (f32[384,768]{1,0:T(8,128)S(1)}, f32[384,768]{1,0:T(8,128)S(1)}, u32[]{:S(2)}, u32[]{:S(2)}) collective-permute-start(f32[384,768]{1,0:T(8,128)S(1)} %get-tuple-element.742), channel_id=1, source_target_pairs={{0,4},{1,3},{2,6},{3,1},{4,0},{5,7},{6,2},{7,5},{8,12},{9,11},{10,... | collective-permute-start | bytes 3538952 | tf_op jit(solution)/shard_map/ppermute | solution.py:909
  88.8 1.6 collective-permute-start.11
  90.3 5.6 %input_back.1 = (f32[8,768]{1,0:T(8,128)S(1)}, f32[8,768]{1,0:T(8,128)S(1)}, f32[768,384]{1,0:T(8,128)S(1)}, f32[8,768]{1,0:T(8,128)S(1)}, bf16[1008,768]{1,0:T(...) custom-call(f32[8,768]{1,0:T(8,128)S(1)} %get-tuple-element.706.refs, ...), custom_call_target="tpu_custom_call", output_to_operand_aliasing={{0}: (0, {}), {1}: (1, {}), {2}: (2, {}), {3}: (3, {}), {4}... | custom-call | flops 1288000000 | tf_op jit(solution)/shard_map/input_back/pallas_call | solution.py:864
  96.0 2.5 %grad_scan.1 = (f32[8,768]{1,0:T(8,128)S(1)}, f32[768,384]{1,0:T(8,128)S(1)}, f32[192,1536]{1,0:T(8,128)S(1)}, f32[384,768]{1,0:T(8,128)S(1)}, f32[776,640]{1,0:...) custom-call(f32[8,768]{1,0:T(8,128)S(1)} %get-tuple-element.721.refs, ...), custom_call_target="tpu_custom_call", output_to_operand_aliasing={{0}: (0, {}), {1}: (1, {}), {2}: (2, {}), {3}: (3, {})} | custom-call | flops 552000000 | tf_op jit(solution)/shard_map/grad_scan/pallas_call | solution.py:864
  99.0 8.8 %collective-permute-done.16.refs_3_ = f32[384,768]{1,0:T(8,128)S(1)} collective-permute-done((f32[384,768]{1,0:T(8,128)S(1)}, f32[384,768]{1,0:T(8,128)S(1)}, u32[]{:S(2)}, u32[]{:S(2)}) %collective-permute-start.16) | collective-permute-done | bytes 1179680 | tf_op jit(solution)/shard_map/ppermute | solution.py:909
  108.2 1.6 collective-permute-start.21
  109.9 6.3 %collective-permute-done.11.refs_1_ = f32[192,1536]{1,0:T(8,128)S(1)} collective-permute-done((f32[192,1536]{1,0:T(8,128)S(1)}, f32[192,1536]{1,0:T(8,128)S(1)}, u32[]{:S(2)}, u32[]{:S(2)}) %collective-permute-start.11) | collective-permute-done | bytes 1179680 | tf_op jit(solution)/shard_map/ppermute | solution.py:909
  116.7 1.5 collective-permute-start.17
  118.8 5.7 %collective-permute-done.21.refs_1_ = f32[384,768]{1,0:T(8,128)S(1)} collective-permute-done((f32[384,768]{1,0:T(8,128)S(1)}, f32[384,768]{1,0:T(8,128)S(1)}, u32[]{:S(2)}, u32[]{:S(2)}) %collective-permute-start.21) | collective-permute-done | bytes 1179680 | tf_op jit(solution)/shard_map/ppermute | solution.py:909
  124.7 1.7 collective-permute-start.22
  126.4 6.6 %output.1 = (f32[8,128]{1,0:T(8,128)S(1)}, bf16[1008,768]{1,0:T(8,128)(2,1)}) custom-call(bf16[1536,768]{1,0:T(8,128)(2,1)} %refs_0_.1, f32[1008,768]{1,0:T(8,128)} %get-tuple-element.495.refs_1_, bf16[1008,1536]{1,0:T(8,128)(2,1)} %get-tuple-element.523.refs_2_), custom_call_target="tpu_custom_call" | custom-call | flops 1610000000 | tf_op jit(solution)/shard_map/output/pallas_call | solution.py:864
  133.0 2.3 %collective-permute-done.17.refs_1_ = f32[392,640]{1,0:T(8,128)S(1)} collective-permute-done((f32[392,640]{1,0:T(8,128)S(1)}, f32[392,640]{1,0:T(8,128)S(1)}, u32[]{:S(2)}, u32[]{:S(2)}) %collective-permute-start.17) | collective-permute-done | bytes 1003552 | tf_op jit(solution)/shard_map/ppermute | solution.py:909
  135.5 1.7 collective-permute-start.19
  137.3 2.7 %collective-permute-start.18 = (f32[48,1536]{1,0:T(8,128)S(1)}, f32[48,1536]{1,0:T(8,128)S(1)}, u32[]{:S(2)}, u32[]{:S(2)}) collective-permute-start(f32[48,1536]{1,0:T(8,128)S(1)} %get-tuple-element.749), channel_id=1, source_target_pairs={{0,16},{1,3},{2,18},{3,1},{4,20},{5,7},{6,22},{7,5},{8,24},{9,11},... | collective-permute-start | bytes 884744 | tf_op jit(solution)/shard_map/ppermute | solution.py:909
  140.1 2.8 %collective-permute-start.23 = (f32[96,768]{1,0:T(8,128)S(1)}, f32[96,768]{1,0:T(8,128)S(1)}, u32[]{:S(2)}, u32[]{:S(2)}) collective-permute-start(f32[96,768]{1,0:T(8,128)S(1)} %get-tuple-element.756), channel_id=1, source_target_pairs={{0,16},{1,9},{2,18},{3,11},{4,20},{5,13},{6,22},{7,15},{8,24},{9,1... | collective-permute-start | bytes 884744 | tf_op jit(solution)/shard_map/ppermute | solution.py:909
  143.0 1.6 collective-permute-done.19.refs_1_
  144.7 2.8 %collective-permute-start.25 = (f32[104,640]{1,0:T(8,128)S(1)}, f32[104,640]{1,0:T(8,128)S(1)}, u32[]{:S(2)}, u32[]{:S(2)}) collective-permute-start(f32[104,640]{1,0:T(8,128)S(1)} %get-tuple-element.757), channel_id=1, source_target_pairs={{0,16},{1,9},{2,18},{3,11},{4,20},{5,13},{6,22},{7,15},{8,24},{9,1... | collective-permute-start | bytes 798728 | tf_op jit(solution)/shard_map/ppermute | solution.py:909
  147.5 2.4 %collective-permute-done.18.refs_1_ = f32[48,1536]{1,0:T(8,128)S(1)} collective-permute-done((f32[48,1536]{1,0:T(8,128)S(1)}, f32[48,1536]{1,0:T(8,128)S(1)}, u32[]{:S(2)}, u32[]{:S(2)}) %collective-permute-start.18) | collective-permute-done | bytes 294944 | tf_op jit(solution)/shard_map/ppermute | solution.py:909
  150.0 1.5 collective-permute-start.20
  151.5 5.0 %collective-permute-done.23.refs_1_ = f32[96,768]{1,0:T(8,128)S(1)} collective-permute-done((f32[96,768]{1,0:T(8,128)S(1)}, f32[96,768]{1,0:T(8,128)S(1)}, u32[]{:S(2)}, u32[]{:S(2)}) %collective-permute-start.23) | collective-permute-done | bytes 294944 | tf_op jit(solution)/shard_map/ppermute | solution.py:909
  158.1 2.3 %collective-permute-done.25.refs_1_ = f32[104,640]{1,0:T(8,128)S(1)} collective-permute-done((f32[104,640]{1,0:T(8,128)S(1)}, f32[104,640]{1,0:T(8,128)S(1)}, u32[]{:S(2)}, u32[]{:S(2)}) %collective-permute-start.25) | collective-permute-done | bytes 266272 | tf_op jit(solution)/shard_map/ppermute | solution.py:909
  160.6 2.3 %collective-permute-start.26 = (f32[56,640]{1,0:T(8,128)S(1)}, f32[56,640]{1,0:T(8,128)S(1)}, u32[]{:S(2)}, u32[]{:S(2)}) collective-permute-start(f32[56,640]{1,0:T(8,128)S(1)} %get-tuple-element.759), channel_id=1, source_target_pairs={{0,8},{1,17},{2,10},{3,19},{4,12},{5,21},{6,14},{7,23},{8,0},{9,25... | collective-permute-start | bytes 430088 | tf_op jit(solution)/shard_map/ppermute | solution.py:909
  162.9 3.1 %collective-permute-done.26.refs_1_ = f32[56,640]{1,0:T(8,128)S(1)} collective-permute-done((f32[56,640]{1,0:T(8,128)S(1)}, f32[56,640]{1,0:T(8,128)S(1)}, u32[]{:S(2)}, u32[]{:S(2)}) %collective-permute-start.26) | collective-permute-done | bytes 143392 | tf_op jit(solution)/shard_map/ppermute | solution.py:909
  166.4 1.5 collective-permute-start.27
  170.7 1.9 %collective-permute-done.27.refs_2_ = f32[56,640]{1,0:T(8,128)S(1)} collective-permute-done((f32[56,640]{1,0:T(8,128)S(1)}, f32[56,640]{1,0:T(8,128)S(1)}, u32[]{:S(2)}, u32[]{:S(2)}) %collective-permute-start.27) | collective-permute-done | bytes 143392 | tf_op jit(solution)/shard_map/ppermute | solution.py:898
  172.8 1.5 collective-permute-done.29.refs_1_
  (55 shorter events, 15.0 us)
Async XLA Ops:
  7.7 5.1 %collective-permute-start = (f32[12,8,128]{2,1,0:T(8,128)S(1)}, f32[12,8,128]{2,1,0:T(8,128)S(1)}, u32[]{:S(2)}, u32[]{:S(2)}) collective-permute-start(f32[12,8,128]{2,1,0:T(8,128)S(1)} %get-tuple-element.414.refs_12_), channel_id=1, source_target_pairs={{0,4},{4,0},{8,12},{12,8},{16,20},{20,16},{24,28},{28,24},{1,5},{5... | collective-permute-start | bytes 147464 | tf_op jit(solution)/shard_map/ppermute | solution.py:898
  12.9 4.2 %collective-permute-start.1 = (f32[12,8,128]{2,1,0:T(8,128)S(1)}, f32[12,8,128]{2,1,0:T(8,128)S(1)}, u32[]{:S(2)}, u32[]{:S(2)}) collective-permute-start(f32[12,8,128]{2,1,0:T(8,128)S(1)} %get-tuple-element.440.refs_14_), channel_id=1, source_target_pairs={{0,8},{4,12},{8,0},{12,4},{16,24},{20,28},{24,16},{28,20},{1,9},{5... | collective-permute-start | bytes 147464 | tf_op jit(solution)/shard_map/ppermute | solution.py:898
  17.2 5.2 %collective-permute-start.2 = (f32[12,8,128]{2,1,0:T(8,128)S(1)}, f32[12,8,128]{2,1,0:T(8,128)S(1)}, u32[]{:S(2)}, u32[]{:S(2)}) collective-permute-start(f32[12,8,128]{2,1,0:T(8,128)S(1)} %get-tuple-element.467.refs_14_), channel_id=1, source_target_pairs={{0,16},{4,20},{8,24},{12,28},{16,0},{20,4},{24,8},{28,12},{1,17},{... | collective-permute-start | bytes 147464 | tf_op jit(solution)/shard_map/ppermute | solution.py:898
  37.8 9.2 %collective-permute-start.3 = (f32[768,1536]{1,0:T(8,128)S(1)}, f32[768,1536]{1,0:T(8,128)S(1)}, u32[]{:S(2)}, u32[]{:S(2)}) collective-permute-start(f32[768,1536]{1,0:T(8,128)S(1)} %get-tuple-element.534), channel_id=1, source_target_pairs={{0,1},{1,0},{2,3},{3,2},{4,5},{5,4},{6,7},{7,6},{8,9},{9,8},{10,11... | collective-permute-start | bytes 14155784 | tf_op jit(solution)/shard_map/ppermute | solution.py:898
  46.5 9.5 %collective-permute-start.4 = (f32[1536,384]{1,0:T(8,128)}, f32[1536,384]{1,0:T(8,128)S(1)}, u32[]{:S(2)}, u32[]{:S(2)}) collective-permute-start(f32[1536,384]{1,0:T(8,128)} %get-tuple-element.559), channel_id=1, source_target_pairs={{0,1},{1,0},{2,3},{3,2},{4,5},{5,4},{6,7},{7,6},{8,9},{9,8},{10,11... | collective-permute-start | bytes 7077896 | tf_op jit(solution)/shard_map/ppermute | solution.py:898
  47.7 28.9 %collective-permute-start.6 = (f32[384,1536]{1,0:T(8,128)S(1)}, f32[384,1536]{1,0:T(8,128)S(1)}, u32[]{:S(2)}, u32[]{:S(2)}) collective-permute-start(f32[384,1536]{1,0:T(8,128)S(1)} %get-tuple-element.637), channel_id=1, source_target_pairs={{0,2},{1,5},{2,0},{3,7},{4,6},{5,1},{6,4},{7,3},{8,10},{9,13},{10,... | collective-permute-start | bytes 7077896 | tf_op jit(solution)/shard_map/ppermute | solution.py:909
  63.4 5.3 %collective-permute-start.5 = (f32[1,9,8,128]{3,2,1,0:T(8,128)S(1)}, f32[1,9,8,128]{3,2,1,0:T(8,128)S(1)}, u32[]{:S(2)}, u32[]{:S(2)}) collective-permute-start(f32[1,9,8,128]{3,2,1,0:T(8,128)S(1)} %get-tuple-element.605.refs_15_), channel_id=1, source_target_pairs={{0,16},{4,20},{8,24},{12,28},{16,0},{20,4},{24,8},{28,12},{1,17},{... | collective-permute-start | bytes 110600 | tf_op jit(solution)/shard_map/ppermute | solution.py:898
  67.7 18.7 %collective-permute-start.9 = (f32[768,384]{1,0:T(8,128)S(1)}, f32[768,384]{1,0:T(8,128)S(1)}, u32[]{:S(2)}, u32[]{:S(2)}) collective-permute-start(f32[768,384]{1,0:T(8,128)S(1)} %get-tuple-element.704), channel_id=1, source_target_pairs={{0,1},{1,0},{2,3},{3,2},{4,5},{5,4},{6,7},{7,6},{8,9},{9,8},{10,11... | collective-permute-start | bytes 3538952 | tf_op jit(solution)/shard_map/ppermute | solution.py:898
  70.4 16.0 %collective-permute-start.10 = (f32[768,384]{1,0:T(8,128)S(1)}, f32[768,384]{1,0:T(8,128)S(1)}, u32[]{:S(2)}, u32[]{:S(2)}) collective-permute-start(f32[768,384]{1,0:T(8,128)S(1)} %get-tuple-element.705), channel_id=1, source_target_pairs={{0,1},{1,0},{2,3},{3,2},{4,5},{5,4},{6,7},{7,6},{8,9},{9,8},{10,11... | collective-permute-start | bytes 3538952 | tf_op jit(solution)/shard_map/ppermute | solution.py:898
  70.5 6.5 %collective-permute-start.7 = (f32[2,9,8,128]{3,2,1,0:T(8,128)S(1)}, f32[2,9,8,128]{3,2,1,0:T(8,128)S(1)}, u32[]{:S(2)}, u32[]{:S(2)}) collective-permute-start(f32[2,9,8,128]{3,2,1,0:T(8,128)S(1)} %get-tuple-element.654.refs_16_), channel_id=1, source_target_pairs={{0,8},{4,12},{8,0},{12,4},{16,24},{20,28},{24,16},{28,20},{1,9},{5... | collective-permute-start | bytes 221192 | tf_op jit(solution)/shard_map/ppermute | solution.py:898
  77.1 5.2 %collective-permute-start.8 = (f32[4,9,8,128]{3,2,1,0:T(8,128)S(1)}, f32[4,9,8,128]{3,2,1,0:T(8,128)S(1)}, u32[]{:S(2)}, u32[]{:S(2)}) collective-permute-start(f32[4,9,8,128]{3,2,1,0:T(8,128)S(1)} %get-tuple-element.671.refs_16_), channel_id=1, source_target_pairs={{0,4},{4,0},{8,12},{12,8},{16,20},{20,16},{24,28},{28,24},{1,5},{5... | collective-permute-start | bytes 442376 | tf_op jit(solution)/shard_map/ppermute | solution.py:898
  79.0 20.0 %collective-permute-start.15 = (f32[768,384]{1,0:T(8,128)S(1)}, f32[768,384]{1,0:T(8,128)S(1)}, u32[]{:S(2)}, u32[]{:S(2)}) collective-permute-start(f32[768,384]{1,0:T(8,128)S(1)} %get-tuple-element.741), channel_id=1, source_target_pairs={{0,4},{1,3},{2,6},{3,1},{4,0},{5,7},{6,2},{7,5},{8,12},{9,11},{10,... | collective-permute-start | bytes 3538952 | tf_op jit(solution)/shard_map/ppermute | solution.py:909
  86.8 21.0 %collective-permute-start.16 = (f32[384,768]{1,0:T(8,128)S(1)}, f32[384,768]{1,0:T(8,128)S(1)}, u32[]{:S(2)}, u32[]{:S(2)}) collective-permute-start(f32[384,768]{1,0:T(8,128)S(1)} %get-tuple-element.742), channel_id=1, source_target_pairs={{0,4},{1,3},{2,6},{3,1},{4,0},{5,7},{6,2},{7,5},{8,12},{9,11},{10,... | collective-permute-start | bytes 3538952 | tf_op jit(solution)/shard_map/ppermute | solution.py:909
  88.8 27.4 %collective-permute-start.11 = (f32[192,1536]{1,0:T(8,128)S(1)}, f32[192,1536]{1,0:T(8,128)S(1)}, u32[]{:S(2)}, u32[]{:S(2)}) collective-permute-start(f32[192,1536]{1,0:T(8,128)S(1)} %get-tuple-element.733), channel_id=1, source_target_pairs={{0,8},{1,17},{2,10},{3,19},{4,12},{5,21},{6,14},{7,23},{8,0},{9,25... | collective-permute-start | bytes 3538952 | tf_op jit(solution)/shard_map/ppermute | solution.py:909
  98.5 17.9 %collective-permute-start.13 = (f32[392,640]{1,0:T(8,128)S(1)}, f32[392,640]{1,0:T(8,128)S(1)}, u32[]{:S(2)}, u32[]{:S(2)}) collective-permute-start(f32[392,640]{1,0:T(8,128)S(1)} %get-tuple-element.737), channel_id=1, source_target_pairs={{0,1},{1,0},{2,3},{3,2},{4,5},{5,4},{6,7},{7,6},{8,9},{9,8},{10,11... | collective-permute-start | bytes 3010568 | tf_op jit(solution)/shard_map/ppermute | solution.py:898
  98.5 17.8 %collective-permute-start.14 = (f32[384,640]{1,0:T(8,128)S(1)}, f32[384,640]{1,0:T(8,128)S(1)}, u32[]{:S(2)}, u32[]{:S(2)}) collective-permute-start(f32[384,640]{1,0:T(8,128)S(1)} %get-tuple-element.738), channel_id=1, source_target_pairs={{0,1},{1,0},{2,3},{3,2},{4,5},{5,4},{6,7},{7,6},{8,9},{9,8},{10,11... | collective-permute-start | bytes 2949128 | tf_op jit(solution)/shard_map/ppermute | solution.py:898
  108.2 16.3 %collective-permute-start.21 = (f32[384,768]{1,0:T(8,128)S(1)}, f32[384,768]{1,0:T(8,128)S(1)}, u32[]{:S(2)}, u32[]{:S(2)}) collective-permute-start(f32[384,768]{1,0:T(8,128)S(1)} %get-tuple-element.752), channel_id=1, source_target_pairs={{0,2},{1,5},{2,0},{3,7},{4,6},{5,1},{6,4},{7,3},{8,10},{9,13},{10,... | collective-permute-start | bytes 3538952 | tf_op jit(solution)/shard_map/ppermute | solution.py:909
  116.7 18.5 %collective-permute-start.17 = (f32[392,640]{1,0:T(8,128)S(1)}, f32[392,640]{1,0:T(8,128)S(1)}, u32[]{:S(2)}, u32[]{:S(2)}) collective-permute-start(f32[392,640]{1,0:T(8,128)S(1)} %get-tuple-element.745), channel_id=1, source_target_pairs={{0,2},{1,5},{2,0},{3,7},{4,6},{5,1},{6,4},{7,3},{8,10},{9,13},{10,... | collective-permute-start | bytes 3010568 | tf_op jit(solution)/shard_map/ppermute | solution.py:909
  118.2 18.9 %collective-permute-start.12 = (f32[96,1536]{1,0:T(8,128)S(1)}, f32[96,1536]{1,0:T(8,128)S(1)}, u32[]{:S(2)}, u32[]{:S(2)}) collective-permute-start(f32[96,1536]{1,0:T(8,128)S(1)} %get-tuple-element.735), channel_id=1, source_target_pairs={{0,4},{1,9},{2,6},{3,11},{4,0},{5,13},{6,2},{7,15},{8,12},{9,1},{1... | collective-permute-start | bytes 1769480 | tf_op jit(solution)/shard_map/ppermute | solution.py:909
  124.7 15.3 %collective-permute-start.22 = (f32[192,768]{1,0:T(8,128)S(1)}, f32[192,768]{1,0:T(8,128)S(1)}, u32[]{:S(2)}, u32[]{:S(2)}) collective-permute-start(f32[192,768]{1,0:T(8,128)S(1)} %get-tuple-element.754), channel_id=1, source_target_pairs={{0,8},{1,17},{2,10},{3,19},{4,12},{5,21},{6,14},{7,23},{8,0},{9,25... | collective-permute-start | bytes 1769480 | tf_op jit(solution)/shard_map/ppermute | solution.py:909
  135.5 9.1 %collective-permute-start.19 = (f32[200,640]{1,0:T(8,128)S(1)}, f32[200,640]{1,0:T(8,128)S(1)}, u32[]{:S(2)}, u32[]{:S(2)}) collective-permute-start(f32[200,640]{1,0:T(8,128)S(1)} %get-tuple-element.750), channel_id=1, source_target_pairs={{0,4},{1,3},{2,6},{3,1},{4,0},{5,7},{6,2},{7,5},{8,12},{9,11},{10,... | collective-permute-start | bytes 1536008 | tf_op jit(solution)/shard_map/ppermute | solution.py:909
  137.3 12.6 %collective-permute-start.18 = (f32[48,1536]{1,0:T(8,128)S(1)}, f32[48,1536]{1,0:T(8,128)S(1)}, u32[]{:S(2)}, u32[]{:S(2)}) collective-permute-start(f32[48,1536]{1,0:T(8,128)S(1)} %get-tuple-element.749), channel_id=1, source_target_pairs={{0,16},{1,3},{2,18},{3,1},{4,20},{5,7},{6,22},{7,5},{8,24},{9,11},... | collective-permute-start | bytes 884744 | tf_op jit(solution)/shard_map/ppermute | solution.py:909
  140.1 16.4 %collective-permute-start.23 = (f32[96,768]{1,0:T(8,128)S(1)}, f32[96,768]{1,0:T(8,128)S(1)}, u32[]{:S(2)}, u32[]{:S(2)}) collective-permute-start(f32[96,768]{1,0:T(8,128)S(1)} %get-tuple-element.756), channel_id=1, source_target_pairs={{0,16},{1,9},{2,18},{3,11},{4,20},{5,13},{6,22},{7,15},{8,24},{9,1... | collective-permute-start | bytes 884744 | tf_op jit(solution)/shard_map/ppermute | solution.py:909
  144.7 15.7 %collective-permute-start.25 = (f32[104,640]{1,0:T(8,128)S(1)}, f32[104,640]{1,0:T(8,128)S(1)}, u32[]{:S(2)}, u32[]{:S(2)}) collective-permute-start(f32[104,640]{1,0:T(8,128)S(1)} %get-tuple-element.757), channel_id=1, source_target_pairs={{0,16},{1,9},{2,18},{3,11},{4,20},{5,13},{6,22},{7,15},{8,24},{9,1... | collective-permute-start | bytes 798728 | tf_op jit(solution)/shard_map/ppermute | solution.py:909
  150.0 16.1 %collective-permute-start.20 = (f32[48,1536]{1,0:T(8,128)S(1)}, f32[48,1536]{1,0:T(8,128)S(1)}, u32[]{:S(2)}, u32[]{:S(2)}) collective-permute-start(f32[48,1536]{1,0:T(8,128)S(1)} %sum_wide.1.refs_2_.refs_1_), channel_id=1, source_target_pairs={{0,2},{1,3},{2,0},{3,1},{4,6},{5,7},{6,4},{7,5},{8,10},{9,11},{10,... | collective-permute-start | bytes 884744 | tf_op jit(solution)/shard_map/ppermute | solution.py:898
  156.6 9.5 %collective-permute-start.24 = (f32[48,1536]{1,0:T(8,128)S(1)}, f32[48,1536]{1,0:T(8,128)S(1)}, u32[]{:S(2)}, u32[]{:S(2)}) collective-permute-start(f32[48,1536]{1,0:T(8,128)S(1)} %pack.1.refs_3_), channel_id=1, source_target_pairs={{0,2},{1,3},{2,0},{3,1},{4,6},{5,7},{6,4},{7,5},{8,10},{9,11},{10,... | collective-permute-start | bytes 884744 | tf_op jit(solution)/shard_map/ppermute | solution.py:898
  160.6 5.4 %collective-permute-start.26 = (f32[56,640]{1,0:T(8,128)S(1)}, f32[56,640]{1,0:T(8,128)S(1)}, u32[]{:S(2)}, u32[]{:S(2)}) collective-permute-start(f32[56,640]{1,0:T(8,128)S(1)} %get-tuple-element.759), channel_id=1, source_target_pairs={{0,8},{1,17},{2,10},{3,19},{4,12},{5,21},{6,14},{7,23},{8,0},{9,25... | collective-permute-start | bytes 430088 | tf_op jit(solution)/shard_map/ppermute | solution.py:909
  166.3 2.9 %collective-permute-start.28 = (f32[96,3072]{1,0:T(8,128)S(1)}, f32[96,3072]{1,0:T(8,128)S(1)}, u32[]{:S(2)}, u32[]{:S(2)}) collective-permute-start(f32[96,3072]{1,0:T(8,128)S(1)} %get-tuple-element.761.refs_0_), channel_id=1, source_target_pairs={{0,1},{1,0},{2,3},{3,2},{4,5},{5,4},{6,7},{7,6},{8,9},{9,8},{10,11... | collective-permute-start | bytes 3538952 | tf_op jit(solution)/shard_map/ppermute | solution.py:898
  166.4 6.2 %collective-permute-start.27 = (f32[56,640]{1,0:T(8,128)S(1)}, f32[56,640]{1,0:T(8,128)S(1)}, u32[]{:S(2)}, u32[]{:S(2)}) collective-permute-start(f32[56,640]{1,0:T(8,128)S(1)} %sum_scan.1.refs_5_.refs_1_), channel_id=1, source_target_pairs={{0,2},{1,3},{2,0},{3,1},{4,6},{5,7},{6,4},{7,5},{8,10},{9,11},{10,... | collective-permute-start | bytes 430088 | tf_op jit(solution)/shard_map/ppermute | solution.py:898
  172.7 1.6 collective-permute-start.29

commit v4 on v3

--- a/solution.py
+++ b/solution.py
@@ -269,7 +269,7 @@
     steps = positions // SUB
     rows = seqs * positions
     width = 2 * chans
-    size = row_block(rows, 144)
+    size = row_block(rows, 336)
     entered(r, tiles, r.chunks, tiles, r.start, r.entries, False)
 
     def scan(seq):
@@ -1111,7 +1111,7 @@
     (hidden_out,) = run(
         pool, lambda r: (r.save(r.hidden, r.hidden_out),
                          grad_narrow_kernel(down_plan, N.hidden, N.cot, N.keep_down, N.send_down, r)), N.grad_down,
-        new=[(N.keep_down, (units, width // 2), F32), (N.send_down, (units, width // 2), F32)],
+        new=[(N.send_down, (units, width // 2), F32), (N.keep_down, (units, width // 2), F32)],
         out=[(N.hidden_out, (rows, units), BF16)], drop=(N.hidden,),
         scratch={N.turned: pltpu.VMEM((rows, width), BF16)},
     )

time: 176 us -> 173 us (0.983)
  Pallas kernels: 79 us -> 76.7 us
    pallas_call x41, Pallas kernels: 76.6 us -> 74.3 us  [run(): pl.pallas_call(body, out_shape=shapes, in_specs=[pl.BlockSpec(memory_spac...]
  transfers between devices with their start and end apart: 30 -> 30, of which waited for: 18 -> 19; matrix products, arithmetic and copies ran while one was open for 0% -> 0% of each run, Pallas kernels for 31% -> 31%
where the time goes in v4:
time: 173 us
  Pallas kernels  76.7 us (44%)
  waiting for transfers between devices  51 us (29%)
  starting transfers between devices  44.2 us (26%)
    pallas_call x41, Pallas kernels, run(): pl.pallas_call(body, out_shape=shapes, in_specs=[pl.BlockSpec(memory_spac...  74.3 us
    ppermute x13, waiting for transfers between devices, across_by_core(): return lax.ppermute(value, (N.seq, N.batch), pairs)  41.8 us
    ppermute x13, starting transfers between devices, across_by_core(): return lax.ppermute(value, (N.seq, N.batch), pairs)  23.3 us
    ppermute x17, starting transfers between devices, across(): return lax.ppermute(value, axis, [(at, at ^ bit) for at in range(size)])  20.9 us
    ppermute x17, waiting for transfers between devices, across(): return lax.ppermute(value, axis, [(at, at ^ bit) for at in range(size)])  9.15 us
  transfers between devices with their start and end apart: 30, of which 19 were waited for; matrix products, arithmetic and copies ran while one was open for 0% of the time, Pallas kernels for 31%

profile of v4, /device:TPU:0, one launch (start us, length us, event | category | flops | bytes accessed | tf_op | source)
XLA Modules:
  0.0 172.9 jit_solution(12606224924362890421)
XLA Ops:
  0.6 7.1 %project.1 = (f32[8,768]{1,0:T(8,128)S(1)}, bf16[768,1920]{1,0:T(8,128)(2,1)S(1)}, bf16[1008,768]{1,0:T(8,128)(2,1)S(1)}, f32[9,1008,128]{2,1,0:T(8,128)S(1)}, f...) custom-call(bf16[1008,768]{1,0:T(8,128)(2,1)} %bitcast.4, ...), custom_call_target="tpu_custom_call" | custom-call | flops 1840000000 | tf_op jit(solution)/shard_map/project/pallas_call | solution.py:864
  7.7 3.0 %collective-permute-start = (f32[12,8,128]{2,1,0:T(8,128)S(1)}, f32[12,8,128]{2,1,0:T(8,128)S(1)}, u32[]{:S(2)}, u32[]{:S(2)}) collective-permute-start(f32[12,8,128]{2,1,0:T(8,128)S(1)} %get-tuple-element.414.refs_12_), channel_id=1, source_target_pairs={{0,4},{4,0},{8,12},{12,8},{16,20},{20,16},{24,28},{28,24},{1,5},{5... | collective-permute-start | bytes 147464 | tf_op jit(solution)/shard_map/ppermute | solution.py:898
  10.8 1.8 %gate.1 = (f32[8,768]{1,0:T(8,128)S(1)}, bf16[1008,768]{1,0:T(8,128)(2,1)S(1)}, f32[9,1008,128]{2,1,0:T(8,128)S(1)}, f32[3,1008,128]{2,1,0:T(8,128)S(1)}, f32[6,...) custom-call(f32[8,768]{1,0:T(8,128)S(1)} %get-tuple-element.393.refs, ...), custom_call_target="tpu_custom_call", output_to_operand_aliasing={{0}: (0, {}), {1}: (1, {}), {2}: (2, {}), {3}: (3, {}), {4}... | custom-call | flops 414000000 | tf_op jit(solution)/shard_map/gate/pallas_call | solution.py:864
  12.9 2.1 %collective-permute-start.1 = (f32[12,8,128]{2,1,0:T(8,128)S(1)}, f32[12,8,128]{2,1,0:T(8,128)S(1)}, u32[]{:S(2)}, u32[]{:S(2)}) collective-permute-start(f32[12,8,128]{2,1,0:T(8,128)S(1)} %get-tuple-element.440.refs_14_), channel_id=1, source_target_pairs={{0,8},{4,12},{8,0},{12,4},{16,24},{20,28},{24,16},{28,20},{1,9},{5... | collective-permute-start | bytes 147464 | tf_op jit(solution)/shard_map/ppermute | solution.py:898
  15.1 1.9 %hidden_back.2 = (f32[8,768]{1,0:T(8,128)S(1)}, bf16[1008,768]{1,0:T(8,128)(2,1)S(1)}, f32[9,1008,128]{2,1,0:T(8,128)S(1)}, f32[3,1008,128]{2,1,0:T(8,128)S(1)},...) custom-call(f32[8,768]{1,0:T(8,128)S(1)} %get-tuple-element.415.refs, ...), custom_call_target="tpu_custom_call", output_to_operand_aliasing={{0}: (0, {}), {1}: (1, {}), {2}: (2, {}), {3}: (3, {}), {4}... | custom-call | flops 437000000 | tf_op jit(solution)/shard_map/hidden_back/pallas_call | solution.py:864
  17.2 3.1 %collective-permute-start.2 = (f32[12,8,128]{2,1,0:T(8,128)S(1)}, f32[12,8,128]{2,1,0:T(8,128)S(1)}, u32[]{:S(2)}, u32[]{:S(2)}) collective-permute-start(f32[12,8,128]{2,1,0:T(8,128)S(1)} %get-tuple-element.467.refs_14_), channel_id=1, source_target_pairs={{0,16},{4,20},{8,24},{12,28},{16,0},{20,4},{24,8},{28,12},{1,17},{... | collective-permute-start | bytes 147464 | tf_op jit(solution)/shard_map/ppermute | solution.py:898
  20.3 1.9 %hidden_back.3 = (f32[8,768]{1,0:T(8,128)S(1)}, bf16[1008,768]{1,0:T(8,128)(2,1)S(1)}, f32[9,1008,128]{2,1,0:T(8,128)S(1)}, f32[3,1008,128]{2,1,0:T(8,128)S(1)},...) custom-call(f32[8,768]{1,0:T(8,128)S(1)} %get-tuple-element.441.refs, ...), custom_call_target="tpu_custom_call", output_to_operand_aliasing={{0}: (0, {}), {1}: (1, {}), {2}: (2, {}), {3}: (3, {}), {4}... | custom-call | flops 437000000 | tf_op jit(solution)/shard_map/hidden_back/pallas_call | solution.py:864
  22.5 3.9 %mix.1 = (f32[8,768]{1,0:T(8,128)S(1)}, bf16[1008,768]{1,0:T(8,128)(2,1)S(1)}, f32[9,1008,128]{2,1,0:T(8,128)S(1)}, f32[9,64,128]{2,1,0:T(8,128)S(1)}, bf16[1008...) custom-call(f32[8,768]{1,0:T(8,128)S(1)} %get-tuple-element.468.refs, ...), custom_call_target="tpu_custom_call", output_to_operand_aliasing={{0}: (0, {}), {1}: (1, {}), {2}: (2, {}), {3}: (3, {}), {4}... | custom-call | flops 1356999936 | tf_op jit(solution)/shard_map/mix/pallas_call | solution.py:864
  26.4 7.3 %ffn.1 = (f32[8,768]{1,0:T(8,128)S(1)}, f32[9,64,128]{2,1,0:T(8,128)S(1)}, bf16[1008,768]{1,0:T(8,128)(2,1)S(1)}, f32[6,64,128]{2,1,0:T(8,128)S(1)}, f32[1008,76...) custom-call(f32[8,768]{1,0:T(8,128)S(1)} %get-tuple-element.481.refs, ...), custom_call_target="tpu_custom_call", output_to_operand_aliasing={{0}: (0, {}), {1}: (1, {}), {2}: (2, {}), {3}: (3, {}), {4}... | custom-call | flops 1679000064 | tf_op jit(solution)/shard_map/ffn/pallas_call | solution.py:864
  33.8 3.2 %grad_gu.2 = (f32[8,768]{1,0:T(8,128)S(1)}, f32[9,64,128]{2,1,0:T(8,128)S(1)}, bf16[1008,768]{1,0:T(8,128)(2,1)S(1)}, f32[6,64,128]{2,1,0:T(8,128)S(1)}, f32[100...) custom-call(f32[8,768]{1,0:T(8,128)S(1)} %get-tuple-element.496.refs, ...), custom_call_target="tpu_custom_call", output_to_operand_aliasing={{0}: (0, {}), {1}: (1, {}), {2}: (2, {}), {3}: (3, {}), {4}... | custom-call | flops 736000000 | tf_op jit(solution)/shard_map/grad_gu/pallas_call | solution.py:864
  37.0 3.2 %grad_gu.3 = (f32[8,768]{1,0:T(8,128)S(1)}, f32[9,64,128]{2,1,0:T(8,128)S(1)}, bf16[1008,768]{1,0:T(8,128)(2,1)S(1)}, f32[6,64,128]{2,1,0:T(8,128)S(1)}, f32[100...) custom-call(f32[8,768]{1,0:T(8,128)S(1)} %get-tuple-element.505.refs, ...), custom_call_target="tpu_custom_call", output_to_operand_aliasing={{0}: (0, {}), {1}: (1, {}), {2}: (2, {}), {3}: (3, {}), {4}... | custom-call | flops 736000000 | tf_op jit(solution)/shard_map/grad_gu/pallas_call | solution.py:864
  40.2 4.0 %grad_down.1 = (f32[8,768]{1,0:T(8,128)S(1)}, f32[9,64,128]{2,1,0:T(8,128)S(1)}, bf16[1008,768]{1,0:T(8,128)(2,1)S(1)}, f32[6,64,128]{2,1,0:T(8,128)S(1)}, f32[1...) custom-call(f32[8,768]{1,0:T(8,128)S(1)} %get-tuple-element.514.refs, ...), custom_call_target="tpu_custom_call", output_to_operand_aliasing={{0}: (0, {}), {1}: (1, {}), {2}: (2, {}), {3}: (3, {}), {4}... | custom-call | flops 828000000 | tf_op jit(solution)/shard_map/grad_down/pallas_call | solution.py:864
  45.6 1.9 %collective-permute-start.6 = (f32[384,1536]{1,0:T(8,128)S(1)}, f32[384,1536]{1,0:T(8,128)S(1)}, u32[]{:S(2)}, u32[]{:S(2)}) collective-permute-start(f32[384,1536]{1,0:T(8,128)S(1)} %get-tuple-element.637), channel_id=1, source_target_pairs={{0,2},{1,5},{2,0},{3,7},{4,6},{5,1},{6,4},{7,3},{8,10},{9,13},{10,... | collective-permute-start | bytes 7077896 | tf_op jit(solution)/shard_map/ppermute | solution.py:909
  47.5 6.5 %ffn_back.1 = (f32[8,768]{1,0:T(8,128)S(1)}, f32[9,64,128]{2,1,0:T(8,128)S(1)}, f32[6,64,128]{2,1,0:T(8,128)S(1)}, f32[1536,384]{1,0:T(8,128)S(1)}, f32[384,1536...) custom-call(f32[8,768]{1,0:T(8,128)S(1)} %get-tuple-element.535.refs, ...), custom_call_target="tpu_custom_call", output_to_operand_aliasing={{0}: (0, {}), {1}: (1, {}), {2}: (2, {}), {3}: (3, {}), {4}... | custom-call | flops 1495000064 | tf_op jit(solution)/shard_map/ffn_back/pallas_call | solution.py:864
  54.4 6.9 %mix_back.1 = (f32[8,768]{1,0:T(8,128)S(1)}, f32[9,64,128]{2,1,0:T(8,128)S(1)}, f32[6,64,128]{2,1,0:T(8,128)S(1)}, f32[384,1536]{1,0:T(8,128)S(1)}, f32[1008,768...) custom-call(f32[8,768]{1,0:T(8,128)S(1)} %get-tuple-element.560.refs, ...), custom_call_target="tpu_custom_call", output_to_operand_aliasing={{0}: (0, {}), {1}: (1, {}), {2}: (2, {}), {3}: (3, {}), {4}... | custom-call | flops 1610000000 | tf_op jit(solution)/shard_map/mix_back/pallas_call | solution.py:864
  61.3 2.7 %collective-permute-start.5 = (f32[1,9,8,128]{3,2,1,0:T(8,128)S(1)}, f32[1,9,8,128]{3,2,1,0:T(8,128)S(1)}, u32[]{:S(2)}, u32[]{:S(2)}) collective-permute-start(f32[1,9,8,128]{3,2,1,0:T(8,128)S(1)} %get-tuple-element.605.refs_15_), channel_id=1, source_target_pairs={{0,16},{4,20},{8,24},{12,28},{16,0},{20,4},{24,8},{28,12},{1,17},{... | collective-permute-start | bytes 110600 | tf_op jit(solution)/shard_map/ppermute | solution.py:898
  66.3 1.6 grad_gate.1
  68.0 1.8 %collective-permute-start.7 = (f32[2,9,8,128]{3,2,1,0:T(8,128)S(1)}, f32[2,9,8,128]{3,2,1,0:T(8,128)S(1)}, u32[]{:S(2)}, u32[]{:S(2)}) collective-permute-start(f32[2,9,8,128]{3,2,1,0:T(8,128)S(1)} %get-tuple-element.654.refs_16_), channel_id=1, source_target_pairs={{0,8},{4,12},{8,0},{12,4},{16,24},{20,28},{24,16},{28,20},{1,9},{5... | collective-permute-start | bytes 221192 | tf_op jit(solution)/shard_map/ppermute | solution.py:898
  69.8 4.7 %collective-permute-done.6.refs_16_ = f32[384,1536]{1,0:T(8,128)S(1)} collective-permute-done((f32[384,1536]{1,0:T(8,128)S(1)}, f32[384,1536]{1,0:T(8,128)S(1)}, u32[]{:S(2)}, u32[]{:S(2)}) %collective-permute-start.6) | collective-permute-done | bytes 2359328 | tf_op jit(solution)/shard_map/ppermute | solution.py:909
  74.9 1.9 %collective-permute-start.8 = (f32[4,9,8,128]{3,2,1,0:T(8,128)S(1)}, f32[4,9,8,128]{3,2,1,0:T(8,128)S(1)}, u32[]{:S(2)}, u32[]{:S(2)}) collective-permute-start(f32[4,9,8,128]{3,2,1,0:T(8,128)S(1)} %get-tuple-element.671.refs_16_), channel_id=1, source_target_pairs={{0,4},{4,0},{8,12},{12,8},{16,20},{20,16},{24,28},{28,24},{1,5},{5... | collective-permute-start | bytes 442376 | tf_op jit(solution)/shard_map/ppermute | solution.py:898
  77.0 3.1 %collective-permute-done.8.refs_17_ = f32[4,9,8,128]{3,2,1,0:T(8,128)S(1)} collective-permute-done((f32[4,9,8,128]{3,2,1,0:T(8,128)S(1)}, f32[4,9,8,128]{3,2,1,0:T(8,128)S(1)}, u32[]{:S(2)}, u32[]{:S(2)}) %collective-permute-start.8) | collective-permute-done | bytes 147488 | tf_op jit(solution)/shard_map/ppermute | solution.py:898
  80.3 4.0 %scan_back.1 = (f32[8,768]{1,0:T(8,128)S(1)}, f32[1008,768]{1,0:T(8,128)S(1)}, f32[8,768]{1,0:T(8,128)S(1)}, f32[768,384]{1,0:T(8,128)S(1)}, bf16[1008,768]{1,0:...) custom-call(f32[8,768]{1,0:T(8,128)S(1)} %get-tuple-element.672.refs, ...), custom_call_target="tpu_custom_call", output_to_operand_aliasing={{0}: (0, {}), {1}: (1, {}), {2}: (2, {}), {3}: (3, {}), {4}... | custom-call | flops 920000000 | tf_op jit(solution)/shard_map/scan_back/pallas_call | solution.py:864
  84.7 1.9 %collective-permute-start.16 = (f32[384,768]{1,0:T(8,128)S(1)}, f32[384,768]{1,0:T(8,128)S(1)}, u32[]{:S(2)}, u32[]{:S(2)}) collective-permute-start(f32[384,768]{1,0:T(8,128)S(1)} %get-tuple-element.742), channel_id=1, source_target_pairs={{0,4},{1,3},{2,6},{3,1},{4,0},{5,7},{6,2},{7,5},{8,12},{9,11},{10,... | collective-permute-start | bytes 3538952 | tf_op jit(solution)/shard_map/ppermute | solution.py:909
  86.6 1.6 collective-permute-start.11
  88.2 5.6 %input_back.1 = (f32[8,768]{1,0:T(8,128)S(1)}, f32[8,768]{1,0:T(8,128)S(1)}, f32[768,384]{1,0:T(8,128)S(1)}, f32[8,768]{1,0:T(8,128)S(1)}, bf16[1008,768]{1,0:T(...) custom-call(f32[8,768]{1,0:T(8,128)S(1)} %get-tuple-element.706.refs, ...), custom_call_target="tpu_custom_call", output_to_operand_aliasing={{0}: (0, {}), {1}: (1, {}), {2}: (2, {}), {3}: (3, {}), {4}... | custom-call | flops 1288000000 | tf_op jit(solution)/shard_map/input_back/pallas_call | solution.py:864
  93.8 2.5 %grad_scan.1 = (f32[8,768]{1,0:T(8,128)S(1)}, f32[768,384]{1,0:T(8,128)S(1)}, f32[192,1536]{1,0:T(8,128)S(1)}, f32[384,768]{1,0:T(8,128)S(1)}, f32[776,640]{1,0:...) custom-call(f32[8,768]{1,0:T(8,128)S(1)} %get-tuple-element.721.refs, ...), custom_call_target="tpu_custom_call", output_to_operand_aliasing={{0}: (0, {}), {1}: (1, {}), {2}: (2, {}), {3}: (3, {})} | custom-call | flops 552000000 | tf_op jit(solution)/shard_map/grad_scan/pallas_call | solution.py:864
  96.9 8.8 %collective-permute-done.16.refs_3_ = f32[384,768]{1,0:T(8,128)S(1)} collective-permute-done((f32[384,768]{1,0:T(8,128)S(1)}, f32[384,768]{1,0:T(8,128)S(1)}, u32[]{:S(2)}, u32[]{:S(2)}) %collective-permute-start.16) | collective-permute-done | bytes 1179680 | tf_op jit(solution)/shard_map/ppermute | solution.py:909
  106.1 1.6 collective-permute-start.21
  107.7 6.3 %collective-permute-done.11.refs_1_ = f32[192,1536]{1,0:T(8,128)S(1)} collective-permute-done((f32[192,1536]{1,0:T(8,128)S(1)}, f32[192,1536]{1,0:T(8,128)S(1)}, u32[]{:S(2)}, u32[]{:S(2)}) %collective-permute-start.11) | collective-permute-done | bytes 1179680 | tf_op jit(solution)/shard_map/ppermute | solution.py:909
  114.5 1.6 collective-permute-start.17
  116.6 5.8 %collective-permute-done.21.refs_1_ = f32[384,768]{1,0:T(8,128)S(1)} collective-permute-done((f32[384,768]{1,0:T(8,128)S(1)}, f32[384,768]{1,0:T(8,128)S(1)}, u32[]{:S(2)}, u32[]{:S(2)}) %collective-permute-start.21) | collective-permute-done | bytes 1179680 | tf_op jit(solution)/shard_map/ppermute | solution.py:909
  122.5 1.7 collective-permute-start.22
  124.3 6.6 %output.1 = (f32[8,128]{1,0:T(8,128)S(1)}, bf16[1008,768]{1,0:T(8,128)(2,1)}) custom-call(bf16[1536,768]{1,0:T(8,128)(2,1)} %refs_0_.1, f32[1008,768]{1,0:T(8,128)} %get-tuple-element.495.refs_1_, bf16[1008,1536]{1,0:T(8,128)(2,1)} %get-tuple-element.523.refs_2_), custom_call_target="tpu_custom_call" | custom-call | flops 1610000000 | tf_op jit(solution)/shard_map/output/pallas_call | solution.py:864
  130.9 2.2 %collective-permute-done.17.refs_1_ = f32[392,640]{1,0:T(8,128)S(1)} collective-permute-done((f32[392,640]{1,0:T(8,128)S(1)}, f32[392,640]{1,0:T(8,128)S(1)}, u32[]{:S(2)}, u32[]{:S(2)}) %collective-permute-start.17) | collective-permute-done | bytes 1003552 | tf_op jit(solution)/shard_map/ppermute | solution.py:909
  133.3 1.6 collective-permute-start.19
  135.1 2.7 %collective-permute-start.18 = (f32[48,1536]{1,0:T(8,128)S(1)}, f32[48,1536]{1,0:T(8,128)S(1)}, u32[]{:S(2)}, u32[]{:S(2)}) collective-permute-start(f32[48,1536]{1,0:T(8,128)S(1)} %get-tuple-element.749), channel_id=1, source_target_pairs={{0,16},{1,3},{2,18},{3,1},{4,20},{5,7},{6,22},{7,5},{8,24},{9,11},... | collective-permute-start | bytes 884744 | tf_op jit(solution)/shard_map/ppermute | solution.py:909
  138.0 2.9 %collective-permute-start.23 = (f32[96,768]{1,0:T(8,128)S(1)}, f32[96,768]{1,0:T(8,128)S(1)}, u32[]{:S(2)}, u32[]{:S(2)}) collective-permute-start(f32[96,768]{1,0:T(8,128)S(1)} %get-tuple-element.756), channel_id=1, source_target_pairs={{0,16},{1,9},{2,18},{3,11},{4,20},{5,13},{6,22},{7,15},{8,24},{9,1... | collective-permute-start | bytes 884744 | tf_op jit(solution)/shard_map/ppermute | solution.py:909
  140.9 1.6 collective-permute-done.19.refs_1_
  142.6 2.8 %collective-permute-start.25 = (f32[104,640]{1,0:T(8,128)S(1)}, f32[104,640]{1,0:T(8,128)S(1)}, u32[]{:S(2)}, u32[]{:S(2)}) collective-permute-start(f32[104,640]{1,0:T(8,128)S(1)} %get-tuple-element.757), channel_id=1, source_target_pairs={{0,16},{1,9},{2,18},{3,11},{4,20},{5,13},{6,22},{7,15},{8,24},{9,1... | collective-permute-start | bytes 798728 | tf_op jit(solution)/shard_map/ppermute | solution.py:909
  145.4 2.3 %collective-permute-done.18.refs_1_ = f32[48,1536]{1,0:T(8,128)S(1)} collective-permute-done((f32[48,1536]{1,0:T(8,128)S(1)}, f32[48,1536]{1,0:T(8,128)S(1)}, u32[]{:S(2)}, u32[]{:S(2)}) %collective-permute-start.18) | collective-permute-done | bytes 294944 | tf_op jit(solution)/shard_map/ppermute | solution.py:909
  147.7 1.6 collective-permute-start.20
  149.3 5.0 %collective-permute-done.23.refs_1_ = f32[96,768]{1,0:T(8,128)S(1)} collective-permute-done((f32[96,768]{1,0:T(8,128)S(1)}, f32[96,768]{1,0:T(8,128)S(1)}, u32[]{:S(2)}, u32[]{:S(2)}) %collective-permute-start.23) | collective-permute-done | bytes 294944 | tf_op jit(solution)/shard_map/ppermute | solution.py:909
  154.5 1.6 collective-permute-start.24
  156.0 2.2 %collective-permute-done.25.refs_1_ = f32[104,640]{1,0:T(8,128)S(1)} collective-permute-done((f32[104,640]{1,0:T(8,128)S(1)}, f32[104,640]{1,0:T(8,128)S(1)}, u32[]{:S(2)}, u32[]{:S(2)}) %collective-permute-start.25) | collective-permute-done | bytes 266272 | tf_op jit(solution)/shard_map/ppermute | solution.py:909
  158.3 2.3 %collective-permute-start.26 = (f32[56,640]{1,0:T(8,128)S(1)}, f32[56,640]{1,0:T(8,128)S(1)}, u32[]{:S(2)}, u32[]{:S(2)}) collective-permute-start(f32[56,640]{1,0:T(8,128)S(1)} %get-tuple-element.759), channel_id=1, source_target_pairs={{0,8},{1,17},{2,10},{3,19},{4,12},{5,21},{6,14},{7,23},{8,0},{9,25... | collective-permute-start | bytes 430088 | tf_op jit(solution)/shard_map/ppermute | solution.py:909
  160.7 3.1 %collective-permute-done.26.refs_1_ = f32[56,640]{1,0:T(8,128)S(1)} collective-permute-done((f32[56,640]{1,0:T(8,128)S(1)}, f32[56,640]{1,0:T(8,128)S(1)}, u32[]{:S(2)}, u32[]{:S(2)}) %collective-permute-start.26) | collective-permute-done | bytes 143392 | tf_op jit(solution)/shard_map/ppermute | solution.py:909
  164.1 1.6 collective-permute-start.27
  168.4 1.9 %collective-permute-done.27.refs_2_ = f32[56,640]{1,0:T(8,128)S(1)} collective-permute-done((f32[56,640]{1,0:T(8,128)S(1)}, f32[56,640]{1,0:T(8,128)S(1)}, u32[]{:S(2)}, u32[]{:S(2)}) %collective-permute-start.27) | collective-permute-done | bytes 143392 | tf_op jit(solution)/shard_map/ppermute | solution.py:898
  (55 shorter events, 14.9 us)
Async XLA Ops:
  7.7 5.1 %collective-permute-start = (f32[12,8,128]{2,1,0:T(8,128)S(1)}, f32[12,8,128]{2,1,0:T(8,128)S(1)}, u32[]{:S(2)}, u32[]{:S(2)}) collective-permute-start(f32[12,8,128]{2,1,0:T(8,128)S(1)} %get-tuple-element.414.refs_12_), channel_id=1, source_target_pairs={{0,4},{4,0},{8,12},{12,8},{16,20},{20,16},{24,28},{28,24},{1,5},{5... | collective-permute-start | bytes 147464 | tf_op jit(solution)/shard_map/ppermute | solution.py:898
  12.9 4.2 %collective-permute-start.1 = (f32[12,8,128]{2,1,0:T(8,128)S(1)}, f32[12,8,128]{2,1,0:T(8,128)S(1)}, u32[]{:S(2)}, u32[]{:S(2)}) collective-permute-start(f32[12,8,128]{2,1,0:T(8,128)S(1)} %get-tuple-element.440.refs_14_), channel_id=1, source_target_pairs={{0,8},{4,12},{8,0},{12,4},{16,24},{20,28},{24,16},{28,20},{1,9},{5... | collective-permute-start | bytes 147464 | tf_op jit(solution)/shard_map/ppermute | solution.py:898
  17.2 5.2 %collective-permute-start.2 = (f32[12,8,128]{2,1,0:T(8,128)S(1)}, f32[12,8,128]{2,1,0:T(8,128)S(1)}, u32[]{:S(2)}, u32[]{:S(2)}) collective-permute-start(f32[12,8,128]{2,1,0:T(8,128)S(1)} %get-tuple-element.467.refs_14_), channel_id=1, source_target_pairs={{0,16},{4,20},{8,24},{12,28},{16,0},{20,4},{24,8},{28,12},{1,17},{... | collective-permute-start | bytes 147464 | tf_op jit(solution)/shard_map/ppermute | solution.py:898
  36.9 8.0 %collective-permute-start.3 = (f32[768,1536]{1,0:T(8,128)S(1)}, f32[768,1536]{1,0:T(8,128)S(1)}, u32[]{:S(2)}, u32[]{:S(2)}) collective-permute-start(f32[768,1536]{1,0:T(8,128)S(1)} %get-tuple-element.534), channel_id=1, source_target_pairs={{0,1},{1,0},{2,3},{3,2},{4,5},{5,4},{6,7},{7,6},{8,9},{9,8},{10,11... | collective-permute-start | bytes 14155784 | tf_op jit(solution)/shard_map/ppermute | solution.py:898
  44.2 9.8 %collective-permute-start.4 = (f32[1536,384]{1,0:T(8,128)S(1)}, f32[1536,384]{1,0:T(8,128)S(1)}, u32[]{:S(2)}, u32[]{:S(2)}) collective-permute-start(f32[1536,384]{1,0:T(8,128)S(1)} %get-tuple-element.559), channel_id=1, source_target_pairs={{0,1},{1,0},{2,3},{3,2},{4,5},{5,4},{6,7},{7,6},{8,9},{9,8},{10,11... | collective-permute-start | bytes 7077896 | tf_op jit(solution)/shard_map/ppermute | solution.py:898
  45.6 28.9 %collective-permute-start.6 = (f32[384,1536]{1,0:T(8,128)S(1)}, f32[384,1536]{1,0:T(8,128)S(1)}, u32[]{:S(2)}, u32[]{:S(2)}) collective-permute-start(f32[384,1536]{1,0:T(8,128)S(1)} %get-tuple-element.637), channel_id=1, source_target_pairs={{0,2},{1,5},{2,0},{3,7},{4,6},{5,1},{6,4},{7,3},{8,10},{9,13},{10,... | collective-permute-start | bytes 7077896 | tf_op jit(solution)/shard_map/ppermute | solution.py:909
  61.3 4.9 %collective-permute-start.5 = (f32[1,9,8,128]{3,2,1,0:T(8,128)S(1)}, f32[1,9,8,128]{3,2,1,0:T(8,128)S(1)}, u32[]{:S(2)}, u32[]{:S(2)}) collective-permute-start(f32[1,9,8,128]{3,2,1,0:T(8,128)S(1)} %get-tuple-element.605.refs_15_), channel_id=1, source_target_pairs={{0,16},{4,20},{8,24},{12,28},{16,0},{20,4},{24,8},{28,12},{1,17},{... | collective-permute-start | bytes 110600 | tf_op jit(solution)/shard_map/ppermute | solution.py:898
  65.5 18.7 %collective-permute-start.9 = (f32[768,384]{1,0:T(8,128)S(1)}, f32[768,384]{1,0:T(8,128)S(1)}, u32[]{:S(2)}, u32[]{:S(2)}) collective-permute-start(f32[768,384]{1,0:T(8,128)S(1)} %get-tuple-element.704), channel_id=1, source_target_pairs={{0,1},{1,0},{2,3},{3,2},{4,5},{5,4},{6,7},{7,6},{8,9},{9,8},{10,11... | collective-permute-start | bytes 3538952 | tf_op jit(solution)/shard_map/ppermute | solution.py:898
  67.9 16.4 %collective-permute-start.10 = (f32[768,384]{1,0:T(8,128)S(1)}, f32[768,384]{1,0:T(8,128)S(1)}, u32[]{:S(2)}, u32[]{:S(2)}) collective-permute-start(f32[768,384]{1,0:T(8,128)S(1)} %get-tuple-element.705), channel_id=1, source_target_pairs={{0,1},{1,0},{2,3},{3,2},{4,5},{5,4},{6,7},{7,6},{8,9},{9,8},{10,11... | collective-permute-start | bytes 3538952 | tf_op jit(solution)/shard_map/ppermute | solution.py:898
  68.0 6.9 %collective-permute-start.7 = (f32[2,9,8,128]{3,2,1,0:T(8,128)S(1)}, f32[2,9,8,128]{3,2,1,0:T(8,128)S(1)}, u32[]{:S(2)}, u32[]{:S(2)}) collective-permute-start(f32[2,9,8,128]{3,2,1,0:T(8,128)S(1)} %get-tuple-element.654.refs_16_), channel_id=1, source_target_pairs={{0,8},{4,12},{8,0},{12,4},{16,24},{20,28},{24,16},{28,20},{1,9},{5... | collective-permute-start | bytes 221192 | tf_op jit(solution)/shard_map/ppermute | solution.py:898
  74.9 5.2 %collective-permute-start.8 = (f32[4,9,8,128]{3,2,1,0:T(8,128)S(1)}, f32[4,9,8,128]{3,2,1,0:T(8,128)S(1)}, u32[]{:S(2)}, u32[]{:S(2)}) collective-permute-start(f32[4,9,8,128]{3,2,1,0:T(8,128)S(1)} %get-tuple-element.671.refs_16_), channel_id=1, source_target_pairs={{0,4},{4,0},{8,12},{12,8},{16,20},{20,16},{24,28},{28,24},{1,5},{5... | collective-permute-start | bytes 442376 | tf_op jit(solution)/shard_map/ppermute | solution.py:898
  76.8 20.1 %collective-permute-start.15 = (f32[768,384]{1,0:T(8,128)S(1)}, f32[768,384]{1,0:T(8,128)S(1)}, u32[]{:S(2)}, u32[]{:S(2)}) collective-permute-start(f32[768,384]{1,0:T(8,128)S(1)} %get-tuple-element.741), channel_id=1, source_target_pairs={{0,4},{1,3},{2,6},{3,1},{4,0},{5,7},{6,2},{7,5},{8,12},{9,11},{10,... | collective-permute-start | bytes 3538952 | tf_op jit(solution)/shard_map/ppermute | solution.py:909
  84.7 21.0 %collective-permute-start.16 = (f32[384,768]{1,0:T(8,128)S(1)}, f32[384,768]{1,0:T(8,128)S(1)}, u32[]{:S(2)}, u32[]{:S(2)}) collective-permute-start(f32[384,768]{1,0:T(8,128)S(1)} %get-tuple-element.742), channel_id=1, source_target_pairs={{0,4},{1,3},{2,6},{3,1},{4,0},{5,7},{6,2},{7,5},{8,12},{9,11},{10,... | collective-permute-start | bytes 3538952 | tf_op jit(solution)/shard_map/ppermute | solution.py:909
  86.6 27.4 %collective-permute-start.11 = (f32[192,1536]{1,0:T(8,128)S(1)}, f32[192,1536]{1,0:T(8,128)S(1)}, u32[]{:S(2)}, u32[]{:S(2)}) collective-permute-start(f32[192,1536]{1,0:T(8,128)S(1)} %get-tuple-element.733), channel_id=1, source_target_pairs={{0,8},{1,17},{2,10},{3,19},{4,12},{5,21},{6,14},{7,23},{8,0},{9,25... | collective-permute-start | bytes 3538952 | tf_op jit(solution)/shard_map/ppermute | solution.py:909
  96.3 17.8 %collective-permute-start.13 = (f32[392,640]{1,0:T(8,128)S(1)}, f32[392,640]{1,0:T(8,128)S(1)}, u32[]{:S(2)}, u32[]{:S(2)}) collective-permute-start(f32[392,640]{1,0:T(8,128)S(1)} %get-tuple-element.737), channel_id=1, source_target_pairs={{0,1},{1,0},{2,3},{3,2},{4,5},{5,4},{6,7},{7,6},{8,9},{9,8},{10,11... | collective-permute-start | bytes 3010568 | tf_op jit(solution)/shard_map/ppermute | solution.py:898
  96.4 17.8 %collective-permute-start.14 = (f32[384,640]{1,0:T(8,128)S(1)}, f32[384,640]{1,0:T(8,128)S(1)}, u32[]{:S(2)}, u32[]{:S(2)}) collective-permute-start(f32[384,640]{1,0:T(8,128)S(1)} %get-tuple-element.738), channel_id=1, source_target_pairs={{0,1},{1,0},{2,3},{3,2},{4,5},{5,4},{6,7},{7,6},{8,9},{9,8},{10,11... | collective-permute-start | bytes 2949128 | tf_op jit(solution)/shard_map/ppermute | solution.py:898
  106.1 16.3 %collective-permute-start.21 = (f32[384,768]{1,0:T(8,128)S(1)}, f32[384,768]{1,0:T(8,128)S(1)}, u32[]{:S(2)}, u32[]{:S(2)}) collective-permute-start(f32[384,768]{1,0:T(8,128)S(1)} %get-tuple-element.752), channel_id=1, source_target_pairs={{0,2},{1,5},{2,0},{3,7},{4,6},{5,1},{6,4},{7,3},{8,10},{9,13},{10,... | collective-permute-start | bytes 3538952 | tf_op jit(solution)/shard_map/ppermute | solution.py:909
  114.5 18.6 %collective-permute-start.17 = (f32[392,640]{1,0:T(8,128)S(1)}, f32[392,640]{1,0:T(8,128)S(1)}, u32[]{:S(2)}, u32[]{:S(2)}) collective-permute-start(f32[392,640]{1,0:T(8,128)S(1)} %get-tuple-element.745), channel_id=1, source_target_pairs={{0,2},{1,5},{2,0},{3,7},{4,6},{5,1},{6,4},{7,3},{8,10},{9,13},{10,... | collective-permute-start | bytes 3010568 | tf_op jit(solution)/shard_map/ppermute | solution.py:909
  116.1 18.9 %collective-permute-start.12 = (f32[96,1536]{1,0:T(8,128)S(1)}, f32[96,1536]{1,0:T(8,128)S(1)}, u32[]{:S(2)}, u32[]{:S(2)}) collective-permute-start(f32[96,1536]{1,0:T(8,128)S(1)} %get-tuple-element.735), channel_id=1, source_target_pairs={{0,4},{1,9},{2,6},{3,11},{4,0},{5,13},{6,2},{7,15},{8,12},{9,1},{1... | collective-permute-start | bytes 1769480 | tf_op jit(solution)/shard_map/ppermute | solution.py:909
  122.5 15.3 %collective-permute-start.22 = (f32[192,768]{1,0:T(8,128)S(1)}, f32[192,768]{1,0:T(8,128)S(1)}, u32[]{:S(2)}, u32[]{:S(2)}) collective-permute-start(f32[192,768]{1,0:T(8,128)S(1)} %get-tuple-element.754), channel_id=1, source_target_pairs={{0,8},{1,17},{2,10},{3,19},{4,12},{5,21},{6,14},{7,23},{8,0},{9,25... | collective-permute-start | bytes 1769480 | tf_op jit(solution)/shard_map/ppermute | solution.py:909
  133.3 9.1 %collective-permute-start.19 = (f32[200,640]{1,0:T(8,128)S(1)}, f32[200,640]{1,0:T(8,128)S(1)}, u32[]{:S(2)}, u32[]{:S(2)}) collective-permute-start(f32[200,640]{1,0:T(8,128)S(1)} %get-tuple-element.750), channel_id=1, source_target_pairs={{0,4},{1,3},{2,6},{3,1},{4,0},{5,7},{6,2},{7,5},{8,12},{9,11},{10,... | collective-permute-start | bytes 1536008 | tf_op jit(solution)/shard_map/ppermute | solution.py:909
  135.1 12.5 %collective-permute-start.18 = (f32[48,1536]{1,0:T(8,128)S(1)}, f32[48,1536]{1,0:T(8,128)S(1)}, u32[]{:S(2)}, u32[]{:S(2)}) collective-permute-start(f32[48,1536]{1,0:T(8,128)S(1)} %get-tuple-element.749), channel_id=1, source_target_pairs={{0,16},{1,3},{2,18},{3,1},{4,20},{5,7},{6,22},{7,5},{8,24},{9,11},... | collective-permute-start | bytes 884744 | tf_op jit(solution)/shard_map/ppermute | solution.py:909
  138.0 16.4 %collective-permute-start.23 = (f32[96,768]{1,0:T(8,128)S(1)}, f32[96,768]{1,0:T(8,128)S(1)}, u32[]{:S(2)}, u32[]{:S(2)}) collective-permute-start(f32[96,768]{1,0:T(8,128)S(1)} %get-tuple-element.756), channel_id=1, source_target_pairs={{0,16},{1,9},{2,18},{3,11},{4,20},{5,13},{6,22},{7,15},{8,24},{9,1... | collective-permute-start | bytes 884744 | tf_op jit(solution)/shard_map/ppermute | solution.py:909
  142.6 15.6 %collective-permute-start.25 = (f32[104,640]{1,0:T(8,128)S(1)}, f32[104,640]{1,0:T(8,128)S(1)}, u32[]{:S(2)}, u32[]{:S(2)}) collective-permute-start(f32[104,640]{1,0:T(8,128)S(1)} %get-tuple-element.757), channel_id=1, source_target_pairs={{0,16},{1,9},{2,18},{3,11},{4,20},{5,13},{6,22},{7,15},{8,24},{9,1... | collective-permute-start | bytes 798728 | tf_op jit(solution)/shard_map/ppermute | solution.py:909
  147.7 16.1 %collective-permute-start.20 = (f32[48,1536]{1,0:T(8,128)S(1)}, f32[48,1536]{1,0:T(8,128)S(1)}, u32[]{:S(2)}, u32[]{:S(2)}) collective-permute-start(f32[48,1536]{1,0:T(8,128)S(1)} %sum_wide.1.refs_2_.refs_1_), channel_id=1, source_target_pairs={{0,2},{1,3},{2,0},{3,1},{4,6},{5,7},{6,4},{7,5},{8,10},{9,11},{10,... | collective-permute-start | bytes 884744 | tf_op jit(solution)/shard_map/ppermute | solution.py:898
  154.5 9.4 %collective-permute-start.24 = (f32[48,1536]{1,0:T(8,128)S(1)}, f32[48,1536]{1,0:T(8,128)S(1)}, u32[]{:S(2)}, u32[]{:S(2)}) collective-permute-start(f32[48,1536]{1,0:T(8,128)S(1)} %pack.1.refs_3_), channel_id=1, source_target_pairs={{0,2},{1,3},{2,0},{3,1},{4,6},{5,7},{6,4},{7,5},{8,10},{9,11},{10,... | collective-permute-start | bytes 884744 | tf_op jit(solution)/shard_map/ppermute | solution.py:898
  158.3 5.4 %collective-permute-start.26 = (f32[56,640]{1,0:T(8,128)S(1)}, f32[56,640]{1,0:T(8,128)S(1)}, u32[]{:S(2)}, u32[]{:S(2)}) collective-permute-start(f32[56,640]{1,0:T(8,128)S(1)} %get-tuple-element.759), channel_id=1, source_target_pairs={{0,8},{1,17},{2,10},{3,19},{4,12},{5,21},{6,14},{7,23},{8,0},{9,25... | collective-permute-start | bytes 430088 | tf_op jit(solution)/shard_map/ppermute | solution.py:909
  164.0 2.9 %collective-permute-start.28 = (f32[96,3072]{1,0:T(8,128)S(1)}, f32[96,3072]{1,0:T(8,128)S(1)}, u32[]{:S(2)}, u32[]{:S(2)}) collective-permute-start(f32[96,3072]{1,0:T(8,128)S(1)} %get-tuple-element.761.refs_0_), channel_id=1, source_target_pairs={{0,1},{1,0},{2,3},{3,2},{4,5},{5,4},{6,7},{7,6},{8,9},{9,8},{10,11... | collective-permute-start | bytes 3538952 | tf_op jit(solution)/shard_map/ppermute | solution.py:898
  164.1 6.2 %collective-permute-start.27 = (f32[56,640]{1,0:T(8,128)S(1)}, f32[56,640]{1,0:T(8,128)S(1)}, u32[]{:S(2)}, u32[]{:S(2)}) collective-permute-start(f32[56,640]{1,0:T(8,128)S(1)} %sum_scan.1.refs_5_.refs_1_), channel_id=1, source_target_pairs={{0,2},{1,3},{2,0},{3,1},{4,6},{5,7},{6,4},{7,5},{8,10},{9,11},{10,... | collective-permute-start | bytes 430088 | tf_op jit(solution)/shard_map/ppermute | solution.py:898
  170.4 1.6 collective-permute-start.29

commit v5 on v4

--- a/solution.py
+++ b/solution.py
@@ -123,12 +123,14 @@
 
     def project(step):
         at = rows_at(step, size)
+        made = dot(r.low[at, :], r.wmix[:, : 3 * chans], 1, 0)
         for part in range(3):
-            made = dot(r.low[at, :], r.wmix[:, part * chans : (part + 1) * chans], 1, 0)
-            if part == 2:
-                made = made + fbias
             for tile in range(tiles):
-                r.pre[part * tiles + tile, at, :] = made[:, tile * LANES : (tile + 1) * LANES]
+                start = part * chans + tile * LANES
+                value = made[:, start : start + LANES]
+                if part == 2:
+                    value = value + fbias[:, tile * LANES : (tile + 1) * LANES]
+                r.pre[part * tiles + tile, at, :] = value
 
     loop(rows // size, project)
 
@@ -562,7 +564,7 @@
     steps = positions // SUB
     rows = seqs * positions
     width = 2 * chans
-    small = row_block(rows, 144)
+    small = row_block(rows, 336)
     r.sums_out[...] = jnp.zeros(r.sums_out.shape, F32)
 
     def mix_back(step):

time: 173 us -> 173 us (level)
  Pallas kernels: 76.7 us -> 74.9 us
    pallas_call x41, Pallas kernels: 74.3 us -> 72.5 us  [run(): pl.pallas_call(body, out_shape=shapes, in_specs=[pl.BlockSpec(memory_spac...]
  transfers between devices with their start and end apart: 30 -> 30, of which waited for: 19 -> 19; matrix products, arithmetic and copies ran while one was open for 0% -> 0% of each run, Pallas kernels for 31% -> 30%
where the time goes in v5:
time: 173 us
  Pallas kernels  74.9 us (43%)
  waiting for transfers between devices  52.6 us (30%)
  starting transfers between devices  44.1 us (25%)
    pallas_call x41, Pallas kernels, run(): pl.pallas_call(body, out_shape=shapes, in_specs=[pl.BlockSpec(memory_spac...  72.5 us
    ppermute x13, waiting for transfers between devices, across_by_core(): return lax.ppermute(value, (N.seq, N.batch), pairs)  43.5 us
    ppermute x13, starting transfers between devices, across_by_core(): return lax.ppermute(value, (N.seq, N.batch), pairs)  23.2 us
    ppermute x17, starting transfers between devices, across(): return lax.ppermute(value, axis, [(at, at ^ bit) for at in range(size)])  21 us
    ppermute x17, waiting for transfers between devices, across(): return lax.ppermute(value, axis, [(at, at ^ bit) for at in range(size)])  9.1 us
  transfers between devices with their start and end apart: 30, of which 19 were waited for; matrix products, arithmetic and copies ran while one was open for 0% of the time, Pallas kernels for 30%

profile of v5, /device:TPU:0, one launch (start us, length us, event | category | flops | bytes accessed | tf_op | source)
XLA Modules:
  0.0 172.7 jit_solution(11291528709518441737)
XLA Ops:
  0.6 6.7 %project.1 = (f32[8,768]{1,0:T(8,128)S(1)}, bf16[768,1920]{1,0:T(8,128)(2,1)S(1)}, bf16[1008,768]{1,0:T(8,128)(2,1)S(1)}, f32[9,1008,128]{2,1,0:T(8,128)S(1)}, f...) custom-call(bf16[1008,768]{1,0:T(8,128)(2,1)} %bitcast.4, ...), custom_call_target="tpu_custom_call" | custom-call | flops 1840000000 | tf_op jit(solution)/shard_map/project/pallas_call | solution.py:866
  7.4 3.0 %collective-permute-start = (f32[12,8,128]{2,1,0:T(8,128)S(1)}, f32[12,8,128]{2,1,0:T(8,128)S(1)}, u32[]{:S(2)}, u32[]{:S(2)}) collective-permute-start(f32[12,8,128]{2,1,0:T(8,128)S(1)} %get-tuple-element.414.refs_12_), channel_id=1, source_target_pairs={{0,4},{4,0},{8,12},{12,8},{16,20},{20,16},{24,28},{28,24},{1,5},{5... | collective-permute-start | bytes 147464 | tf_op jit(solution)/shard_map/ppermute | solution.py:900
  10.4 1.9 %gate.1 = (f32[8,768]{1,0:T(8,128)S(1)}, bf16[1008,768]{1,0:T(8,128)(2,1)S(1)}, f32[9,1008,128]{2,1,0:T(8,128)S(1)}, f32[3,1008,128]{2,1,0:T(8,128)S(1)}, f32[6,...) custom-call(f32[8,768]{1,0:T(8,128)S(1)} %get-tuple-element.393.refs, ...), custom_call_target="tpu_custom_call", output_to_operand_aliasing={{0}: (0, {}), {1}: (1, {}), {2}: (2, {}), {3}: (3, {}), {4}... | custom-call | flops 414000000 | tf_op jit(solution)/shard_map/gate/pallas_call | solution.py:866
  12.6 2.1 %collective-permute-start.1 = (f32[12,8,128]{2,1,0:T(8,128)S(1)}, f32[12,8,128]{2,1,0:T(8,128)S(1)}, u32[]{:S(2)}, u32[]{:S(2)}) collective-permute-start(f32[12,8,128]{2,1,0:T(8,128)S(1)} %get-tuple-element.440.refs_14_), channel_id=1, source_target_pairs={{0,8},{4,12},{8,0},{12,4},{16,24},{20,28},{24,16},{28,20},{1,9},{5... | collective-permute-start | bytes 147464 | tf_op jit(solution)/shard_map/ppermute | solution.py:900
  14.8 1.9 %hidden_back.2 = (f32[8,768]{1,0:T(8,128)S(1)}, bf16[1008,768]{1,0:T(8,128)(2,1)S(1)}, f32[9,1008,128]{2,1,0:T(8,128)S(1)}, f32[3,1008,128]{2,1,0:T(8,128)S(1)},...) custom-call(f32[8,768]{1,0:T(8,128)S(1)} %get-tuple-element.415.refs, ...), custom_call_target="tpu_custom_call", output_to_operand_aliasing={{0}: (0, {}), {1}: (1, {}), {2}: (2, {}), {3}: (3, {}), {4}... | custom-call | flops 437000000 | tf_op jit(solution)/shard_map/hidden_back/pallas_call | solution.py:866
  16.9 3.1 %collective-permute-start.2 = (f32[12,8,128]{2,1,0:T(8,128)S(1)}, f32[12,8,128]{2,1,0:T(8,128)S(1)}, u32[]{:S(2)}, u32[]{:S(2)}) collective-permute-start(f32[12,8,128]{2,1,0:T(8,128)S(1)} %get-tuple-element.467.refs_14_), channel_id=1, source_target_pairs={{0,16},{4,20},{8,24},{12,28},{16,0},{20,4},{24,8},{28,12},{1,17},{... | collective-permute-start | bytes 147464 | tf_op jit(solution)/shard_map/ppermute | solution.py:900
  20.0 1.9 %hidden_back.3 = (f32[8,768]{1,0:T(8,128)S(1)}, bf16[1008,768]{1,0:T(8,128)(2,1)S(1)}, f32[9,1008,128]{2,1,0:T(8,128)S(1)}, f32[3,1008,128]{2,1,0:T(8,128)S(1)},...) custom-call(f32[8,768]{1,0:T(8,128)S(1)} %get-tuple-element.441.refs, ...), custom_call_target="tpu_custom_call", output_to_operand_aliasing={{0}: (0, {}), {1}: (1, {}), {2}: (2, {}), {3}: (3, {}), {4}... | custom-call | flops 437000000 | tf_op jit(solution)/shard_map/hidden_back/pallas_call | solution.py:866
  22.2 3.9 %mix.1 = (f32[8,768]{1,0:T(8,128)S(1)}, bf16[1008,768]{1,0:T(8,128)(2,1)S(1)}, f32[9,1008,128]{2,1,0:T(8,128)S(1)}, f32[9,64,128]{2,1,0:T(8,128)S(1)}, bf16[1008...) custom-call(f32[8,768]{1,0:T(8,128)S(1)} %get-tuple-element.468.refs, ...), custom_call_target="tpu_custom_call", output_to_operand_aliasing={{0}: (0, {}), {1}: (1, {}), {2}: (2, {}), {3}: (3, {}), {4}... | custom-call | flops 1356999936 | tf_op jit(solution)/shard_map/mix/pallas_call | solution.py:866
  26.1 7.3 %ffn.1 = (f32[8,768]{1,0:T(8,128)S(1)}, f32[9,64,128]{2,1,0:T(8,128)S(1)}, bf16[1008,768]{1,0:T(8,128)(2,1)S(1)}, f32[6,64,128]{2,1,0:T(8,128)S(1)}, f32[1008,76...) custom-call(f32[8,768]{1,0:T(8,128)S(1)} %get-tuple-element.481.refs, ...), custom_call_target="tpu_custom_call", output_to_operand_aliasing={{0}: (0, {}), {1}: (1, {}), {2}: (2, {}), {3}: (3, {}), {4}... | custom-call | flops 1679000064 | tf_op jit(solution)/shard_map/ffn/pallas_call | solution.py:866
  33.4 3.2 %grad_gu.2 = (f32[8,768]{1,0:T(8,128)S(1)}, f32[9,64,128]{2,1,0:T(8,128)S(1)}, bf16[1008,768]{1,0:T(8,128)(2,1)S(1)}, f32[6,64,128]{2,1,0:T(8,128)S(1)}, f32[100...) custom-call(f32[8,768]{1,0:T(8,128)S(1)} %get-tuple-element.496.refs, ...), custom_call_target="tpu_custom_call", output_to_operand_aliasing={{0}: (0, {}), {1}: (1, {}), {2}: (2, {}), {3}: (3, {}), {4}... | custom-call | flops 736000000 | tf_op jit(solution)/shard_map/grad_gu/pallas_call | solution.py:866
  36.7 3.2 %grad_gu.3 = (f32[8,768]{1,0:T(8,128)S(1)}, f32[9,64,128]{2,1,0:T(8,128)S(1)}, bf16[1008,768]{1,0:T(8,128)(2,1)S(1)}, f32[6,64,128]{2,1,0:T(8,128)S(1)}, f32[100...) custom-call(f32[8,768]{1,0:T(8,128)S(1)} %get-tuple-element.505.refs, ...), custom_call_target="tpu_custom_call", output_to_operand_aliasing={{0}: (0, {}), {1}: (1, {}), {2}: (2, {}), {3}: (3, {}), {4}... | custom-call | flops 736000000 | tf_op jit(solution)/shard_map/grad_gu/pallas_call | solution.py:866
  39.9 4.0 %grad_down.1 = (f32[8,768]{1,0:T(8,128)S(1)}, f32[9,64,128]{2,1,0:T(8,128)S(1)}, bf16[1008,768]{1,0:T(8,128)(2,1)S(1)}, f32[6,64,128]{2,1,0:T(8,128)S(1)}, f32[1...) custom-call(f32[8,768]{1,0:T(8,128)S(1)} %get-tuple-element.514.refs, ...), custom_call_target="tpu_custom_call", output_to_operand_aliasing={{0}: (0, {}), {1}: (1, {}), {2}: (2, {}), {3}: (3, {}), {4}... | custom-call | flops 828000000 | tf_op jit(solution)/shard_map/grad_down/pallas_call | solution.py:866
  45.3 1.9 %collective-permute-start.6 = (f32[384,1536]{1,0:T(8,128)S(1)}, f32[384,1536]{1,0:T(8,128)S(1)}, u32[]{:S(2)}, u32[]{:S(2)}) collective-permute-start(f32[384,1536]{1,0:T(8,128)S(1)} %get-tuple-element.637), channel_id=1, source_target_pairs={{0,2},{1,5},{2,0},{3,7},{4,6},{5,1},{6,4},{7,3},{8,10},{9,13},{10,... | collective-permute-start | bytes 7077896 | tf_op jit(solution)/shard_map/ppermute | solution.py:911
  47.2 6.4 %ffn_back.1 = (f32[8,768]{1,0:T(8,128)S(1)}, f32[9,64,128]{2,1,0:T(8,128)S(1)}, f32[6,64,128]{2,1,0:T(8,128)S(1)}, f32[1536,384]{1,0:T(8,128)S(1)}, f32[384,1536...) custom-call(f32[8,768]{1,0:T(8,128)S(1)} %get-tuple-element.535.refs, ...), custom_call_target="tpu_custom_call", output_to_operand_aliasing={{0}: (0, {}), {1}: (1, {}), {2}: (2, {}), {3}: (3, {}), {4}... | custom-call | flops 1495000064 | tf_op jit(solution)/shard_map/ffn_back/pallas_call | solution.py:866
  53.9 5.4 %mix_back.1 = (f32[8,768]{1,0:T(8,128)S(1)}, f32[9,64,128]{2,1,0:T(8,128)S(1)}, f32[6,64,128]{2,1,0:T(8,128)S(1)}, f32[384,1536]{1,0:T(8,128)S(1)}, f32[1008,768...) custom-call(f32[8,768]{1,0:T(8,128)S(1)} %get-tuple-element.560.refs, ...), custom_call_target="tpu_custom_call", output_to_operand_aliasing={{0}: (0, {}), {1}: (1, {}), {2}: (2, {}), {3}: (3, {}), {4}... | custom-call | flops 1610000000 | tf_op jit(solution)/shard_map/mix_back/pallas_call | solution.py:866
  59.3 2.7 %collective-permute-start.5 = (f32[1,9,8,128]{3,2,1,0:T(8,128)S(1)}, f32[1,9,8,128]{3,2,1,0:T(8,128)S(1)}, u32[]{:S(2)}, u32[]{:S(2)}) collective-permute-start(f32[1,9,8,128]{3,2,1,0:T(8,128)S(1)} %get-tuple-element.605.refs_15_), channel_id=1, source_target_pairs={{0,16},{4,20},{8,24},{12,28},{16,0},{20,4},{24,8},{28,12},{1,17},{... | collective-permute-start | bytes 110600 | tf_op jit(solution)/shard_map/ppermute | solution.py:900
  62.0 1.5 grad_out.1
  64.3 1.6 grad_gate.1
  65.9 1.8 %collective-permute-start.7 = (f32[2,9,8,128]{3,2,1,0:T(8,128)S(1)}, f32[2,9,8,128]{3,2,1,0:T(8,128)S(1)}, u32[]{:S(2)}, u32[]{:S(2)}) collective-permute-start(f32[2,9,8,128]{3,2,1,0:T(8,128)S(1)} %get-tuple-element.654.refs_16_), channel_id=1, source_target_pairs={{0,8},{4,12},{8,0},{12,4},{16,24},{20,28},{24,16},{28,20},{1,9},{5... | collective-permute-start | bytes 221192 | tf_op jit(solution)/shard_map/ppermute | solution.py:900
  67.7 6.4 %collective-permute-done.6.refs_16_ = f32[384,1536]{1,0:T(8,128)S(1)} collective-permute-done((f32[384,1536]{1,0:T(8,128)S(1)}, f32[384,1536]{1,0:T(8,128)S(1)}, u32[]{:S(2)}, u32[]{:S(2)}) %collective-permute-start.6) | collective-permute-done | bytes 2359328 | tf_op jit(solution)/shard_map/ppermute | solution.py:911
  74.6 1.9 %collective-permute-start.8 = (f32[4,9,8,128]{3,2,1,0:T(8,128)S(1)}, f32[4,9,8,128]{3,2,1,0:T(8,128)S(1)}, u32[]{:S(2)}, u32[]{:S(2)}) collective-permute-start(f32[4,9,8,128]{3,2,1,0:T(8,128)S(1)} %get-tuple-element.671.refs_16_), channel_id=1, source_target_pairs={{0,4},{4,0},{8,12},{12,8},{16,20},{20,16},{24,28},{28,24},{1,5},{5... | collective-permute-start | bytes 442376 | tf_op jit(solution)/shard_map/ppermute | solution.py:900
  76.7 3.1 %collective-permute-done.8.refs_17_ = f32[4,9,8,128]{3,2,1,0:T(8,128)S(1)} collective-permute-done((f32[4,9,8,128]{3,2,1,0:T(8,128)S(1)}, f32[4,9,8,128]{3,2,1,0:T(8,128)S(1)}, u32[]{:S(2)}, u32[]{:S(2)}) %collective-permute-start.8) | collective-permute-done | bytes 147488 | tf_op jit(solution)/shard_map/ppermute | solution.py:900
  80.0 4.2 %scan_back.1 = (f32[8,768]{1,0:T(8,128)S(1)}, f32[1008,768]{1,0:T(8,128)S(1)}, f32[8,768]{1,0:T(8,128)S(1)}, f32[768,384]{1,0:T(8,128)S(1)}, bf16[1008,768]{1,0:...) custom-call(f32[8,768]{1,0:T(8,128)S(1)} %get-tuple-element.672.refs, ...), custom_call_target="tpu_custom_call", output_to_operand_aliasing={{0}: (0, {}), {1}: (1, {}), {2}: (2, {}), {3}: (3, {}), {4}... | custom-call | flops 920000000 | tf_op jit(solution)/shard_map/scan_back/pallas_call | solution.py:866
  84.6 1.9 %collective-permute-start.16 = (f32[384,768]{1,0:T(8,128)S(1)}, f32[384,768]{1,0:T(8,128)S(1)}, u32[]{:S(2)}, u32[]{:S(2)}) collective-permute-start(f32[384,768]{1,0:T(8,128)S(1)} %get-tuple-element.742), channel_id=1, source_target_pairs={{0,4},{1,3},{2,6},{3,1},{4,0},{5,7},{6,2},{7,5},{8,12},{9,11},{10,... | collective-permute-start | bytes 3538952 | tf_op jit(solution)/shard_map/ppermute | solution.py:911
  86.5 1.6 collective-permute-start.11
  88.1 5.6 %input_back.1 = (f32[8,768]{1,0:T(8,128)S(1)}, f32[8,768]{1,0:T(8,128)S(1)}, f32[768,384]{1,0:T(8,128)S(1)}, f32[8,768]{1,0:T(8,128)S(1)}, bf16[1008,768]{1,0:T(...) custom-call(f32[8,768]{1,0:T(8,128)S(1)} %get-tuple-element.706.refs, ...), custom_call_target="tpu_custom_call", output_to_operand_aliasing={{0}: (0, {}), {1}: (1, {}), {2}: (2, {}), {3}: (3, {}), {4}... | custom-call | flops 1288000000 | tf_op jit(solution)/shard_map/input_back/pallas_call | solution.py:866
  93.7 2.5 %grad_scan.1 = (f32[8,768]{1,0:T(8,128)S(1)}, f32[768,384]{1,0:T(8,128)S(1)}, f32[192,1536]{1,0:T(8,128)S(1)}, f32[384,768]{1,0:T(8,128)S(1)}, f32[776,640]{1,0:...) custom-call(f32[8,768]{1,0:T(8,128)S(1)} %get-tuple-element.721.refs, ...), custom_call_target="tpu_custom_call", output_to_operand_aliasing={{0}: (0, {}), {1}: (1, {}), {2}: (2, {}), {3}: (3, {})} | custom-call | flops 552000000 | tf_op jit(solution)/shard_map/grad_scan/pallas_call | solution.py:866
  96.8 8.6 %collective-permute-done.16.refs_3_ = f32[384,768]{1,0:T(8,128)S(1)} collective-permute-done((f32[384,768]{1,0:T(8,128)S(1)}, f32[384,768]{1,0:T(8,128)S(1)}, u32[]{:S(2)}, u32[]{:S(2)}) %collective-permute-start.16) | collective-permute-done | bytes 1179680 | tf_op jit(solution)/shard_map/ppermute | solution.py:911
  105.8 1.6 collective-permute-start.21
  107.4 6.5 %collective-permute-done.11.refs_1_ = f32[192,1536]{1,0:T(8,128)S(1)} collective-permute-done((f32[192,1536]{1,0:T(8,128)S(1)}, f32[192,1536]{1,0:T(8,128)S(1)}, u32[]{:S(2)}, u32[]{:S(2)}) %collective-permute-start.11) | collective-permute-done | bytes 1179680 | tf_op jit(solution)/shard_map/ppermute | solution.py:911
  116.5 5.6 %collective-permute-done.21.refs_1_ = f32[384,768]{1,0:T(8,128)S(1)} collective-permute-done((f32[384,768]{1,0:T(8,128)S(1)}, f32[384,768]{1,0:T(8,128)S(1)}, u32[]{:S(2)}, u32[]{:S(2)}) %collective-permute-start.21) | collective-permute-done | bytes 1179680 | tf_op jit(solution)/shard_map/ppermute | solution.py:911
  122.2 1.7 collective-permute-start.22
  123.9 6.6 %output.1 = (f32[8,128]{1,0:T(8,128)S(1)}, bf16[1008,768]{1,0:T(8,128)(2,1)}) custom-call(bf16[1536,768]{1,0:T(8,128)(2,1)} %refs_0_.1, f32[1008,768]{1,0:T(8,128)} %get-tuple-element.495.refs_1_, bf16[1008,1536]{1,0:T(8,128)(2,1)} %get-tuple-element.523.refs_2_), custom_call_target="tpu_custom_call" | custom-call | flops 1610000000 | tf_op jit(solution)/shard_map/output/pallas_call | solution.py:866
  130.5 2.2 %collective-permute-done.17.refs_1_ = f32[392,640]{1,0:T(8,128)S(1)} collective-permute-done((f32[392,640]{1,0:T(8,128)S(1)}, f32[392,640]{1,0:T(8,128)S(1)}, u32[]{:S(2)}, u32[]{:S(2)}) %collective-permute-start.17) | collective-permute-done | bytes 1003552 | tf_op jit(solution)/shard_map/ppermute | solution.py:911
  133.0 1.6 collective-permute-start.19
  134.8 2.7 %collective-permute-start.18 = (f32[48,1536]{1,0:T(8,128)S(1)}, f32[48,1536]{1,0:T(8,128)S(1)}, u32[]{:S(2)}, u32[]{:S(2)}) collective-permute-start(f32[48,1536]{1,0:T(8,128)S(1)} %get-tuple-element.749), channel_id=1, source_target_pairs={{0,16},{1,3},{2,18},{3,1},{4,20},{5,7},{6,22},{7,5},{8,24},{9,11},... | collective-permute-start | bytes 884744 | tf_op jit(solution)/shard_map/ppermute | solution.py:911
  137.7 2.9 %collective-permute-start.23 = (f32[96,768]{1,0:T(8,128)S(1)}, f32[96,768]{1,0:T(8,128)S(1)}, u32[]{:S(2)}, u32[]{:S(2)}) collective-permute-start(f32[96,768]{1,0:T(8,128)S(1)} %get-tuple-element.756), channel_id=1, source_target_pairs={{0,16},{1,9},{2,18},{3,11},{4,20},{5,13},{6,22},{7,15},{8,24},{9,1... | collective-permute-start | bytes 884744 | tf_op jit(solution)/shard_map/ppermute | solution.py:911
  140.5 1.6 collective-permute-done.19.refs_1_
  142.3 2.8 %collective-permute-start.25 = (f32[104,640]{1,0:T(8,128)S(1)}, f32[104,640]{1,0:T(8,128)S(1)}, u32[]{:S(2)}, u32[]{:S(2)}) collective-permute-start(f32[104,640]{1,0:T(8,128)S(1)} %get-tuple-element.757), channel_id=1, source_target_pairs={{0,16},{1,9},{2,18},{3,11},{4,20},{5,13},{6,22},{7,15},{8,24},{9,1... | collective-permute-start | bytes 798728 | tf_op jit(solution)/shard_map/ppermute | solution.py:911
  145.0 2.3 %collective-permute-done.18.refs_1_ = f32[48,1536]{1,0:T(8,128)S(1)} collective-permute-done((f32[48,1536]{1,0:T(8,128)S(1)}, f32[48,1536]{1,0:T(8,128)S(1)}, u32[]{:S(2)}, u32[]{:S(2)}) %collective-permute-start.18) | collective-permute-done | bytes 294944 | tf_op jit(solution)/shard_map/ppermute | solution.py:911
  147.5 1.6 collective-permute-start.20
  149.1 4.9 %collective-permute-done.23.refs_1_ = f32[96,768]{1,0:T(8,128)S(1)} collective-permute-done((f32[96,768]{1,0:T(8,128)S(1)}, f32[96,768]{1,0:T(8,128)S(1)}, u32[]{:S(2)}, u32[]{:S(2)}) %collective-permute-start.23) | collective-permute-done | bytes 294944 | tf_op jit(solution)/shard_map/ppermute | solution.py:911
  154.2 1.6 collective-permute-start.24
  155.8 2.2 %collective-permute-done.25.refs_1_ = f32[104,640]{1,0:T(8,128)S(1)} collective-permute-done((f32[104,640]{1,0:T(8,128)S(1)}, f32[104,640]{1,0:T(8,128)S(1)}, u32[]{:S(2)}, u32[]{:S(2)}) %collective-permute-start.25) | collective-permute-done | bytes 266272 | tf_op jit(solution)/shard_map/ppermute | solution.py:911
  158.0 2.3 %collective-permute-start.26 = (f32[56,640]{1,0:T(8,128)S(1)}, f32[56,640]{1,0:T(8,128)S(1)}, u32[]{:S(2)}, u32[]{:S(2)}) collective-permute-start(f32[56,640]{1,0:T(8,128)S(1)} %get-tuple-element.759), channel_id=1, source_target_pairs={{0,8},{1,17},{2,10},{3,19},{4,12},{5,21},{6,14},{7,23},{8,0},{9,25... | collective-permute-start | bytes 430088 | tf_op jit(solution)/shard_map/ppermute | solution.py:911
  160.4 3.1 %collective-permute-done.26.refs_1_ = f32[56,640]{1,0:T(8,128)S(1)} collective-permute-done((f32[56,640]{1,0:T(8,128)S(1)}, f32[56,640]{1,0:T(8,128)S(1)}, u32[]{:S(2)}, u32[]{:S(2)}) %collective-permute-start.26) | collective-permute-done | bytes 143392 | tf_op jit(solution)/shard_map/ppermute | solution.py:911
  163.8 1.6 collective-permute-start.27
  168.1 1.9 %collective-permute-done.27.refs_2_ = f32[56,640]{1,0:T(8,128)S(1)} collective-permute-done((f32[56,640]{1,0:T(8,128)S(1)}, f32[56,640]{1,0:T(8,128)S(1)}, u32[]{:S(2)}, u32[]{:S(2)}) %collective-permute-start.27) | collective-permute-done | bytes 143392 | tf_op jit(solution)/shard_map/ppermute | solution.py:900
  (55 shorter events, 14.8 us)
Async XLA Ops:
  7.4 5.1 %collective-permute-start = (f32[12,8,128]{2,1,0:T(8,128)S(1)}, f32[12,8,128]{2,1,0:T(8,128)S(1)}, u32[]{:S(2)}, u32[]{:S(2)}) collective-permute-start(f32[12,8,128]{2,1,0:T(8,128)S(1)} %get-tuple-element.414.refs_12_), channel_id=1, source_target_pairs={{0,4},{4,0},{8,12},{12,8},{16,20},{20,16},{24,28},{28,24},{1,5},{5... | collective-permute-start | bytes 147464 | tf_op jit(solution)/shard_map/ppermute | solution.py:900
  12.6 4.2 %collective-permute-start.1 = (f32[12,8,128]{2,1,0:T(8,128)S(1)}, f32[12,8,128]{2,1,0:T(8,128)S(1)}, u32[]{:S(2)}, u32[]{:S(2)}) collective-permute-start(f32[12,8,128]{2,1,0:T(8,128)S(1)} %get-tuple-element.440.refs_14_), channel_id=1, source_target_pairs={{0,8},{4,12},{8,0},{12,4},{16,24},{20,28},{24,16},{28,20},{1,9},{5... | collective-permute-start | bytes 147464 | tf_op jit(solution)/shard_map/ppermute | solution.py:900
  16.9 5.2 %collective-permute-start.2 = (f32[12,8,128]{2,1,0:T(8,128)S(1)}, f32[12,8,128]{2,1,0:T(8,128)S(1)}, u32[]{:S(2)}, u32[]{:S(2)}) collective-permute-start(f32[12,8,128]{2,1,0:T(8,128)S(1)} %get-tuple-element.467.refs_14_), channel_id=1, source_target_pairs={{0,16},{4,20},{8,24},{12,28},{16,0},{20,4},{24,8},{28,12},{1,17},{... | collective-permute-start | bytes 147464 | tf_op jit(solution)/shard_map/ppermute | solution.py:900
  36.6 8.0 %collective-permute-start.3 = (f32[768,1536]{1,0:T(8,128)S(1)}, f32[768,1536]{1,0:T(8,128)S(1)}, u32[]{:S(2)}, u32[]{:S(2)}) collective-permute-start(f32[768,1536]{1,0:T(8,128)S(1)} %get-tuple-element.534), channel_id=1, source_target_pairs={{0,1},{1,0},{2,3},{3,2},{4,5},{5,4},{6,7},{7,6},{8,9},{9,8},{10,11... | collective-permute-start | bytes 14155784 | tf_op jit(solution)/shard_map/ppermute | solution.py:900
  43.9 9.6 %collective-permute-start.4 = (f32[1536,384]{1,0:T(8,128)S(1)}, f32[1536,384]{1,0:T(8,128)S(1)}, u32[]{:S(2)}, u32[]{:S(2)}) collective-permute-start(f32[1536,384]{1,0:T(8,128)S(1)} %get-tuple-element.559), channel_id=1, source_target_pairs={{0,1},{1,0},{2,3},{3,2},{4,5},{5,4},{6,7},{7,6},{8,9},{9,8},{10,11... | collective-permute-start | bytes 7077896 | tf_op jit(solution)/shard_map/ppermute | solution.py:900
  45.3 28.9 %collective-permute-start.6 = (f32[384,1536]{1,0:T(8,128)S(1)}, f32[384,1536]{1,0:T(8,128)S(1)}, u32[]{:S(2)}, u32[]{:S(2)}) collective-permute-start(f32[384,1536]{1,0:T(8,128)S(1)} %get-tuple-element.637), channel_id=1, source_target_pairs={{0,2},{1,5},{2,0},{3,7},{4,6},{5,1},{6,4},{7,3},{8,10},{9,13},{10,... | collective-permute-start | bytes 7077896 | tf_op jit(solution)/shard_map/ppermute | solution.py:911
  59.3 4.9 %collective-permute-start.5 = (f32[1,9,8,128]{3,2,1,0:T(8,128)S(1)}, f32[1,9,8,128]{3,2,1,0:T(8,128)S(1)}, u32[]{:S(2)}, u32[]{:S(2)}) collective-permute-start(f32[1,9,8,128]{3,2,1,0:T(8,128)S(1)} %get-tuple-element.605.refs_15_), channel_id=1, source_target_pairs={{0,16},{4,20},{8,24},{12,28},{16,0},{20,4},{24,8},{28,12},{1,17},{... | collective-permute-start | bytes 110600 | tf_op jit(solution)/shard_map/ppermute | solution.py:900
  63.5 20.6 %collective-permute-start.9 = (f32[768,384]{1,0:T(8,128)S(1)}, f32[768,384]{1,0:T(8,128)S(1)}, u32[]{:S(2)}, u32[]{:S(2)}) collective-permute-start(f32[768,384]{1,0:T(8,128)S(1)} %get-tuple-element.704), channel_id=1, source_target_pairs={{0,1},{1,0},{2,3},{3,2},{4,5},{5,4},{6,7},{7,6},{8,9},{9,8},{10,11... | collective-permute-start | bytes 3538952 | tf_op jit(solution)/shard_map/ppermute | solution.py:900
  65.9 18.3 %collective-permute-start.10 = (f32[768,384]{1,0:T(8,128)S(1)}, f32[768,384]{1,0:T(8,128)S(1)}, u32[]{:S(2)}, u32[]{:S(2)}) collective-permute-start(f32[768,384]{1,0:T(8,128)S(1)} %get-tuple-element.705), channel_id=1, source_target_pairs={{0,1},{1,0},{2,3},{3,2},{4,5},{5,4},{6,7},{7,6},{8,9},{9,8},{10,11... | collective-permute-start | bytes 3538952 | tf_op jit(solution)/shard_map/ppermute | solution.py:900
  65.9 8.6 %collective-permute-start.7 = (f32[2,9,8,128]{3,2,1,0:T(8,128)S(1)}, f32[2,9,8,128]{3,2,1,0:T(8,128)S(1)}, u32[]{:S(2)}, u32[]{:S(2)}) collective-permute-start(f32[2,9,8,128]{3,2,1,0:T(8,128)S(1)} %get-tuple-element.654.refs_16_), channel_id=1, source_target_pairs={{0,8},{4,12},{8,0},{12,4},{16,24},{20,28},{24,16},{28,20},{1,9},{5... | collective-permute-start | bytes 221192 | tf_op jit(solution)/shard_map/ppermute | solution.py:900
  74.6 5.2 %collective-permute-start.8 = (f32[4,9,8,128]{3,2,1,0:T(8,128)S(1)}, f32[4,9,8,128]{3,2,1,0:T(8,128)S(1)}, u32[]{:S(2)}, u32[]{:S(2)}) collective-permute-start(f32[4,9,8,128]{3,2,1,0:T(8,128)S(1)} %get-tuple-element.671.refs_16_), channel_id=1, source_target_pairs={{0,4},{4,0},{8,12},{12,8},{16,20},{20,16},{24,28},{28,24},{1,5},{5... | collective-permute-start | bytes 442376 | tf_op jit(solution)/shard_map/ppermute | solution.py:900
  76.5 20.3 %collective-permute-start.15 = (f32[768,384]{1,0:T(8,128)S(1)}, f32[768,384]{1,0:T(8,128)S(1)}, u32[]{:S(2)}, u32[]{:S(2)}) collective-permute-start(f32[768,384]{1,0:T(8,128)S(1)} %get-tuple-element.741), channel_id=1, source_target_pairs={{0,4},{1,3},{2,6},{3,1},{4,0},{5,7},{6,2},{7,5},{8,12},{9,11},{10,... | collective-permute-start | bytes 3538952 | tf_op jit(solution)/shard_map/ppermute | solution.py:911
  84.6 20.8 %collective-permute-start.16 = (f32[384,768]{1,0:T(8,128)S(1)}, f32[384,768]{1,0:T(8,128)S(1)}, u32[]{:S(2)}, u32[]{:S(2)}) collective-permute-start(f32[384,768]{1,0:T(8,128)S(1)} %get-tuple-element.742), channel_id=1, source_target_pairs={{0,4},{1,3},{2,6},{3,1},{4,0},{5,7},{6,2},{7,5},{8,12},{9,11},{10,... | collective-permute-start | bytes 3538952 | tf_op jit(solution)/shard_map/ppermute | solution.py:911
  86.5 27.4 %collective-permute-start.11 = (f32[192,1536]{1,0:T(8,128)S(1)}, f32[192,1536]{1,0:T(8,128)S(1)}, u32[]{:S(2)}, u32[]{:S(2)}) collective-permute-start(f32[192,1536]{1,0:T(8,128)S(1)} %get-tuple-element.733), channel_id=1, source_target_pairs={{0,8},{1,17},{2,10},{3,19},{4,12},{5,21},{6,14},{7,23},{8,0},{9,25... | collective-permute-start | bytes 3538952 | tf_op jit(solution)/shard_map/ppermute | solution.py:911
  96.2 17.9 %collective-permute-start.13 = (f32[392,640]{1,0:T(8,128)S(1)}, f32[392,640]{1,0:T(8,128)S(1)}, u32[]{:S(2)}, u32[]{:S(2)}) collective-permute-start(f32[392,640]{1,0:T(8,128)S(1)} %get-tuple-element.737), channel_id=1, source_target_pairs={{0,1},{1,0},{2,3},{3,2},{4,5},{5,4},{6,7},{7,6},{8,9},{9,8},{10,11... | collective-permute-start | bytes 3010568 | tf_op jit(solution)/shard_map/ppermute | solution.py:900
  96.3 17.8 %collective-permute-start.14 = (f32[384,640]{1,0:T(8,128)S(1)}, f32[384,640]{1,0:T(8,128)S(1)}, u32[]{:S(2)}, u32[]{:S(2)}) collective-permute-start(f32[384,640]{1,0:T(8,128)S(1)} %get-tuple-element.738), channel_id=1, source_target_pairs={{0,1},{1,0},{2,3},{3,2},{4,5},{5,4},{6,7},{7,6},{8,9},{9,8},{10,11... | collective-permute-start | bytes 2949128 | tf_op jit(solution)/shard_map/ppermute | solution.py:900
  105.8 16.3 %collective-permute-start.21 = (f32[384,768]{1,0:T(8,128)S(1)}, f32[384,768]{1,0:T(8,128)S(1)}, u32[]{:S(2)}, u32[]{:S(2)}) collective-permute-start(f32[384,768]{1,0:T(8,128)S(1)} %get-tuple-element.752), channel_id=1, source_target_pairs={{0,2},{1,5},{2,0},{3,7},{4,6},{5,1},{6,4},{7,3},{8,10},{9,13},{10,... | collective-permute-start | bytes 3538952 | tf_op jit(solution)/shard_map/ppermute | solution.py:911
  114.4 18.3 %collective-permute-start.17 = (f32[392,640]{1,0:T(8,128)S(1)}, f32[392,640]{1,0:T(8,128)S(1)}, u32[]{:S(2)}, u32[]{:S(2)}) collective-permute-start(f32[392,640]{1,0:T(8,128)S(1)} %get-tuple-element.745), channel_id=1, source_target_pairs={{0,2},{1,5},{2,0},{3,7},{4,6},{5,1},{6,4},{7,3},{8,10},{9,13},{10,... | collective-permute-start | bytes 3010568 | tf_op jit(solution)/shard_map/ppermute | solution.py:911
  116.0 18.7 %collective-permute-start.12 = (f32[96,1536]{1,0:T(8,128)S(1)}, f32[96,1536]{1,0:T(8,128)S(1)}, u32[]{:S(2)}, u32[]{:S(2)}) collective-permute-start(f32[96,1536]{1,0:T(8,128)S(1)} %get-tuple-element.735), channel_id=1, source_target_pairs={{0,4},{1,9},{2,6},{3,11},{4,0},{5,13},{6,2},{7,15},{8,12},{9,1},{1... | collective-permute-start | bytes 1769480 | tf_op jit(solution)/shard_map/ppermute | solution.py:911
  122.2 15.3 %collective-permute-start.22 = (f32[192,768]{1,0:T(8,128)S(1)}, f32[192,768]{1,0:T(8,128)S(1)}, u32[]{:S(2)}, u32[]{:S(2)}) collective-permute-start(f32[192,768]{1,0:T(8,128)S(1)} %get-tuple-element.754), channel_id=1, source_target_pairs={{0,8},{1,17},{2,10},{3,19},{4,12},{5,21},{6,14},{7,23},{8,0},{9,25... | collective-permute-start | bytes 1769480 | tf_op jit(solution)/shard_map/ppermute | solution.py:911
  133.0 9.1 %collective-permute-start.19 = (f32[200,640]{1,0:T(8,128)S(1)}, f32[200,640]{1,0:T(8,128)S(1)}, u32[]{:S(2)}, u32[]{:S(2)}) collective-permute-start(f32[200,640]{1,0:T(8,128)S(1)} %get-tuple-element.750), channel_id=1, source_target_pairs={{0,4},{1,3},{2,6},{3,1},{4,0},{5,7},{6,2},{7,5},{8,12},{9,11},{10,... | collective-permute-start | bytes 1536008 | tf_op jit(solution)/shard_map/ppermute | solution.py:911
  134.8 12.5 %collective-permute-start.18 = (f32[48,1536]{1,0:T(8,128)S(1)}, f32[48,1536]{1,0:T(8,128)S(1)}, u32[]{:S(2)}, u32[]{:S(2)}) collective-permute-start(f32[48,1536]{1,0:T(8,128)S(1)} %get-tuple-element.749), channel_id=1, source_target_pairs={{0,16},{1,3},{2,18},{3,1},{4,20},{5,7},{6,22},{7,5},{8,24},{9,11},... | collective-permute-start | bytes 884744 | tf_op jit(solution)/shard_map/ppermute | solution.py:911
  137.7 16.4 %collective-permute-start.23 = (f32[96,768]{1,0:T(8,128)S(1)}, f32[96,768]{1,0:T(8,128)S(1)}, u32[]{:S(2)}, u32[]{:S(2)}) collective-permute-start(f32[96,768]{1,0:T(8,128)S(1)} %get-tuple-element.756), channel_id=1, source_target_pairs={{0,16},{1,9},{2,18},{3,11},{4,20},{5,13},{6,22},{7,15},{8,24},{9,1... | collective-permute-start | bytes 884744 | tf_op jit(solution)/shard_map/ppermute | solution.py:911
  142.3 15.7 %collective-permute-start.25 = (f32[104,640]{1,0:T(8,128)S(1)}, f32[104,640]{1,0:T(8,128)S(1)}, u32[]{:S(2)}, u32[]{:S(2)}) collective-permute-start(f32[104,640]{1,0:T(8,128)S(1)} %get-tuple-element.757), channel_id=1, source_target_pairs={{0,16},{1,9},{2,18},{3,11},{4,20},{5,13},{6,22},{7,15},{8,24},{9,1... | collective-permute-start | bytes 798728 | tf_op jit(solution)/shard_map/ppermute | solution.py:911
  147.5 16.1 %collective-permute-start.20 = (f32[48,1536]{1,0:T(8,128)S(1)}, f32[48,1536]{1,0:T(8,128)S(1)}, u32[]{:S(2)}, u32[]{:S(2)}) collective-permute-start(f32[48,1536]{1,0:T(8,128)S(1)} %sum_wide.1.refs_2_.refs_1_), channel_id=1, source_target_pairs={{0,2},{1,3},{2,0},{3,1},{4,6},{5,7},{6,4},{7,5},{8,10},{9,11},{10,... | collective-permute-start | bytes 884744 | tf_op jit(solution)/shard_map/ppermute | solution.py:900
  154.2 9.4 %collective-permute-start.24 = (f32[48,1536]{1,0:T(8,128)S(1)}, f32[48,1536]{1,0:T(8,128)S(1)}, u32[]{:S(2)}, u32[]{:S(2)}) collective-permute-start(f32[48,1536]{1,0:T(8,128)S(1)} %pack.1.refs_3_), channel_id=1, source_target_pairs={{0,2},{1,3},{2,0},{3,1},{4,6},{5,7},{6,4},{7,5},{8,10},{9,11},{10,... | collective-permute-start | bytes 884744 | tf_op jit(solution)/shard_map/ppermute | solution.py:900
  158.0 5.4 %collective-permute-start.26 = (f32[56,640]{1,0:T(8,128)S(1)}, f32[56,640]{1,0:T(8,128)S(1)}, u32[]{:S(2)}, u32[]{:S(2)}) collective-permute-start(f32[56,640]{1,0:T(8,128)S(1)} %get-tuple-element.759), channel_id=1, source_target_pairs={{0,8},{1,17},{2,10},{3,19},{4,12},{5,21},{6,14},{7,23},{8,0},{9,25... | collective-permute-start | bytes 430088 | tf_op jit(solution)/shard_map/ppermute | solution.py:911
  163.7 2.9 %collective-permute-start.28 = (f32[96,3072]{1,0:T(8,128)S(1)}, f32[96,3072]{1,0:T(8,128)S(1)}, u32[]{:S(2)}, u32[]{:S(2)}) collective-permute-start(f32[96,3072]{1,0:T(8,128)S(1)} %get-tuple-element.761.refs_0_), channel_id=1, source_target_pairs={{0,1},{1,0},{2,3},{3,2},{4,5},{5,4},{6,7},{7,6},{8,9},{9,8},{10,11... | collective-permute-start | bytes 3538952 | tf_op jit(solution)/shard_map/ppermute | solution.py:900
  163.8 6.2 %collective-permute-start.27 = (f32[56,640]{1,0:T(8,128)S(1)}, f32[56,640]{1,0:T(8,128)S(1)}, u32[]{:S(2)}, u32[]{:S(2)}) collective-permute-start(f32[56,640]{1,0:T(8,128)S(1)} %sum_scan.1.refs_5_.refs_1_), channel_id=1, source_target_pairs={{0,2},{1,3},{2,0},{3,1},{4,6},{5,7},{6,4},{7,5},{8,10},{9,11},{10,... | collective-permute-start | bytes 430088 | tf_op jit(solution)/shard_map/ppermute | solution.py:900
  170.1 1.6 collective-permute-start.29
